TPU v7x, 256 devices: a whole 4x4x8 slice. The times are simulated.
256 devices in a mesh: dp: 16 (over z_lo, x), tensor: 16 (over z_hi, y, core).
Axes of the slice: x: 4, y: 4, z: 8 (z_hi: 2, z_lo: 4; z = z_hi * 4 + z_lo), core: 2. Of those that a mesh axis runs over, the one named last changes fastest.
Arguments:
- tokens: bfloat16 [8192, 8192], P('dp', 'tensor'), may hold values from -6 to 6
- cotangent: bfloat16 [8192, 8192], P('dp', 'tensor'), may hold values from -6 to 6
- w_first: bfloat16 [32, 256, 1024], P('tensor', 'dp'), may hold values from -0.375 to 0.375
- w_second: bfloat16 [128, 256, 256], P('tensor', 'dp'), may hold values from -0.375 to 0.375
- w_third: bfloat16 [128, 256, 256], P('tensor', 'dp'), may hold values from -0.375 to 0.375
- w_fourth: bfloat16 [32, 1024, 256], P('tensor', 'dp'), may hold values from -0.1875 to 0.1875
Outputs:
- layer_out: bfloat16 [8192, 8192], P('dp', 'tensor')
- grad_tokens: bfloat16 [8192, 8192], P('dp', 'tensor')
- grad_first: float32 [32, 256, 1024], P('tensor', 'dp')
- grad_second: float32 [128, 256, 256], P('tensor', 'dp')
- grad_third: float32 [128, 256, 256], P('tensor', 'dp')
- grad_fourth: float32 [32, 1024, 256], P('tensor', 'dp')
All inputs are finite; a program needn't handle non-finite values.
Results may differ from a plain program's by a relative error of at most 0.0068.
Values may be sent and summed in bfloat16 or wider, within the bound.
No kernel may reach another device: no remote copies, remote signals or barrier semaphores. Data moves between devices by JAX's collectives and lax.ppermute only.
A program may use at most 64 MiB of HBM per device.

v0:
```python
import jax
import jax.numpy as jnp
from jax import lax
from jax.sharding import PartitionSpec as P

BS = 256
NA = 32
NJ = 128
RR = 8


def gelu_tanh(values):
    return jax.nn.gelu(values, approximate=True)


def to_groups(values):
    return lax.all_to_all(values, "tensor", split_axis=1, concat_axis=0, tiled=True)


def to_blocks(values):
    return lax.all_to_all(values, "tensor", split_axis=0, concat_axis=1, tiled=True)


def body(tokens, cotangent, w_first, w_second, w_third, w_fourth):
    groups = lax.axis_size("tensor")
    blocks_here = NA // groups
    groups_here = NJ // groups
    rows = tokens.shape[0]
    full_first, full_second, full_third, full_fourth = (
        lax.all_gather(w_first, "dp", axis=1, tiled=True),
        lax.all_gather(w_second, "dp", axis=1, tiled=True),
        lax.all_gather(w_third, "dp", axis=1, tiled=True),
        lax.all_gather(w_fourth, "dp", axis=1, tiled=True),
    )
    first = full_first.reshape(blocks_here, BS, NJ, RR)
    second = full_second.reshape(groups_here, NA, RR, BS)
    third = full_third.reshape(groups_here, BS, NA, RR)
    fourth = full_fourth.reshape(blocks_here, NJ, RR, BS)
    inputs = tokens.reshape(rows, blocks_here, BS)
    upstream = cotangent.reshape(rows, blocks_here, BS)
    mid_local = jnp.einsum(
        "tai,aijr->ajrt", inputs, first, preferred_element_type=jnp.float32
    ).astype(jnp.bfloat16)
    mid = to_groups(mid_local)
    pre = jnp.einsum("ajrt,jarc->jtc", mid, second, preferred_element_type=jnp.float32)
    hidden = gelu_tanh(pre).astype(jnp.bfloat16)
    back_groups = jnp.einsum(
        "jtc,jcar->ajrt", hidden, third, preferred_element_type=jnp.float32
    ).astype(jnp.bfloat16)
    back = to_blocks(back_groups)
    layer_out = (
        jnp.einsum("ajrt,ajro->tao", back, fourth, preferred_element_type=jnp.float32)
        .astype(jnp.bfloat16)
        .reshape(rows, blocks_here * BS)
    )
    g_back_local = jnp.einsum(
        "tao,ajro->ajrt", upstream, fourth, preferred_element_type=jnp.float32
    ).astype(jnp.bfloat16)
    grad4 = jnp.einsum(
        "ajrt,tao->ajro", back, upstream, preferred_element_type=jnp.float32
    ).reshape(blocks_here, NJ * RR, BS)
    g_back = to_groups(g_back_local)
    g_hidden = jnp.einsum("ajrt,jcar->jtc", g_back, third, preferred_element_type=jnp.float32)
    grad3 = jnp.einsum(
        "jtc,ajrt->jcar", hidden, g_back, preferred_element_type=jnp.float32
    ).reshape(groups_here, BS, NA * RR)
    _, pull = jax.vjp(gelu_tanh, pre)
    g_pre = pull(g_hidden)[0].astype(jnp.bfloat16)
    g_mid_groups = jnp.einsum(
        "jtc,jarc->ajrt", g_pre, second, preferred_element_type=jnp.float32
    ).astype(jnp.bfloat16)
    grad2 = jnp.einsum("ajrt,jtc->jarc", mid, g_pre, preferred_element_type=jnp.float32).reshape(
        groups_here, NA * RR, BS
    )
    g_mid = to_blocks(g_mid_groups)
    grad_tokens = (
        jnp.einsum("ajrt,aijr->tai", g_mid, first, preferred_element_type=jnp.float32)
        .astype(jnp.bfloat16)
        .reshape(rows, blocks_here * BS)
    )
    grad1 = jnp.einsum("tai,ajrt->aijr", inputs, g_mid, preferred_element_type=jnp.float32).reshape(
        blocks_here, BS, NJ * RR
    )
    sum1, sum2, sum3, sum4 = (
        lax.psum_scatter(grad1, "dp", scatter_dimension=1, tiled=True),
        lax.psum_scatter(grad2, "dp", scatter_dimension=1, tiled=True),
        lax.psum_scatter(grad3, "dp", scatter_dimension=1, tiled=True),
        lax.psum_scatter(grad4, "dp", scatter_dimension=1, tiled=True),
    )
    return (layer_out, grad_tokens, sum1, sum2, sum3, sum4)


def solution(mesh):
    in_specs = (
        P("dp", "tensor"),
        P("dp", "tensor"),
        P("tensor", "dp", None),
        P("tensor", "dp", None),
        P("tensor", "dp", None),
        P("tensor", "dp", None),
    )
    out_specs = (
        P("dp", "tensor"),
        P("dp", "tensor"),
        P("tensor", "dp", None),
        P("tensor", "dp", None),
        P("tensor", "dp", None),
        P("tensor", "dp", None),
    )
    return jax.shard_map(body, mesh=mesh, in_specs=in_specs, out_specs=out_specs, check_vma=False)
```

profile of v0, /device:TPU:16, one launch (start us, length us, event | category | flops | bytes accessed | tf_op | source)
XLA Modules:
  0.0 886.7 jit_solution(8743700597360208317)
XLA Ops:
  7.2 0.0 all-gather.5.cloned.1.call-start
  7.2 1.5 copy.51
  8.8 1.2 reshape.49
  9.9 84.3 %all-gather.5.cloned.1.call-done = bf16[2,256,1024]{2,0,1:T(2,128)(2,1)} async-done(((bf16[2,16,1024]{2,0,1:T(2,128)(2,1)}), bf16[2,256,1024]{2,0,1:T(2,128)(2,1)}) %all-gather.5.cloned.1.call-update) | async-done | bytes 1048592 | tf_op jit(solution)/shard_map/all_gather | solution.py:30
  94.2 2.4 copy.52
  96.7 1.0 copy.72
  97.7 0.9 convolution_convert_fusion.1
  98.6 2.5 copy.55
  101.1 9.1 %all-to-all-start = ((bf16[2,128,8,512]{3,2,0,1:T(8,128)(2,1)}), bf16[2,128,8,512]{3,2,0,1:T(8,128)(2,1)S(1)}, u32[]{:S(2)}, u32[]{:S(2)}) async-start(bf16[2,128,8,512]{3,2,0,1:T(8,128)(2,1)} %copy.55), calls=%async_computation | async-start | bytes 4194304 | tf_op jit(solution)/shard_map/all_to_all | solution.py:17
  110.3 0.0 all-gather.11.cloned.1.call-start
  110.3 0.7 all-gather.11.cloned.1.call-update
  111.0 1.2 reshape.54
  112.2 87.1 %all-gather.11.cloned.1.call-done = bf16[2,1024,256]{2,1,0:T(8,128)(2,1)} async-done(((bf16[2,64,256]{2,1,0:T(8,128)(2,1)}), bf16[2,1024,256]{2,1,0:T(8,128)(2,1)}) %all-gather.11.cloned.1.call-update) | async-done | bytes 1048592 | tf_op jit(solution)/shard_map/all_gather | solution.py:33
  199.3 2.6 copy.63
  201.9 2.2 convolution_convert_fusion
  204.1 2.5 copy.66
  206.6 6.2 all-to-all-start.2
  212.7 0.0 all-gather.9.cloned.1.call-start
  212.8 0.7 copy.58
  213.4 0.0 all-gather.9.cloned.1.call-update
  213.5 0.2 all-gather.7.cloned.1.call-start
  213.7 0.3 all-gather.7.cloned.1.call-update
  214.1 90.4 %all-gather.9.cloned.1.call-done = bf16[8,256,256]{2,0,1:T(8,128)(2,1)} async-done(((bf16[8,16,256]{2,0,1:T(8,128)(2,1)}), bf16[8,256,256]{2,0,1:T(8,128)(2,1)}) %all-gather.9.cloned.1.call-update) | async-done | bytes 1048592 | tf_op jit(solution)/shard_map/all_gather | solution.py:32
  304.5 2.4 copy.59
  306.9 3.5 copy.157
  310.4 2.7 all_to_all.55
  313.2 5.1 copy.155
  318.3 4.2 all_to_all.63
  322.4 60.9 %all-gather.7.cloned.1.call-done = bf16[8,256,256]{2,1,0:T(8,128)(2,1)} async-done(((bf16[8,16,256]{2,1,0:T(8,128)(2,1)}), bf16[8,256,256]{2,1,0:T(8,128)(2,1)}) %all-gather.7.cloned.1.call-update) | async-done | bytes 1048592 | tf_op jit(solution)/shard_map/all_gather | solution.py:31
  383.3 2.2 fusion.59
  385.6 3.5 fusion.6
  389.1 0.7 convert_bitcast_fusion
  389.8 0.6 copy-done
  390.5 2.5 copy.70
  393.0 9.1 %all-to-all-start.3 = ((bf16[32,8,8,512]{3,2,1,0:T(8,128)(2,1)}), bf16[32,8,8,512]{3,2,1,0:T(8,128)(2,1)}, u32[]{:S(2)}, u32[]{:S(2)}) async-start(bf16[32,8,8,512]{3,2,1,0:T(8,128)(2,1)} %copy.70), calls=%async_computation.3 | async-start | bytes 4194304 | tf_op jit(solution)/shard_map/all_to_all | solution.py:21
  402.1 0.0 reduce-scatter.6.cloned.1.call-start
  402.2 6.3 fusion.38
  408.5 3.1 copy.78
  411.6 0.3 all-reduce.3.cloned.1.call-start
  411.9 40.7 %all-to-all-done.3 = bf16[32,8,8,512]{3,2,1,0:T(8,128)(2,1)} async-done(((bf16[32,8,8,512]{3,2,1,0:T(8,128)(2,1)}), bf16[32,8,8,512]{3,2,1,0:T(8,128)(2,1)}, u32[]{:S(2)}, u32[]{:S(2)}) %all-to-all-start.3) | async-done | bytes 2097184 | tf_op jit(solution)/shard_map/all_to_all | solution.py:21
  452.6 2.9 fusion.46
  455.5 2.5 copy.154
  458.0 4.3 copy.75
  462.3 4.2 convert_bitcast_fusion.1
  466.5 2.5 copy.61
  469.0 12.0 %all-to-all-start.1 = ((bf16[32,8,8,512]{3,2,1,0:T(8,128)(2,1)}), bf16[32,8,8,512]{3,2,1,0:T(8,128)(2,1)}, u32[]{:S(2)}, u32[]{:S(2)}) async-start(bf16[32,8,8,512]{3,2,1,0:T(8,128)(2,1)} %copy.61), calls=%async_computation.1 | async-start | bytes 4194304 | tf_op jit(solution)/shard_map/all_to_all | solution.py:21
  480.9 0.0 reduce-scatter.4.cloned.1.call-start
  481.0 4.3 fusion.33
  485.3 0.3 reduce-scatter.8.cloned.1.call-start
  485.6 29.3 %all-to-all-done.1 = bf16[32,8,8,512]{3,2,1,0:T(8,128)(2,1)} async-done(((bf16[32,8,8,512]{3,2,1,0:T(8,128)(2,1)}), bf16[32,8,8,512]{3,2,1,0:T(8,128)(2,1)}, u32[]{:S(2)}, u32[]{:S(2)}) %all-to-all-start.1) | async-done | bytes 2097184 | tf_op jit(solution)/shard_map/all_to_all | solution.py:21
  515.0 2.3 copy.156
  517.3 2.6 fusion.43
  519.9 0.6 copy-done.8
  520.5 0.6 dynamic-slice
  521.8 3.1 fusion.53
  524.9 1.0 copy.82
  525.9 3.0 fusion.52
  528.9 1.0 copy.81
  529.9 1.6 copy.84
  531.5 171.5 %all-reduce.3.cloned.1.call-done = f32[2,256,1024]{2,0,1:T(2,128)} async-done(((f32[2,256,1024]{2,0,1:T(2,128)}), f32[2,256,1024]{2,0,1:T(2,128)}) %all-reduce.3.cloned.1.call-update) | async-done | bytes 2097168
  703.0 0.9 constant_dynamic-slice_fusion
  703.9 0.7 copy.83
  704.6 87.8 %reduce-scatter.4.cloned.1.call-done = f32[8,16,256]{2,1,0:T(8,128)} async-done(((f32[8,256,256]{2,1,0:T(8,128)}), f32[8,16,256]{2,1,0:T(8,128)}) %reduce-scatter.4.cloned.1.call-update) | async-done | bytes 131088 | tf_op jit(solution)/shard_map/reduce_scatter | solution.py:86
  792.4 87.5 %reduce-scatter.8.cloned.1.call-done = f32[2,64,256]{2,1,0:T(8,128)} async-done(((f32[2,1024,256]{2,1,0:T(8,128)}), f32[2,64,256]{2,1,0:T(8,128)}) %reduce-scatter.8.cloned.1.call-update) | async-done | bytes 131088 | tf_op jit(solution)/shard_map/reduce_scatter | solution.py:88
  (26 shorter events, 0.1 us)
Async XLA Ops:
  7.2 87.1 %all-gather.5.cloned.1.call-start = ((), (), s32[]{:S(2)}) async-start(), calls=%async_computation.7 | async-start | bytes 1114112 | tf_op jit(solution)/shard_map/all_gather | solution.py:30
  97.7 3.5 copy-start.1
  101.1 105.4 %all-to-all-start = ((bf16[2,128,8,512]{3,2,0,1:T(8,128)(2,1)}), bf16[2,128,8,512]{3,2,0,1:T(8,128)(2,1)S(1)}, u32[]{:S(2)}, u32[]{:S(2)}) async-start(bf16[2,128,8,512]{3,2,0,1:T(8,128)(2,1)} %copy.55), calls=%async_computation | async-start | bytes 4194304 | tf_op jit(solution)/shard_map/all_to_all | solution.py:17
  110.3 89.0 %all-gather.11.cloned.1.call-start = ((), (), s32[]{:S(2)}) async-start(), calls=%async_computation.10 | async-start | bytes 1114112 | tf_op jit(solution)/shard_map/all_gather | solution.py:33
  206.6 6.2 copy-start.7
  206.6 106.6 %all-to-all-start.2 = ((bf16[2,128,8,512]{3,2,0,1:T(8,128)(2,1)}), bf16[2,128,8,512]{3,2,0,1:T(8,128)(2,1)}, u32[]{:S(2)}, u32[]{:S(2)}) async-start(bf16[2,128,8,512]{3,2,0,1:T(8,128)(2,1)} %copy.66), calls=%async_computation.2 | async-start | bytes 4194304 | tf_op jit(solution)/shard_map/all_to_all | solution.py:17
  212.7 91.7 %all-gather.9.cloned.1.call-start = ((), (), s32[]{:S(2)}) async-start(), calls=%async_computation.9 | async-start | bytes 1114112 | tf_op jit(solution)/shard_map/all_gather | solution.py:32
  213.5 169.8 %all-gather.7.cloned.1.call-start = ((), (), s32[]{:S(2)}) async-start(), calls=%async_computation.8 | async-start | bytes 1114112 | tf_op jit(solution)/shard_map/all_gather | solution.py:31
  383.3 2.2 copy-start.4
  383.3 2.2 copy-start.6
  385.5 3.5 copy-start.9
  385.6 3.5 copy-start.5
  389.1 1.4 copy-start
  393.0 59.6 %all-to-all-start.3 = ((bf16[32,8,8,512]{3,2,1,0:T(8,128)(2,1)}), bf16[32,8,8,512]{3,2,1,0:T(8,128)(2,1)}, u32[]{:S(2)}, u32[]{:S(2)}) async-start(bf16[32,8,8,512]{3,2,1,0:T(8,128)(2,1)} %copy.70), calls=%async_computation.3 | async-start | bytes 4194304 | tf_op jit(solution)/shard_map/all_to_all | solution.py:21
  402.1 127.8 %reduce-scatter.6.cloned.1.call-start = ((), (), s32[]{:S(2)}) async-start(), calls=%async_computation.12 | async-start | bytes 2228224 | tf_op jit(solution)/shard_map/reduce_scatter | solution.py:87
  411.6 291.3 %all-reduce.3.cloned.1.call-start = ((), (), s32[]{:S(2)}) async-start(), calls=%async_computation.14 | async-start | bytes 4194304
  469.0 46.0 %all-to-all-start.1 = ((bf16[32,8,8,512]{3,2,1,0:T(8,128)(2,1)}), bf16[32,8,8,512]{3,2,1,0:T(8,128)(2,1)}, u32[]{:S(2)}, u32[]{:S(2)}) async-start(bf16[32,8,8,512]{3,2,1,0:T(8,128)(2,1)} %copy.61), calls=%async_computation.1 | async-start | bytes 4194304 | tf_op jit(solution)/shard_map/all_to_all | solution.py:21
  480.9 311.4 %reduce-scatter.4.cloned.1.call-start = ((), (), s32[]{:S(2)}) async-start(), calls=%async_computation.11 | async-start | bytes 2228224 | tf_op jit(solution)/shard_map/reduce_scatter | solution.py:86
  485.3 394.6 %reduce-scatter.8.cloned.1.call-start = ((), (), s32[]{:S(2)}) async-start(), calls=%async_computation.13 | async-start | bytes 2228224 | tf_op jit(solution)/shard_map/reduce_scatter | solution.py:88
  519.9 0.7 copy-start.8
  519.9 1.9 copy-start.2
  521.8 4.1 copy-start.3
Sparse Core Ops, SparseCore 0:
  10.4 83.8 all-gather.4
  112.9 86.3 all-gather.10
  215.9 88.4 all-gather.8
  306.1 77.1 all-gather.6
  411.7 103.5 reduce-scatter.5
  517.8 185.0 all-reduce.2
  706.1 86.2 reduce-scatter.3
  795.5 84.3 reduce-scatter.7
where the time goes:
time: 888 us; the launch traced here: 887 us
  waiting for transfers between devices  741 us (83%)
  local copies, waits for them, and re-layouts  57.8 us (7%)
  starting transfers between devices  37.4 us (4%)
  matrix products  35.9 us (4%)
  between operations  15 us (2%)
    unnamed x9, waiting for transfers between devices  173 us
    all_gather x1, waiting for transfers between devices, body(): lax.all_gather(w_third, 'dp', axis=1, tiled=True)  90.4 us
    reduce_scatter x1, waiting for transfers between devices, body(): lax.psum_scatter(grad2, 'dp', scatter_dimension=1, tiled=True)  87.8 us
    reduce_scatter x1, waiting for transfers between devices, body(): lax.psum_scatter(grad4, 'dp', scatter_dimension=1, tiled=True)  87.5 us
    all_gather x1, waiting for transfers between devices, body(): lax.all_gather(w_fourth, 'dp', axis=1, tiled=True)  87.1 us
    all_gather x1, waiting for transfers between devices, body(): lax.all_gather(w_first, 'dp', axis=1, tiled=True)  84.3 us
    all_to_all x2, waiting for transfers between devices, to_blocks(): lax.all_to_all(values, 'tensor', split_axis=0, concat_axis=1, tiled=True)  70 us
    all_gather x1, waiting for transfers between devices, body(): lax.all_gather(w_second, 'dp', axis=1, tiled=True)  60.9 us
  transfers between devices with their start and end apart: 12, of which 9 were waited for; matrix products, arithmetic and copies ran while one was open for 8% of the time, Pallas kernels for 0%

commit v1 on v0

v1 whole, which is shorter than its diff:
```python
import jax
import jax.numpy as jnp
from jax import lax
from jax.experimental import pallas as pl
from jax.experimental.pallas import tpu as pltpu
from jax.sharding import Mesh
from jax.sharding import PartitionSpec as P

BS = 256
NA = 32
NJ = 128
RR = 8
AXES = ("zl", "x1", "x0", "zh", "y", "c")
WAYS = ("x1", "y", "c", "x0")
COPIES = ("zh", "zl")
bf16 = jnp.bfloat16
f32 = jnp.float32
C0 = 0.7978845608028654
C1 = 0.044715


def dot(a, b, ca, cb):
    return lax.dot_general(a, b, (((ca,), (cb,)), ((), ())), preferred_element_type=f32)


def call(kernel, grid, in_specs, out_specs, out_shape, flops, nbytes, trans=0):
    return pl.pallas_call(
        kernel,
        grid=grid,
        in_specs=in_specs,
        out_specs=out_specs,
        out_shape=out_shape,
        compiler_params=pltpu.CompilerParams(vmem_limit_bytes=48 * 1024 * 1024),
        cost_estimate=pl.CostEstimate(flops=flops, bytes_accessed=nbytes, transcendentals=trans),
    )


ONE = 2 * 1024 * 1024 * 256


def from_copies(block):
    return block.reshape(2, 4, 2, 16, BS).swapaxes(0, 1).reshape(BS, BS)


def to_copies(rows):
    return rows.reshape(4, 2, 2, 16, BS).swapaxes(0, 1)


def swap(pieces):
    x0 = lax.axis_index("x0")
    got = []
    for k in range(2):
        pairs = [
            (a * 4 + b * 2 + c, c * 4 + (b ^ k) * 2 + a)
            for a in range(2)
            for b in range(2)
            for c in range(2)
        ]
        piece = jnp.where((x0 ^ k) == 0, pieces[0], pieces[1])
        got.append(lax.ppermute(piece, ("x1", "x0", "zh"), pairs))
    first = x0 == 0
    return jnp.where(first, got[0], got[1]), jnp.where(first, got[1], got[0])


def mid_kernel(x_ref, w_ref, out_ref):
    w = from_copies(w_ref[...])
    out = dot(w.T, x_ref[...].reshape(1024, BS), 1, 1)
    out_ref[...] = out.astype(bf16).reshape(8, 32, 1024)


def g_back_kernel(g_ref, w_ref, out_ref):
    w = w_ref[...].reshape(BS, BS)
    out = dot(w, g_ref[...].reshape(1024, BS), 1, 1)
    out_ref[...] = out.astype(bf16).reshape(8, 32, 1024)


def group_rows(ref, k):
    rows = ref[...].astype(f32).reshape(NA, 2, RR, 1024)
    return rows[:, k].reshape(NA * RR, 1024).astype(bf16)


def both_groups(values):
    rows = [v.astype(bf16).astype(f32).reshape(NA, 1, RR, 1024) for v in values]
    return jnp.concatenate(rows, axis=1).reshape(NA, 2 * RR, 1024).astype(bf16)


def forward_kernel(mid_ref, w2_ref, w3_ref, back_ref):
    backs = []
    for k in range(2):
        mid = group_rows(mid_ref, k)
        second = from_copies(w2_ref[:, :, :, 0, k * 16 : (k + 1) * 16, :])
        third = from_copies(w3_ref[:, :, :, 0, k * 16 : (k + 1) * 16, :])
        pre = dot(second.T, mid, 1, 0)
        th = jnp.tanh(C0 * (pre + C1 * (pre * pre * pre)))
        hidden = (0.5 * pre * (1.0 + th)).astype(bf16)
        backs.append(dot(third.T, hidden, 1, 0))
    back_ref[...] = both_groups(backs)


def backward_kernel(mid_ref, gb_ref, w2_ref, w3_ref, gmid_ref, grad_ref):
    outs = []
    for k in range(2):
        rows = slice(k * 16, (k + 1) * 16)
        mid = group_rows(mid_ref, k)
        g_back = group_rows(gb_ref, k)
        second = from_copies(w2_ref[:, :, :, 0, rows, :])
        third = from_copies(w3_ref[:, :, :, 0, rows, :])
        pre = dot(second.T, mid, 1, 0)
        sq = pre * pre
        th = jnp.tanh(C0 * (pre + C1 * (sq * pre)))
        hidden = (0.5 * pre * (1.0 + th)).astype(bf16)
        slope = 0.5 * (1.0 + th) + 0.5 * pre * (1.0 - th * th) * (C0 * (1.0 + 3.0 * C1 * sq))
        g_pre = (dot(third, g_back, 1, 0) * slope).astype(bf16)
        outs.append(dot(second, g_pre, 1, 0))
        grad2 = dot(mid, g_pre, 1, 1)
        grad3 = dot(hidden, g_back, 1, 1)
        grad_ref[:, :, :, 0, rows, :] = to_copies(grad2.astype(bf16))
        grad_ref[:, :, :, 1, rows, :] = to_copies(grad3.astype(bf16))
    gmid_ref[...] = both_groups(outs)


def out_kernel(back_ref, g_ref, w_ref, out_ref, grad_ref, acc_ref):
    step = pl.program_id(0)
    back = back_ref[...].reshape(BS, 1024)
    w = w_ref[...].reshape(BS, BS)

    @pl.when(step == 0)
    def _():
        acc_ref[...] = jnp.zeros_like(acc_ref)

    acc_ref[...] += dot(w.T, back, 1, 0)
    grad = dot(back, g_ref[...].reshape(1024, BS), 1, 0)
    grad_ref[...] = grad.astype(bf16).reshape(grad_ref.shape)

    @pl.when(step == 3)
    def _():
        out_ref[...] = acc_ref[...].T.astype(bf16).reshape(2, 512, BS)


def in_kernel(gmid_ref, x_ref, w_ref, others_ref, out_ref, grad_ref, acc_ref):
    step = pl.program_id(0)
    gmid = gmid_ref[...].reshape(BS, 1024)
    w = from_copies(w_ref[...])

    @pl.when(step == 0)
    def _():
        acc_ref[...] = jnp.zeros_like(acc_ref)

    acc_ref[...] += dot(w, gmid, 1, 0)
    grad = dot(gmid, x_ref[...].reshape(1024, BS), 1, 0)
    grad_ref[...] = to_copies(grad.T.astype(bf16)).reshape(grad_ref.shape)

    @pl.when(step == 3)
    def _():
        out_ref[...] = acc_ref[...].T.astype(bf16).reshape(2, 512, BS)


S = jax.ShapeDtypeStruct
SPEC_T = pl.BlockSpec((2, 512, BS), lambda q: (0, 0, 0))
SPEC_R = pl.BlockSpec((8, 32, 1024), lambda q: (q, 0, 0))
SPEC_J = pl.BlockSpec((NA, 16, 1024), lambda q: (0, q, 0))


def spec_cols(f):
    return pl.BlockSpec((2, 4, 2, 1, 16, BS), lambda q: (0, 0, 0, f, q, 0))


def spec_rows(f):
    return pl.BlockSpec((2, 1, 2, 1, 64, BS), lambda q: (0, q, 0, f, 0, 0))


def spec_pair(f):
    return pl.BlockSpec((2, 4, 2, 1, 32, BS), lambda q: (0, 0, 0, f, q, 0))


ROWS = S((NA, 32, 1024), bf16)
TOKS = S((2, 512, BS), bf16)


def body(tokens, cotangent, w_first, w_second, w_third, w_fourth):
    first = w_first.reshape(2, 16, 4, BS).transpose(0, 2, 1, 3).reshape(2, 64, BS)
    second = w_second.reshape(2, 64, BS)
    third = w_third.reshape(2, 64, BS)
    w = jnp.stack([first, w_fourth, second, third], axis=1)
    w = jnp.stack(swap((w[0], w[1])))
    w14 = lax.all_gather(w[None, None, :, :2], COPIES, axis=0, tiled=True).reshape(2, 4, 2, 2, 64, BS)
    w23 = lax.all_gather(w[None, None, :, 2:], COPIES, axis=0, tiled=True).reshape(2, 4, 2, 2, 64, BS)
    acts = jnp.stack([tokens.reshape(512, 2, BS), cotangent.reshape(512, 2, BS)])
    first_half, second_half = swap((acts[:, :, 0], acts[:, :, 1]))
    x = jnp.stack([first_half[0], second_half[0]])
    g = jnp.stack([first_half[1], second_half[1]])

    mid = call(mid_kernel, (4,), [SPEC_T, spec_cols(0)], SPEC_R, ROWS, ONE, 3 << 20)(x, w14)
    mid = lax.all_to_all(mid, WAYS, 0, 0, tiled=True)
    g_back = call(g_back_kernel, (4,), [SPEC_T, spec_rows(1)], SPEC_R, ROWS, ONE, 3 << 20)(g, w14)
    g_back = lax.all_to_all(g_back, WAYS, 0, 0, tiled=True)
    back = call(
        forward_kernel, (2,), [SPEC_J, spec_pair(0), spec_pair(1)], SPEC_J, ROWS, 2 * ONE, 5 << 20, 1 << 20
    )(mid, w23, w23)
    back = lax.all_to_all(back, WAYS, 0, 0, tiled=True)
    g_mid, grad23 = call(
        backward_kernel,
        (2,),
        [SPEC_J, SPEC_J, spec_pair(0), spec_pair(1)],
        [SPEC_J, pl.BlockSpec((2, 4, 2, 2, 32, BS), lambda q: (0, 0, 0, 0, q, 0))],
        [ROWS, S((2, 4, 2, 2, 64, BS), bf16)],
        5 * ONE,
        8 << 20,
        1 << 20,
    )(mid, g_back, w23, w23)
    g_mid = lax.all_to_all(g_mid, WAYS, 0, 0, tiled=True)
    acc = pltpu.VMEM((BS, 1024), f32)
    params = pltpu.CompilerParams(vmem_limit_bytes=48 * 1024 * 1024)
    out, grad14 = pl.pallas_call(
        out_kernel,
        grid=(4,),
        in_specs=[SPEC_R, SPEC_T, spec_rows(1)],
        out_specs=[SPEC_T, spec_rows(1)],
        out_shape=[TOKS, S((2, 4, 2, 2, 64, BS), bf16)],
        scratch_shapes=[acc],
        compiler_params=params,
        cost_estimate=pl.CostEstimate(flops=2 * ONE, bytes_accessed=4 << 20, transcendentals=0),
    )(back, g, w14)
    g_in, grad14 = pl.pallas_call(
        in_kernel,
        grid=(4,),
        in_specs=[SPEC_R, SPEC_T, spec_cols(0), pl.BlockSpec(memory_space=pl.ANY)],
        out_specs=[SPEC_T, spec_cols(0)],
        out_shape=[TOKS, S((2, 4, 2, 2, 64, BS), bf16)],
        input_output_aliases={3: 1},
        scratch_shapes=[acc],
        compiler_params=params,
        cost_estimate=pl.CostEstimate(flops=2 * ONE, bytes_accessed=4 << 20, transcendentals=0),
    )(g_mid, x, w14, grad14)

    out = jnp.concatenate(swap((out[0], out[1])), axis=1)
    g_in = jnp.concatenate(swap((g_in[0], g_in[1])), axis=1)
    grad23 = grad23.reshape(8, 2, 2, 64, BS)
    grad14 = grad14.reshape(8, 2, 2, 64, BS)
    sum23 = lax.psum_scatter(grad23, COPIES, scatter_dimension=0, tiled=True)[0]
    sum14 = lax.psum_scatter(grad14, COPIES, scatter_dimension=0, tiled=True)[0]
    sum23 = jnp.stack(swap((sum23[0], sum23[1]))).astype(f32)
    sum14 = jnp.stack(swap((sum14[0], sum14[1]))).astype(f32)
    sum1 = sum14[:, 0].reshape(2, 4, 16, BS).transpose(0, 2, 1, 3).reshape(2, 16, 1024)
    return (
        out,
        g_in,
        sum1,
        sum23[:, 0].reshape(8, 16, BS),
        sum23[:, 1].reshape(8, 16, BS),
        sum14[:, 1],
    )


def solution(mesh):
    fine = Mesh(mesh.devices.reshape(4, 2, 2, 2, 4, 2), AXES)
    dp, tensor = ("zl", "x1", "x0"), ("zh", "y", "c")
    acts, weights = P(dp, tensor), P(tensor, dp, None)
    return jax.shard_map(
        body,
        mesh=fine,
        in_specs=(acts, acts, weights, weights, weights, weights),
        out_specs=(acts, acts, weights, weights, weights, weights),
        check_vma=False,
    )
```

time: 888 us -> 361 us (0.41)
  the two profiles are of different devices: /device:TPU:16 before, /device:TPU:36 now
where the time goes in v1:
time: 361 us; the launch traced here: 360 us
  waiting for transfers between devices  205 us (57%)
  starting transfers between devices  92.6 us (26%)
  local copies, waits for them, and re-layouts  21.9 us (6%)
  Pallas kernels  19.4 us (5%)
  between operations  14.1 us (4%)
  other arithmetic  7.74 us (2%)
    ppermute x12, waiting for transfers between devices, swap(): got.append(lax.ppermute(piece, ('x1', 'x0', 'zh'), pairs))  108 us
    ppermute x12, starting transfers between devices, swap(): got.append(lax.ppermute(piece, ('x1', 'x0', 'zh'), pairs))  63.6 us
    all_gather x1, waiting for transfers between devices, body(): lax.all_gather(w[None, None, :, 2:], COPIES, axis=0, tiled=True)  38.2 us
    all_to_all x1, waiting for transfers between devices, body(): mid = lax.all_to_all(mid, WAYS, 0, 0, tiled=True)  21.7 us
    all_to_all x1, waiting for transfers between devices, body(): g_mid = lax.all_to_all(g_mid, WAYS, 0, 0, tiled=True)  18.7 us
    unnamed x46, local copies, waits for them, and re-layouts  17.7 us
    all_to_all x1, waiting for transfers between devices, body(): back = lax.all_to_all(back, WAYS, 0, 0, tiled=True)  16.9 us
    all_to_all x1, starting transfers between devices, body(): mid = lax.all_to_all(mid, WAYS, 0, 0, tiled=True)  7.74 us
  transfers between devices with their start and end apart: 20, of which 13 were waited for; matrix products, arithmetic and copies ran while one was open for 2% of the time, Pallas kernels for 5%

profile of v1, /device:TPU:36, one launch (start us, length us, event | category | flops | bytes accessed | tf_op | source)
XLA Modules:
  0.0 360.4 jit_solution(1839215172300140343)
XLA Ops:
  7.2 0.9 copy.39
  8.1 1.0 pad_maximum_fusion.5
  9.2 8.1 %collective-permute-start.2 = (bf16[4,64,256]{2,1,0:T(8,128)(2,1)S(1)}, bf16[4,64,256]{2,1,0:T(8,128)(2,1)S(1)}, u32[]{:S(2)}, u32[]{:S(2)}) collective-permute-start(bf16[4,64,256]{2,1,0:T(8,128)(2,1)S(1)} %get-tuple-element.43), channel_id=1, source_target_pairs={{0,0},{8,32},{16,16},{24,48},{32,8},{40,40},{48,24},{56,56},{1,1},... | collective-permute-start | bytes 393224 | tf_op jit(solution)/shard_map/ppermute | solution.py:60
  17.3 1.3 collective-permute-start.3
  18.6 8.6 %collective-permute-done.2 = bf16[4,64,256]{2,1,0:T(8,128)(2,1)S(1)} collective-permute-done((bf16[4,64,256]{2,1,0:T(8,128)(2,1)S(1)}, bf16[4,64,256]{2,1,0:T(8,128)(2,1)S(1)}, u32[]{:S(2)}, u32[]{:S(2)}) %collective-permute-start.2) | collective-permute-done | bytes 131104 | tf_op jit(solution)/shard_map/ppermute | solution.py:60
  27.3 2.9 collective-permute-done.3
  30.2 0.7 pad_maximum_fusion.6
  31.9 9.7 %collective-permute-start = (bf16[2,512,256]{2,1,0:T(8,128)(2,1)S(1)}, bf16[2,512,256]{2,1,0:T(8,128)(2,1)S(1)}, u32[]{:S(2)}, u32[]{:S(2)}) collective-permute-start(bf16[2,512,256]{2,1,0:T(8,128)(2,1)S(1)} %get-tuple-element.20), channel_id=1, source_target_pairs={{0,0},{8,32},{16,16},{24,48},{32,8},{40,40},{48,24},{56,56},{1,1},... | collective-permute-start | bytes 1572872 | tf_op jit(solution)/shard_map/ppermute | solution.py:60
  41.7 1.6 collective-permute-start.1
  43.3 38.4 %collective-permute-done = bf16[2,512,256]{2,1,0:T(8,128)(2,1)S(1)} collective-permute-done((bf16[2,512,256]{2,1,0:T(8,128)(2,1)S(1)}, bf16[2,512,256]{2,1,0:T(8,128)(2,1)S(1)}, u32[]{:S(2)}, u32[]{:S(2)}) %collective-permute-start) | collective-permute-done | bytes 524320 | tf_op jit(solution)/shard_map/ppermute | solution.py:60
  81.7 13.6 %collective-permute-done.1 = bf16[2,512,256]{2,1,0:T(8,128)(2,1)S(1)} collective-permute-done((bf16[2,512,256]{2,1,0:T(8,128)(2,1)S(1)}, bf16[2,512,256]{2,1,0:T(8,128)(2,1)S(1)}, u32[]{:S(2)}, u32[]{:S(2)}) %collective-permute-start.1) | collective-permute-done | bytes 524320 | tf_op jit(solution)/shard_map/ppermute | solution.py:60
  95.4 0.8 fusion.2
  96.2 1.2 copy-done
  97.5 1.4 shard_map.109
  98.9 1.3 copy-done.5
  100.3 0.8 copy-done.6
  101.0 7.7 %all-to-all-start = ((bf16[32,32,1024]{2,1,0:T(8,128)(2,1)}), bf16[32,32,1024]{2,1,0:T(8,128)(2,1)S(1)}, u32[]{:S(2)}, u32[]{:S(2)}) async-start(bf16[32,32,1024]{2,1,0:T(8,128)(2,1)} %copy-done.5), calls=%async_computation | async-start | bytes 4194304 | tf_op jit(solution)/shard_map/all_to_all | solution.py:194
  108.8 1.0 pad_maximum_fusion.2.g_ref
  109.8 1.4 shard_map.112
  111.3 1.3 copy-done.4
  112.6 0.8 copy-done.13
  113.4 21.7 %all-to-all-done.mid_ref = bf16[32,32,1024]{2,1,0:T(8,128)(2,1)S(1)} async-done(((bf16[32,32,1024]{2,1,0:T(8,128)(2,1)}), bf16[32,32,1024]{2,1,0:T(8,128)(2,1)S(1)}, u32[]{:S(2)}, u32[]{:S(2)}) %all-to-all-start) | async-done | bytes 2097184 | tf_op jit(solution)/shard_map/all_to_all | solution.py:194
  135.1 6.8 %all-to-all-start.2 = ((bf16[32,32,1024]{2,1,0:T(8,128)(2,1)}), bf16[32,32,1024]{2,1,0:T(8,128)(2,1)}, u32[]{:S(2)}, u32[]{:S(2)}) async-start(bf16[32,32,1024]{2,1,0:T(8,128)(2,1)} %copy-done.4), calls=%async_computation.2 | async-start | bytes 4194304 | tf_op jit(solution)/shard_map/all_to_all | solution.py:196
  141.9 0.7 all-gather.7.cloned.1.call-update
  142.6 38.2 %all-gather.7.cloned.1.call-done = bf16[16,2,64,256]{3,2,1,0:T(8,128)(2,1)} async-done(((bf16[2,2,64,256]{3,2,1,0:T(8,128)(2,1)}), bf16[16,2,64,256]{3,2,1,0:T(8,128)(2,1)}) %all-gather.7.cloned.1.call-update) | async-done | bytes 1048592 | tf_op jit(solution)/shard_map/all_gather | solution.py:187
  180.9 1.2 copy-done.11
  182.1 3.0 shard_map.110
  185.1 1.3 copy-done.3
  186.4 7.5 %all-to-all-start.1 = ((bf16[32,32,1024]{2,1,0:T(8,128)(2,1)}), bf16[32,32,1024]{2,1,0:T(8,128)(2,1)}, u32[]{:S(2)}, u32[]{:S(2)}) async-start(bf16[32,32,1024]{2,1,0:T(8,128)(2,1)} %copy-done.3), calls=%async_computation.1 | async-start | bytes 4194304 | tf_op jit(solution)/shard_map/all_to_all | solution.py:200
  194.0 7.1 %shard_map.113 = (bf16[32,32,1024]{2,1,0:T(8,128)(2,1)S(1)}, bf16[2,4,2,2,64,256]{5,4,3,2,1,0:T(8,128)(2,1)S(1)}) custom-call(bf16[32,32,1024]{2,1,0:T(8,128)(2,1)} %copy-done.2, bf16[32,32,1024]{2,1,0:T(8,128)(2,1)} %all-to-all-done.2.gb_ref, bf16[2,4,2,2,64,256]{5,4,3,2,1,0:T(8,128)(2,1)S(1)} %bitcast.70, bf16[2,4,2,2,64,256]{5,4,3,2,1,0:T(8,128)(2,1)S(1)} %bitcast.71), custom_call_target="tpu_custom_call" | custom-call | flops 2684354560 | bytes 8388608 | tf_op jit(solution)/shard_map/pallas_call | solution.py:201
  201.1 1.3 copy-done.15
  202.4 1.0 copy-done.16
  203.4 16.9 %all-to-all-done.1.back_ref = bf16[32,32,1024]{2,1,0:T(8,128)(2,1)} async-done(((bf16[32,32,1024]{2,1,0:T(8,128)(2,1)}), bf16[32,32,1024]{2,1,0:T(8,128)(2,1)}, u32[]{:S(2)}, u32[]{:S(2)}) %all-to-all-start.1) | async-done | bytes 2097184 | tf_op jit(solution)/shard_map/all_to_all | solution.py:200
  220.3 6.8 %all-to-all-start.3 = ((bf16[32,32,1024]{2,1,0:T(8,128)(2,1)}), bf16[32,32,1024]{2,1,0:T(8,128)(2,1)S(1)}, u32[]{:S(2)}, u32[]{:S(2)}) async-start(bf16[32,32,1024]{2,1,0:T(8,128)(2,1)} %copy-done.15), calls=%async_computation.3 | async-start | bytes 4194304 | tf_op jit(solution)/shard_map/all_to_all | solution.py:211
  227.1 0.7 reduce-scatter.5.cloned.1.call-update
  227.8 1.0 copy-done.14
  228.9 3.9 %shard_map.111 = (bf16[2,512,256]{2,1,0:T(8,128)(2,1)S(1)}, bf16[2,4,2,2,64,256]{5,4,3,2,1,0:T(8,128)(2,1)S(1)}) custom-call(bf16[32,32,1024]{2,1,0:T(8,128)(2,1)} %all-to-all-done.1.back_ref, bf16[2,512,256]{2,1,0:T(8,128)(2,1)S(1)} %copy-done.14, bf16[2,4,2,2,64,256]{5,4,3,2,1,0:T(8,128)(2,1)S(1)} %bitcast.65), custom_call_target="tpu_custom_call" | custom-call | flops 1073741824 | bytes 4194304 | tf_op jit(solution)/shard_map/pallas_call | solution.py:214
  232.8 1.0 copy-done.8
  233.8 0.8 copy-done.17
  234.6 18.7 %all-to-all-done.3.gmid_ref = bf16[32,32,1024]{2,1,0:T(8,128)(2,1)S(1)} async-done(((bf16[32,32,1024]{2,1,0:T(8,128)(2,1)}), bf16[32,32,1024]{2,1,0:T(8,128)(2,1)S(1)}, u32[]{:S(2)}, u32[]{:S(2)}) %all-to-all-start.3) | async-done | bytes 2097184 | tf_op jit(solution)/shard_map/all_to_all | solution.py:211
  253.3 1.0 copy-done.7
  254.4 1.2 copy-done.9
  255.6 2.6 shard_map.114
  258.2 1.0 copy-done.10
  259.2 0.8 copy-done.19
  260.0 1.1 select_bitcast_fusion.3
  261.1 6.6 %collective-permute-start.6 = (bf16[512,256]{1,0:T(8,128)(2,1)S(1)}, bf16[512,256]{1,0:T(8,128)(2,1)S(1)}, u32[]{:S(2)}, u32[]{:S(2)}) collective-permute-start(bf16[512,256]{1,0:T(8,128)(2,1)S(1)} %get-tuple-element.24), channel_id=1, source_target_pairs={{0,0},{8,32},{16,16},{24,48},{32,8},{40,40},{48,24},{56,56},{1,1},... | collective-permute-start | bytes 786440 | tf_op jit(solution)/shard_map/ppermute | solution.py:60
  267.8 2.8 collective-permute-start.7
  270.5 0.9 select_bitcast_fusion.13
  271.4 7.3 %collective-permute-start.10 = (bf16[2,64,256]{2,1,0:T(8,128)(2,1)S(1)}, bf16[2,64,256]{2,1,0:T(8,128)(2,1)S(1)}, u32[]{:S(2)}, u32[]{:S(2)}) collective-permute-start(bf16[2,64,256]{2,1,0:T(8,128)(2,1)S(1)} %get-tuple-element.46), channel_id=1, source_target_pairs={{0,0},{8,32},{16,16},{24,48},{32,8},{40,40},{48,24},{56,56},{1,1},... | collective-permute-start | bytes 196616 | tf_op jit(solution)/shard_map/ppermute | solution.py:60
  278.7 3.2 collective-permute-start.11
  281.9 6.6 %collective-permute-start.4 = (bf16[512,256]{1,0:T(8,128)(2,1)S(1)}, bf16[512,256]{1,0:T(8,128)(2,1)S(1)}, u32[]{:S(2)}, u32[]{:S(2)}) collective-permute-start(bf16[512,256]{1,0:T(8,128)(2,1)S(1)} %get-tuple-element.28), channel_id=1, source_target_pairs={{0,0},{8,32},{16,16},{24,48},{32,8},{40,40},{48,24},{56,56},{1,1},... | collective-permute-start | bytes 786440 | tf_op jit(solution)/shard_map/ppermute | solution.py:60
  288.5 30.2 %collective-permute-done.10 = bf16[2,64,256]{2,1,0:T(8,128)(2,1)S(1)} collective-permute-done((bf16[2,64,256]{2,1,0:T(8,128)(2,1)S(1)}, bf16[2,64,256]{2,1,0:T(8,128)(2,1)S(1)}, u32[]{:S(2)}, u32[]{:S(2)}) %collective-permute-start.10) | collective-permute-done | bytes 65568 | tf_op jit(solution)/shard_map/ppermute | solution.py:60
  318.6 5.6 %collective-permute-start.5 = (bf16[512,256]{1,0:T(8,128)(2,1)S(1)}, bf16[512,256]{1,0:T(8,128)(2,1)S(1)}, u32[]{:S(2)}, u32[]{:S(2)}) collective-permute-start(bf16[512,256]{1,0:T(8,128)(2,1)S(1)} %get-tuple-element.29), channel_id=1, source_target_pairs={{0,16},{8,48},{16,0},{24,32},{32,24},{40,56},{48,8},{56,40},{1,17}... | collective-permute-start | bytes 786440 | tf_op jit(solution)/shard_map/ppermute | solution.py:60
  324.3 0.7 fusion.4
  325.1 0.8 pad_maximum_fusion.4
  325.9 1.6 collective-permute-done.4
  327.5 5.6 %collective-permute-done.5 = bf16[512,256]{1,0:T(8,128)(2,1)S(1)} collective-permute-done((bf16[512,256]{1,0:T(8,128)(2,1)S(1)}, bf16[512,256]{1,0:T(8,128)(2,1)S(1)}, u32[]{:S(2)}, u32[]{:S(2)}) %collective-permute-start.5) | collective-permute-done | bytes 262176 | tf_op jit(solution)/shard_map/ppermute | solution.py:60
  333.2 0.9 select_bitcast_fusion.17
  334.0 9.3 %collective-permute-start.8 = (bf16[2,64,256]{2,1,0:T(8,128)(2,1)S(1)}, bf16[2,64,256]{2,1,0:T(8,128)(2,1)S(1)}, u32[]{:S(2)}, u32[]{:S(2)}) collective-permute-start(bf16[2,64,256]{2,1,0:T(8,128)(2,1)S(1)} %get-tuple-element.50), channel_id=1, source_target_pairs={{0,0},{8,32},{16,16},{24,48},{32,8},{40,40},{48,24},{56,56},{1,1},... | collective-permute-start | bytes 196616 | tf_op jit(solution)/shard_map/ppermute | solution.py:60
  343.4 1.5 collective-permute-start.9
  344.8 0.8 pad_maximum_fusion.3
  345.7 1.1 collective-permute-done.8
  346.8 5.7 %collective-permute-done.9 = bf16[2,64,256]{2,1,0:T(8,128)(2,1)S(1)} collective-permute-done((bf16[2,64,256]{2,1,0:T(8,128)(2,1)S(1)}, bf16[2,64,256]{2,1,0:T(8,128)(2,1)S(1)}, u32[]{:S(2)}, u32[]{:S(2)}) %collective-permute-start.9) | collective-permute-done | bytes 65568 | tf_op jit(solution)/shard_map/ppermute | solution.py:60
  (59 shorter events, 2.9 us)
Async XLA Ops:
  7.2 23.8 %copy-start.20 = (bf16[512,512]{1,0:T(8,128)(2,1)S(1)}, bf16[512,512]{1,0:T(8,128)(2,1)}, u32[]{:S(2)}) copy-start(bf16[512,512]{1,0:T(8,128)(2,1)} %param.6) | copy-start | bytes 1572868
  7.2 89.1 %all-gather.5.cloned.1.call-start = ((), (), s32[]{:S(2)}) async-start(), calls=%async_computation.8 | async-start | bytes 1179648 | tf_op jit(solution)/shard_map/all_gather | solution.py:186
  8.1 23.3 %copy-start.21 = (bf16[512,512]{1,0:T(8,128)(2,1)S(1)}, bf16[512,512]{1,0:T(8,128)(2,1)}, u32[]{:S(2)}) copy-start(bf16[512,512]{1,0:T(8,128)(2,1)} %param.7) | copy-start | bytes 1572868
  9.2 18.1 %collective-permute-start.2 = (bf16[4,64,256]{2,1,0:T(8,128)(2,1)S(1)}, bf16[4,64,256]{2,1,0:T(8,128)(2,1)S(1)}, u32[]{:S(2)}, u32[]{:S(2)}) collective-permute-start(bf16[4,64,256]{2,1,0:T(8,128)(2,1)S(1)} %get-tuple-element.43), channel_id=1, source_target_pairs={{0,0},{8,32},{16,16},{24,48},{32,8},{40,40},{48,24},{56,56},{1,1},... | collective-permute-start | bytes 393224 | tf_op jit(solution)/shard_map/ppermute | solution.py:60
  17.3 12.9 %collective-permute-start.3 = (bf16[4,64,256]{2,1,0:T(8,128)(2,1)S(1)}, bf16[4,64,256]{2,1,0:T(8,128)(2,1)S(1)}, u32[]{:S(2)}, u32[]{:S(2)}) collective-permute-start(bf16[4,64,256]{2,1,0:T(8,128)(2,1)S(1)} %get-tuple-element.42), channel_id=1, source_target_pairs={{0,16},{8,48},{16,0},{24,32},{32,24},{40,56},{48,8},{56,40},{1,17}... | collective-permute-start | bytes 393224 | tf_op jit(solution)/shard_map/ppermute | solution.py:60
  31.9 49.8 %collective-permute-start = (bf16[2,512,256]{2,1,0:T(8,128)(2,1)S(1)}, bf16[2,512,256]{2,1,0:T(8,128)(2,1)S(1)}, u32[]{:S(2)}, u32[]{:S(2)}) collective-permute-start(bf16[2,512,256]{2,1,0:T(8,128)(2,1)S(1)} %get-tuple-element.20), channel_id=1, source_target_pairs={{0,0},{8,32},{16,16},{24,48},{32,8},{40,40},{48,24},{56,56},{1,1},... | collective-permute-start | bytes 1572872 | tf_op jit(solution)/shard_map/ppermute | solution.py:60
  41.7 53.6 %collective-permute-start.1 = (bf16[2,512,256]{2,1,0:T(8,128)(2,1)S(1)}, bf16[2,512,256]{2,1,0:T(8,128)(2,1)S(1)}, u32[]{:S(2)}, u32[]{:S(2)}) collective-permute-start(bf16[2,512,256]{2,1,0:T(8,128)(2,1)S(1)} %get-tuple-element.21), channel_id=1, source_target_pairs={{0,16},{8,48},{16,0},{24,32},{32,24},{40,56},{48,8},{56,40},{1,17}... | collective-permute-start | bytes 1572872 | tf_op jit(solution)/shard_map/ppermute | solution.py:60
  96.2 1.2 copy-start
  98.9 1.4 copy-start.5
  100.3 0.8 copy-start.6
  101.0 8.8 %copy-start.1 = (bf16[16,2,64,256]{3,2,1,0:T(8,128)(2,1)S(1)}, bf16[16,2,64,256]{3,2,1,0:T(8,128)(2,1)}, u32[]{:S(2)}) copy-start(bf16[16,2,64,256]{3,2,1,0:T(8,128)(2,1)} %all-gather.5.cloned.1.call-done) | copy-start | bytes 3145732
  101.0 34.0 %all-to-all-start = ((bf16[32,32,1024]{2,1,0:T(8,128)(2,1)}), bf16[32,32,1024]{2,1,0:T(8,128)(2,1)S(1)}, u32[]{:S(2)}, u32[]{:S(2)}) async-start(bf16[32,32,1024]{2,1,0:T(8,128)(2,1)} %copy-done.5), calls=%async_computation | async-start | bytes 4194304 | tf_op jit(solution)/shard_map/all_to_all | solution.py:194
  111.3 1.3 copy-start.4
  112.6 0.8 copy-start.13
  135.1 45.8 %copy-start.2 = (bf16[32,32,1024]{2,1,0:T(8,128)(2,1)}, bf16[32,32,1024]{2,1,0:T(8,128)(2,1)S(1)}, u32[]{:S(2)}) copy-start(bf16[32,32,1024]{2,1,0:T(8,128)(2,1)S(1)} %all-to-all-done.mid_ref) | copy-start | bytes 6291460
  135.1 51.4 %all-to-all-start.2 = ((bf16[32,32,1024]{2,1,0:T(8,128)(2,1)}), bf16[32,32,1024]{2,1,0:T(8,128)(2,1)}, u32[]{:S(2)}, u32[]{:S(2)}) async-start(bf16[32,32,1024]{2,1,0:T(8,128)(2,1)} %copy-done.4), calls=%async_computation.2 | async-start | bytes 4194304 | tf_op jit(solution)/shard_map/all_to_all | solution.py:196
  141.9 39.0 %all-gather.7.cloned.1.call-start = ((), (), s32[]{:S(2)}) async-start(), calls=%async_computation.9 | async-start | bytes 1179648 | tf_op jit(solution)/shard_map/all_gather | solution.py:187
  180.9 1.2 copy-start.11
  185.1 1.4 copy-start.3
  186.4 7.5 %copy-start.12 = (bf16[16,2,64,256]{3,2,1,0:T(8,128)(2,1)S(1)}, bf16[16,2,64,256]{3,2,1,0:T(8,128)(2,1)}, u32[]{:S(2)}) copy-start(bf16[16,2,64,256]{3,2,1,0:T(8,128)(2,1)} %all-gather.7.cloned.1.call-done) | copy-start | bytes 3145732
  186.4 33.8 %all-to-all-start.1 = ((bf16[32,32,1024]{2,1,0:T(8,128)(2,1)}), bf16[32,32,1024]{2,1,0:T(8,128)(2,1)}, u32[]{:S(2)}, u32[]{:S(2)}) async-start(bf16[32,32,1024]{2,1,0:T(8,128)(2,1)} %copy-done.3), calls=%async_computation.1 | async-start | bytes 4194304 | tf_op jit(solution)/shard_map/all_to_all | solution.py:200
  201.1 1.4 copy-start.15
  202.4 1.0 copy-start.16
  220.3 33.0 %all-to-all-start.3 = ((bf16[32,32,1024]{2,1,0:T(8,128)(2,1)}), bf16[32,32,1024]{2,1,0:T(8,128)(2,1)S(1)}, u32[]{:S(2)}, u32[]{:S(2)}) async-start(bf16[32,32,1024]{2,1,0:T(8,128)(2,1)} %copy-done.15), calls=%async_computation.3 | async-start | bytes 4194304 | tf_op jit(solution)/shard_map/all_to_all | solution.py:211
  227.0 43.5 %reduce-scatter.5.cloned.1.call-start = ((), (), s32[]{:S(2)}) async-start(), calls=%async_computation.7 | async-start | bytes 1179648 | tf_op jit(solution)/shard_map/reduce_scatter | solution.py:240
  227.8 105.4 %reduce-scatter.3.cloned.1.call-start = ((), (), s32[]{:S(2)}) async-start(), calls=%async_computation.6 | async-start | bytes 1179648 | tf_op jit(solution)/shard_map/reduce_scatter | solution.py:241
  227.8 1.0 copy-start.14
  232.8 1.0 copy-start.8
  233.8 0.8 copy-start.17
  253.3 1.0 copy-start.7
  254.4 1.2 copy-start.9
  258.2 1.0 copy-start.10
  259.2 0.8 copy-start.19
  260.0 21.8 %copy-start.18 = (bf16[2,512,256]{2,1,0:T(8,128)(2,1)S(1)}, bf16[2,512,256]{2,1,0:T(8,128)(2,1)}, u32[]{:S(2)}) copy-start(bf16[2,512,256]{2,1,0:T(8,128)(2,1)} %copy-done.17) | copy-start | bytes 1572868
  261.1 63.9 %collective-permute-start.6 = (bf16[512,256]{1,0:T(8,128)(2,1)S(1)}, bf16[512,256]{1,0:T(8,128)(2,1)S(1)}, u32[]{:S(2)}, u32[]{:S(2)}) collective-permute-start(bf16[512,256]{1,0:T(8,128)(2,1)S(1)} %get-tuple-element.24), channel_id=1, source_target_pairs={{0,0},{8,32},{16,16},{24,48},{32,8},{40,40},{48,24},{56,56},{1,1},... | collective-permute-start | bytes 786440 | tf_op jit(solution)/shard_map/ppermute | solution.py:60
  267.8 57.3 %collective-permute-start.7 = (bf16[512,256]{1,0:T(8,128)(2,1)S(1)}, bf16[512,256]{1,0:T(8,128)(2,1)S(1)}, u32[]{:S(2)}, u32[]{:S(2)}) collective-permute-start(bf16[512,256]{1,0:T(8,128)(2,1)S(1)} %get-tuple-element.25), channel_id=1, source_target_pairs={{0,16},{8,48},{16,0},{24,32},{32,24},{40,56},{48,8},{56,40},{1,17}... | collective-permute-start | bytes 786440 | tf_op jit(solution)/shard_map/ppermute | solution.py:60
  271.4 47.2 %collective-permute-start.10 = (bf16[2,64,256]{2,1,0:T(8,128)(2,1)S(1)}, bf16[2,64,256]{2,1,0:T(8,128)(2,1)S(1)}, u32[]{:S(2)}, u32[]{:S(2)}) collective-permute-start(bf16[2,64,256]{2,1,0:T(8,128)(2,1)S(1)} %get-tuple-element.46), channel_id=1, source_target_pairs={{0,0},{8,32},{16,16},{24,48},{32,8},{40,40},{48,24},{56,56},{1,1},... | collective-permute-start | bytes 196616 | tf_op jit(solution)/shard_map/ppermute | solution.py:60
  278.7 45.6 %collective-permute-start.11 = (bf16[2,64,256]{2,1,0:T(8,128)(2,1)S(1)}, bf16[2,64,256]{2,1,0:T(8,128)(2,1)S(1)}, u32[]{:S(2)}, u32[]{:S(2)}) collective-permute-start(bf16[2,64,256]{2,1,0:T(8,128)(2,1)S(1)} %get-tuple-element.47), channel_id=1, source_target_pairs={{0,16},{8,48},{16,0},{24,32},{32,24},{40,56},{48,8},{56,40},{1,17}... | collective-permute-start | bytes 196616 | tf_op jit(solution)/shard_map/ppermute | solution.py:60
  281.9 45.6 %collective-permute-start.4 = (bf16[512,256]{1,0:T(8,128)(2,1)S(1)}, bf16[512,256]{1,0:T(8,128)(2,1)S(1)}, u32[]{:S(2)}, u32[]{:S(2)}) collective-permute-start(bf16[512,256]{1,0:T(8,128)(2,1)S(1)} %get-tuple-element.28), channel_id=1, source_target_pairs={{0,0},{8,32},{16,16},{24,48},{32,8},{40,40},{48,24},{56,56},{1,1},... | collective-permute-start | bytes 786440 | tf_op jit(solution)/shard_map/ppermute | solution.py:60
  318.6 14.4 %collective-permute-start.5 = (bf16[512,256]{1,0:T(8,128)(2,1)S(1)}, bf16[512,256]{1,0:T(8,128)(2,1)S(1)}, u32[]{:S(2)}, u32[]{:S(2)}) collective-permute-start(bf16[512,256]{1,0:T(8,128)(2,1)S(1)} %get-tuple-element.29), channel_id=1, source_target_pairs={{0,16},{8,48},{16,0},{24,32},{32,24},{40,56},{48,8},{56,40},{1,17}... | collective-permute-start | bytes 786440 | tf_op jit(solution)/shard_map/ppermute | solution.py:60
  334.0 12.7 %collective-permute-start.8 = (bf16[2,64,256]{2,1,0:T(8,128)(2,1)S(1)}, bf16[2,64,256]{2,1,0:T(8,128)(2,1)S(1)}, u32[]{:S(2)}, u32[]{:S(2)}) collective-permute-start(bf16[2,64,256]{2,1,0:T(8,128)(2,1)S(1)} %get-tuple-element.50), channel_id=1, source_target_pairs={{0,0},{8,32},{16,16},{24,48},{32,8},{40,40},{48,24},{56,56},{1,1},... | collective-permute-start | bytes 196616 | tf_op jit(solution)/shard_map/ppermute | solution.py:60
  343.4 9.2 %collective-permute-start.9 = (bf16[2,64,256]{2,1,0:T(8,128)(2,1)S(1)}, bf16[2,64,256]{2,1,0:T(8,128)(2,1)S(1)}, u32[]{:S(2)}, u32[]{:S(2)}) collective-permute-start(bf16[2,64,256]{2,1,0:T(8,128)(2,1)S(1)} %get-tuple-element.51), channel_id=1, source_target_pairs={{0,16},{8,48},{16,0},{24,32},{32,24},{40,56},{48,8},{56,40},{1,17}... | collective-permute-start | bytes 196616 | tf_op jit(solution)/shard_map/ppermute | solution.py:60
Sparse Core Ops, SparseCore 0:
  31.1 54.8 all-gather.4
  145.1 35.7 all-gather.6
  230.4 37.0 reduce-scatter.4
  269.9 50.0 reduce-scatter.2

commit v2 on v0

v2 whole, which is shorter than its diff:
```python
import jax
import jax.numpy as jnp
from jax import lax
from jax.experimental import pallas as pl
from jax.experimental.pallas import tpu as pltpu
from jax.sharding import Mesh
from jax.sharding import PartitionSpec as P

BS = 256
NA = 32
RR = 8
ROWS = 1024
AXES = ("zl", "x1", "x0", "zh", "y", "c")
WAYS = ("x1", "y", "c", "x0")
COPIES = ("zh", "zl")
SIDE = ("x1", "x0")
FAR = ("zl", "x1", "x0", "zh")
bf16 = jnp.bfloat16
f32 = jnp.float32
C0 = 0.7978845608028654
C1 = 0.044715
VMEM = 60 * 1024 * 1024
ONE = 2 * 1024 * 1024 * 256
S = jax.ShapeDtypeStruct


def dot(a, b, ca, cb):
    return lax.dot_general(a, b, (((ca,), (cb,)), ((), ())), preferred_element_type=f32)


def pack_kernel(zh_ref, x_ref, g_ref, first_ref, fourth_ref, out_ref):
    zh = zh_ref[0]
    for p in range(2):
        acts = jnp.where(zh == p, x_ref[...], g_ref[...])
        for b in range(2):
            first = jnp.concatenate([first_ref[b, :, q * BS : q * BS + BS] for q in range(4)], axis=0)
            rows = jnp.where(zh == p, first, fourth_ref[b])
            for t in range(2):
                out_ref[0, p, b, t, :64, :] = acts[t * 64 : t * 64 + 64, b * BS : b * BS + BS]
                out_ref[0, p, b, t, 64:, :] = rows


def up_kernel(x1_ref, x_ref, g_ref, first_ref, fourth_ref, out_ref):
    first = first_ref[...].reshape(BS, BS)
    mid = dot(first.T, x_ref[...].reshape(ROWS, BS), 1, 1).astype(bf16)
    g_back = dot(fourth_ref[...].reshape(BS, BS), g_ref[...].reshape(ROWS, BS), 1, 1).astype(bf16)
    for which, values in enumerate((mid, g_back)):
        values = values.reshape(2, 2, 2, 2, 16, ROWS)
        for a in range(2):
            out_ref[a, :, :, :, which, 0] = values[:, :, a]


def group_kernel(in_ref, w_ref, out_ref, grad_ref):
    def rows_of(which, m):
        rows = in_ref[:, which, 0].astype(f32).reshape(NA, 2, RR, ROWS)
        return rows[:, m].reshape(NA * RR, ROWS).astype(bf16)

    def both(values):
        rows = [v.astype(bf16).astype(f32).reshape(NA, 1, RR, ROWS) for v in values]
        return jnp.concatenate(rows, axis=1).reshape(NA, 2 * RR, ROWS).astype(bf16)

    def swapped(values):
        return jnp.concatenate([values[:, 128:], values[:, :128]], axis=1)

    backs, g_mids = [], []
    for m in range(2):
        second = w_ref[0, :, :, 0, m].reshape(BS, BS)
        third = swapped(w_ref[0, :, :, 1, m].reshape(BS, BS))
        mid = rows_of(0, m)
        g_back = rows_of(1, m)
        pre = dot(second.T, mid, 1, 0)
        sq = pre * pre
        th = jnp.tanh(C0 * (pre + C1 * (sq * pre)))
        hidden = (0.5 * pre * (1.0 + th)).astype(bf16)
        backs.append(dot(third.T, hidden, 1, 0))
        slope = 0.5 * (1.0 + th) + 0.5 * pre * (1.0 - th * th) * (C0 * (1.0 + 3.0 * C1 * sq))
        g_pre = (dot(third, g_back, 1, 0) * slope).astype(bf16)
        g_mids.append(dot(second, g_pre, 1, 0))
        grad_ref[0, :, :, 0, m] = dot(mid, g_pre, 1, 1).astype(bf16).reshape(4, 4, 16, BS)
        grad_ref[0, :, :, 1, m] = swapped(dot(hidden, g_back, 1, 1)).astype(bf16).reshape(4, 4, 16, BS)
    out_ref[:, 0, 0] = both(g_mids)
    out_ref[:, 1, 0] = both(backs)


def down_kernel(x1_ref, in_ref, x_ref, g_ref, first_ref, fourth_ref, out_ref, in_acc, out_acc):
    step = pl.program_id(0)
    x1 = x1_ref[0]
    g_mid, back = (
        jnp.stack([in_ref[a, :, :, :, which, 0] for a in range(2)], axis=2).reshape(BS, ROWS) for which in range(2)
    )
    g_in = dot(first_ref[...].reshape(BS, BS), g_mid, 1, 0)
    out = dot(fourth_ref[...].reshape(BS, BS).T, back, 1, 0)

    @pl.when(step == 0)
    def _():
        in_acc[...] = g_in
        out_acc[...] = out

    @pl.when(step > 0)
    def _():
        in_acc[...] += g_in
        out_acc[...] += out

    grad1 = dot(g_mid, x_ref[...].reshape(ROWS, BS), 1, 0)
    grad4 = dot(back, g_ref[...].reshape(ROWS, BS), 1, 0)
    at = pl.multiple_of(64 + step * 16, 16)
    out_ref[:, x1, pl.ds(at, 16), :] = grad1.T.astype(bf16).reshape(16, 16, BS)
    out_ref[pl.ds(step * 4, 4), 1 - x1, 64:, :] = grad4.astype(bf16).reshape(4, 64, BS)

    @pl.when(step == 3)
    def _():
        out_ref[:, x1, :64, :] = in_acc[...].T.astype(bf16).reshape(16, 64, BS)
        out_ref[:, 1 - x1, :64, :] = out_acc[...].T.astype(bf16).reshape(16, 64, BS)


def unpack_kernel(zh_ref, in_ref, out_side_ref, g_in_ref, out_ref, sum1_ref, sum4_ref):
    step = pl.program_id(0)

    @pl.when(step == 0)
    def _():
        sum1_ref[...] = jnp.zeros_like(sum1_ref)
        sum4_ref[...] = jnp.zeros_like(sum4_ref)

    for b in range(2):
        for t in range(2):
            g_in_ref[t * 64 : t * 64 + 64, b * BS : b * BS + BS] = in_ref[0, 0, b, t, :64, :]
            out_ref[t * 64 : t * 64 + 64, b * BS : b * BS + BS] = out_side_ref[0, 0, b, t, :64, :]
        grad1 = in_ref[0, 0, b, 0, 64:, :].astype(f32) + in_ref[0, 0, b, 1, 64:, :].astype(f32)
        for q in range(4):
            sum1_ref[b, :, q * BS : q * BS + BS] += grad1[q * 16 : q * 16 + 16]
        sum4_ref[b] += out_side_ref[0, 0, b, 0, 64:, :].astype(f32) + out_side_ref[0, 0, b, 1, 64:, :].astype(f32)


def call(kernel, grid, in_specs, out_specs, out_shape, flops, nbytes, trans=0, scratch=()):
    return pl.pallas_call(
        kernel,
        grid_spec=pltpu.PrefetchScalarGridSpec(
            num_scalar_prefetch=1,
            grid=grid,
            in_specs=in_specs,
            out_specs=out_specs,
            scratch_shapes=scratch,
        ),
        out_shape=out_shape,
        compiler_params=pltpu.CompilerParams(vmem_limit_bytes=VMEM),
        cost_estimate=pl.CostEstimate(flops=flops, bytes_accessed=nbytes, transcendentals=trans),
    )


SPEC_X = pl.BlockSpec((16, 1, 64, BS), lambda q, x1: (0, x1[0], 0, 0))
SPEC_G = pl.BlockSpec((16, 1, 64, BS), lambda q, x1: (0, 1 - x1[0], 0, 0))
SPEC_1 = pl.BlockSpec((16, 1, 16, BS), lambda q, x1: (0, x1[0], 4 + q, 0))
SPEC_4 = pl.BlockSpec((4, 1, 64, BS), lambda q, x1: (q, 1 - x1[0], 1, 0))
SPEC_Q = pl.BlockSpec((2, 2, 2, 2, 2, 1, 16, ROWS), lambda q, x1: (0, q % 2, 0, 0, 0, q // 2, 0, 0))
SPEC_J = pl.BlockSpec((NA, 2, 1, 16, ROWS), lambda k: (0, 0, k, 0, 0))
SPEC_W = pl.BlockSpec((1, 4, 4, 2, 2, 16, BS), lambda k: (k, 0, 0, 0, 0, 0, 0))
SPEC_T = pl.BlockSpec((128, 512), lambda z, zh: (z, 0))
WIRE = (2, 4, 2, 2, 2, 2, 16, ROWS)
PAIRS = (NA, 2, 2, 16, ROWS)


def body(tokens, cotangent, w_first, w_second, w_third, w_fourth):
    x1, zh = (lax.axis_index(n).astype(jnp.int32).reshape(1) for n in ("x1", "zh"))
    inner = jnp.stack([w_second.reshape(4, 2, 16, BS), w_third.reshape(4, 2, 16, BS)], axis=1)
    inner = lax.all_to_all(inner, SIDE, 0, 0, tiled=True)
    inner = lax.all_gather(inner[None], COPIES, axis=0, tiled=True).reshape(2, 4, 4, 2, 2, 16, BS)

    outer = call(
        pack_kernel,
        (4,),
        [
            SPEC_T,
            SPEC_T,
            pl.BlockSpec((2, 16, 1024), lambda z, zh: (0, 0, 0)),
            pl.BlockSpec((2, 64, BS), lambda z, zh: (0, 0, 0)),
        ],
        pl.BlockSpec((1, 2, 2, 2, 128, BS), lambda z, zh: (z, 0, 0, 0, 0, 0)),
        S((4, 2, 2, 2, 128, BS), bf16),
        0,
        3 << 20,
    )(zh, tokens, cotangent, w_first, w_fourth)
    outer = lax.all_to_all(outer.reshape(32, 128, BS), FAR, 0, 0, tiled=True).reshape(16, 2, 128, BS)

    wire = call(up_kernel, (4,), [SPEC_X, SPEC_G, SPEC_1, SPEC_4], SPEC_Q, S(WIRE, bf16), 2 * ONE, 6 << 20)(
        x1, outer, outer, outer, outer
    )
    wire = lax.all_to_all(wire.reshape(PAIRS), WAYS, 0, 0, tiled=True)
    wire, grads = pl.pallas_call(
        group_kernel,
        grid=(2,),
        in_specs=[SPEC_J, SPEC_W],
        out_specs=[SPEC_J, SPEC_W],
        out_shape=[S(PAIRS, bf16), S((2, 4, 4, 2, 2, 16, BS), bf16)],
        compiler_params=pltpu.CompilerParams(vmem_limit_bytes=VMEM),
        cost_estimate=pl.CostEstimate(flops=6 * ONE, bytes_accessed=10 << 20, transcendentals=1 << 20),
    )(wire, inner)
    wire = lax.all_to_all(wire, WAYS, 0, 0, tiled=True)
    sums = lax.psum_scatter(grads.reshape(8, 4, 2, 2, 16, BS), COPIES, scatter_dimension=0, tiled=True)[0]
    sums = lax.all_to_all(sums, SIDE, 0, 0, tiled=True)

    acc = pltpu.VMEM((BS, ROWS), f32)
    outer = call(
        down_kernel,
        (4,),
        [SPEC_Q, SPEC_X, SPEC_G, SPEC_1, SPEC_4],
        pl.BlockSpec((16, 2, 128, BS), lambda q, x1: (0, 0, 0, 0)),
        S((16, 2, 128, BS), bf16),
        4 * ONE,
        8 << 20,
        scratch=[acc, acc],
    )(x1, wire.reshape(WIRE), outer, outer, outer, outer)

    outer = lax.all_to_all(outer.reshape(32, 128, BS), FAR, 0, 0, tiled=True).reshape(4, 2, 2, 2, 128, BS)
    g_in, out, sum1, sum4 = call(
        unpack_kernel,
        (4,),
        [
            pl.BlockSpec((1, 1, 2, 2, 128, BS), lambda z, zh: (z, zh[0], 0, 0, 0, 0)),
            pl.BlockSpec((1, 1, 2, 2, 128, BS), lambda z, zh: (z, 1 - zh[0], 0, 0, 0, 0)),
        ],
        [
            SPEC_T,
            SPEC_T,
            pl.BlockSpec((2, 16, 1024), lambda z, zh: (0, 0, 0)),
            pl.BlockSpec((2, 64, BS), lambda z, zh: (0, 0, 0)),
        ],
        [S((512, 512), bf16), S((512, 512), bf16), S((2, 16, 1024), f32), S((2, 64, BS), f32)],
        1 << 20,
        4 << 20,
    )(zh, outer, outer)
    sum2, sum3 = (sums[:, f].reshape(8, 16, BS).astype(f32) for f in range(2))
    return out, g_in, sum1, sum2, sum3, sum4


def solution(mesh):
    fine = Mesh(mesh.devices.reshape(4, 2, 2, 2, 4, 2), AXES)
    dp, tensor = ("zl", "x1", "x0"), ("zh", "y", "c")
    acts, weights = P(dp, tensor), P(tensor, dp, None)
    return jax.shard_map(
        body,
        mesh=fine,
        in_specs=(acts, acts, weights, weights, weights, weights),
        out_specs=(acts, acts, weights, weights, weights, weights),
        check_vma=False,
    )
```

time: 888 us -> 301 us (0.34)
  waiting for transfers between devices: 741 us -> 202 us
  local copies, waits for them, and re-layouts: 57.8 us -> 2.02 us
  matrix products: 35.9 us -> 0 us
  Pallas kernels: 0 us -> 30.1 us
  starting transfers between devices: 37.4 us -> 48 us
    all_gather x4 -> x1, waiting for transfers between devices: 323 us -> 40.9 us  [body(): lax.all_gather(inner[None], COPIES, axis=0, tiled=True)]
    unnamed x9 -> x2, waiting for transfers between devices: 173 us -> 1.38 us
    reduce_scatter x3 -> x1, waiting for transfers between devices: 175 us -> 40.9 us  [body(): lax.psum_scatter(grads.reshape(8, 4, 2, 2, 16, BS), COPIES, scatter_dimen...]
    all_to_all x4 -> x6, waiting for transfers between devices: 70 us -> 119 us  [the longest x2 96.2 us: body(): lax.all_to_all(outer.reshape(32, 128, BS), FAR, 0, 0, tiled=True)]
    dot_general x12 -> x0, matrix products: 35.9 us -> none  [the longest x1 6.29 us: body(): jnp.einsum('jtc,ajrt->jcar', hidden, g_back, preferred_element_type=jnp.f...]
    pallas_call x0 -> x5, Pallas kernels: none -> 30.1 us  [the longest x1 9.11 us: body(): pl.pallas_call(group_kernel, grid=(2,), in_specs=[SPEC_J, SPEC_W], out_sp...]
    all_to_all x5 -> x0, local copies, waits for them, and re-layouts: 17.8 us -> none  [the longest x4 15.5 us: to_groups(): lax.all_to_all(values, 'tensor', split_axis=1, concat_axis=0, tiled=True)]
    reshape x6 -> x0, local copies, waits for them, and re-layouts: 13.4 us -> none  [the longest x1 4.25 us: body(): jnp.einsum('tai,ajrt->aijr', inputs, g_mid, preferred_element_type=jnp.fl...]
  transfers between devices with their start and end apart: 12 -> 8, of which waited for: 9 -> 7; matrix products, arithmetic and copies ran while one was open for 8% -> 0% of each run, Pallas kernels for 0% -> 5%
where the time goes in v2:
time: 301 us; the launch traced here: 298 us
  waiting for transfers between devices  202 us (67%)
  starting transfers between devices  48 us (16%)
  Pallas kernels  30.1 us (10%)
  between operations  14.1 us (5%)
    all_to_all x2, waiting for transfers between devices, body(): lax.all_to_all(outer.reshape(32, 128, BS), FAR, 0, 0, tiled=True)  96.2 us
    all_gather x1, waiting for transfers between devices, body(): lax.all_gather(inner[None], COPIES, axis=0, tiled=True)  40.9 us
    reduce_scatter x1, waiting for transfers between devices, body(): lax.psum_scatter(grads.reshape(8, 4, 2, 2, 16, BS), COPIES, scatter_dimen...  40.9 us
    all_to_all x2, starting transfers between devices, body(): lax.all_to_all(outer.reshape(32, 128, BS), FAR, 0, 0, tiled=True)  20 us
    all_to_all x1, waiting for transfers between devices, body(): wire = lax.all_to_all(wire.reshape(PAIRS), WAYS, 0, 0, tiled=True)  11.3 us
    all_to_all x1, waiting for transfers between devices, body(): wire = lax.all_to_all(wire, WAYS, 0, 0, tiled=True)  11.2 us
    all_to_all x1, starting transfers between devices, body(): wire = lax.all_to_all(wire, WAYS, 0, 0, tiled=True)  9.77 us
    pallas_call x1, Pallas kernels, body(): pl.pallas_call(group_kernel, grid=(2,), in_specs=[SPEC_J, SPEC_W], out_sp...  9.11 us
  transfers between devices with their start and end apart: 8, of which 7 were waited for; matrix products, arithmetic and copies ran while one was open for 0% of the time, Pallas kernels for 5%

profile of v2, /device:TPU:16, one launch (start us, length us, event | category | flops | bytes accessed | tf_op | source)
XLA Modules:
  0.0 298.0 jit_solution(3132698480283983104)
XLA Ops:
  7.2 0.0 copy-start.3
  7.2 0.0 copy-start.4
  7.2 3.7 %shard_map.109 = bf16[4,2,2,2,128,256]{5,4,3,2,1,0:T(8,128)(2,1)} custom-call(s32[1]{0:T(128)} %bitcast.zh_ref, bf16[512,512]{1,0:T(8,128)(2,1)} %x_ref.1, bf16[512,512]{1,0:T(8,128)(2,1)} %g_ref.1, bf16[2,16,1024]{2,1,0:T(8,128)(2,1)} %first_ref.1, bf16[2,64,256]{2,1,0:T(8,128)(2,1)} %fourth_ref.1), custom_call_target="tpu_custom_call" | custom-call | bytes 3145728 | tf_op jit(solution)/shard_map/pallas_call | solution.py:168
  10.9 11.3 %all-to-all-start = ((bf16[32,128,256]{2,1,0:T(8,128)(2,1)}), bf16[32,128,256]{2,1,0:T(8,128)(2,1)S(1)}, u32[]{:S(2)}, u32[]{:S(2)}) async-start(bf16[32,128,256]{2,1,0:T(8,128)(2,1)} %bitcast.30), calls=%async_computation | async-start | bytes 4194304 | tf_op jit(solution)/shard_map/all_to_all | solution.py:182
  22.3 0.0 copy-done.3
  22.3 0.0 copy-done.4
  22.3 0.7 pad_maximum_fusion
  22.9 48.4 %all-to-all-done = bf16[32,128,256]{2,1,0:T(8,128)(2,1)S(1)} async-done(((bf16[32,128,256]{2,1,0:T(8,128)(2,1)}), bf16[32,128,256]{2,1,0:T(8,128)(2,1)S(1)}, u32[]{:S(2)}, u32[]{:S(2)}) %all-to-all-start) | async-done | bytes 2097184 | tf_op jit(solution)/shard_map/all_to_all | solution.py:182
  71.3 0.0 copy-start
  71.3 4.0 %all-to-all-start.2 = ((bf16[4,2,2,16,256]{4,3,2,1,0:T(8,128)(2,1)}), bf16[4,2,2,16,256]{4,3,2,1,0:T(8,128)(2,1)S(1)}, u32[]{:S(2)}, u32[]{:S(2)}) async-start(bf16[4,2,2,16,256]{4,3,2,1,0:T(8,128)(2,1)} %pad_maximum_fusion), calls=%async_computation.2 | async-start | bytes 262144 | tf_op jit(solution)/shard_map/all_to_all | solution.py:165
  75.3 0.0 copy-done
  75.3 5.5 %shard_map.110 = bf16[2,4,2,2,2,2,16,1024]{7,6,5,4,3,2,1,0:T(8,128)(2,1)} custom-call(s32[1]{0:T(128)} %bitcast.1.x1_ref, bf16[16,2,128,256]{3,2,1,0:T(8,128)(2,1)} %bitcast.19, bf16[16,2,128,256]{3,2,1,0:T(8,128)(2,1)} %bitcast.20, bf16[16,2,128,256]{3,2,1,0:T(8,128)(2,1)} %bitcast.21, bf16[16,2,128,256]{3,2,1,0:T(8,128)(2,1)} %bitcast.22), custom_call_target="tpu_custom_call" | custom-call | flops 1073741824 | bytes 6291456 | tf_op jit(solution)/shard_map/pallas_call | solution.py:184
  80.8 0.5 all-to-all-done.2
  81.3 0.0 copy-start.2
  81.3 0.7 copy-done.2
  81.9 7.5 %all-to-all-start.1 = ((bf16[32,2,2,16,1024]{4,3,2,1,0:T(8,128)(2,1)}), bf16[32,2,2,16,1024]{4,3,2,1,0:T(8,128)(2,1)}, u32[]{:S(2)}, u32[]{:S(2)}) async-start(bf16[32,2,2,16,1024]{4,3,2,1,0:T(8,128)(2,1)} %bitcast.29), calls=%async_computation.1 | async-start | bytes 8388608 | tf_op jit(solution)/shard_map/all_to_all | solution.py:187
  89.4 0.0 all-gather.3.cloned.1.call-start
  89.5 0.7 all-gather.3.cloned.1.call-update
  90.2 40.9 %all-gather.3.cloned.1.call-done = bf16[32,2,2,16,256]{4,3,2,1,0:T(8,128)(2,1)} async-done(((bf16[4,2,2,16,256]{4,3,2,1,0:T(8,128)(2,1)}), bf16[32,2,2,16,256]{4,3,2,1,0:T(8,128)(2,1)}) %all-gather.3.cloned.1.call-update) | async-done | bytes 1048592 | tf_op jit(solution)/shard_map/all_gather | solution.py:166
  131.1 11.3 %all-to-all-done.1.in_ref = bf16[32,2,2,16,1024]{4,3,2,1,0:T(8,128)(2,1)} async-done(((bf16[32,2,2,16,1024]{4,3,2,1,0:T(8,128)(2,1)}), bf16[32,2,2,16,1024]{4,3,2,1,0:T(8,128)(2,1)}, u32[]{:S(2)}, u32[]{:S(2)}) %all-to-all-start.1) | async-done | bytes 4194336 | tf_op jit(solution)/shard_map/all_to_all | solution.py:187
  142.3 9.1 %shard_map.111 = (bf16[32,2,2,16,1024]{4,3,2,1,0:T(8,128)(2,1)}, bf16[2,4,4,2,2,16,256]{6,5,4,3,2,1,0:T(8,128)(2,1)}) custom-call(bf16[32,2,2,16,1024]{4,3,2,1,0:T(8,128)(2,1)} %all-to-all-done.1.in_ref, bf16[2,4,4,2,2,16,256]{6,5,4,3,2,1,0:T(8,128)(2,1)} %bitcast.36), custom_call_target="tpu_custom_call" | custom-call | flops 3221225472 | bytes 10485760 | tf_op jit(solution)/shard_map/pallas_call | solution.py:188
  151.5 9.8 %all-to-all-start.3 = ((bf16[32,2,2,16,1024]{4,3,2,1,0:T(8,128)(2,1)}), bf16[32,2,2,16,1024]{4,3,2,1,0:T(8,128)(2,1)}, u32[]{:S(2)}, u32[]{:S(2)}) async-start(bf16[32,2,2,16,1024]{4,3,2,1,0:T(8,128)(2,1)} %get-tuple-element.12), calls=%async_computation.3 | async-start | bytes 8388608 | tf_op jit(solution)/shard_map/all_to_all | solution.py:197
  161.2 0.0 reduce-scatter.2.cloned.1.call-start
  161.3 0.7 reduce-scatter.2.cloned.1.call-update
  162.0 40.9 %reduce-scatter.2.cloned.1.call-done = bf16[1,4,2,2,16,256]{5,4,3,2,1,0:T(8,128)(2,1)} async-done(((bf16[8,4,2,2,16,256]{5,4,3,2,1,0:T(8,128)(2,1)}), bf16[1,4,2,2,16,256]{5,4,3,2,1,0:T(8,128)(2,1)}) %reduce-scatter.2.cloned.1.call-update) | async-done | bytes 131088 | tf_op jit(solution)/shard_map/reduce_scatter | solution.py:198
  202.9 11.2 %all-to-all-done.3 = bf16[32,2,2,16,1024]{4,3,2,1,0:T(8,128)(2,1)} async-done(((bf16[32,2,2,16,1024]{4,3,2,1,0:T(8,128)(2,1)}), bf16[32,2,2,16,1024]{4,3,2,1,0:T(8,128)(2,1)}, u32[]{:S(2)}, u32[]{:S(2)}) %all-to-all-start.3) | async-done | bytes 4194336 | tf_op jit(solution)/shard_map/all_to_all | solution.py:197
  214.1 6.6 %all-to-all-start.5 = ((bf16[4,2,2,16,256]{4,3,2,1,0:T(8,128)(2,1)}), bf16[4,2,2,16,256]{4,3,2,1,0:T(8,128)(2,1)S(1)}, u32[]{:S(2)}, u32[]{:S(2)}) async-start(bf16[4,2,2,16,256]{4,3,2,1,0:T(8,128)(2,1)} %bitcast.33), calls=%async_computation.6 | async-start | bytes 262144 | tf_op jit(solution)/shard_map/all_to_all | solution.py:199
  220.7 8.0 %shard_map.112 = bf16[16,2,128,256]{3,2,1,0:T(8,128)(2,1)} custom-call(s32[1]{0:T(128)} %bitcast.1.x1_ref, bf16[2,4,2,2,2,2,16,1024]{7,6,5,4,3,2,1,0:T(8,128)(2,1)} %bitcast.8.in_ref, bf16[16,2,128,256]{3,2,1,0:T(8,128)(2,1)} %bitcast.23, bf16[16,2,128,256]{3,2,1,0:T(8,128)(2,1)} %bitcast.24, bf16[16,2,128,256]{3,2,1,0:T(8,128)(2,1)} %bitcast.25, ...), custom_call_target="tpu_custom_call" | custom-call | flops 2147483648 | bytes 8388608 | tf_op jit(solution)/shard_map/pallas_call | solution.py:202
  228.8 0.0 all-to-all-done.5
  228.8 8.7 %all-to-all-start.4 = ((bf16[32,128,256]{2,1,0:T(8,128)(2,1)}), bf16[32,128,256]{2,1,0:T(8,128)(2,1)S(1)}, u32[]{:S(2)}, u32[]{:S(2)}) async-start(bf16[32,128,256]{2,1,0:T(8,128)(2,1)} %bitcast.31), calls=%async_computation.4 | async-start | bytes 4194304 | tf_op jit(solution)/shard_map/all_to_all | solution.py:213
  237.5 0.7 bitcast_convert_fusion
  238.2 47.9 %all-to-all-done.4 = bf16[32,128,256]{2,1,0:T(8,128)(2,1)S(1)} async-done(((bf16[32,128,256]{2,1,0:T(8,128)(2,1)}), bf16[32,128,256]{2,1,0:T(8,128)(2,1)S(1)}, u32[]{:S(2)}, u32[]{:S(2)}) %all-to-all-start.4) | async-done | bytes 2097184 | tf_op jit(solution)/shard_map/all_to_all | solution.py:213
  286.1 0.0 copy-start.1
  286.1 1.3 copy-done.1
  287.4 3.7 %shard_map.113 = (bf16[512,512]{1,0:T(8,128)(2,1)}, bf16[512,512]{1,0:T(8,128)(2,1)}, f32[2,16,1024]{2,1,0:T(8,128)}, f32[2,64,256]{2,1,0:T(8,128)}) custom-call(s32[1]{0:T(128)} %bitcast.zh_ref, bf16[4,2,2,2,128,256]{5,4,3,2,1,0:T(8,128)(2,1)} %bitcast.27, bf16[4,2,2,2,128,256]{5,4,3,2,1,0:T(8,128)(2,1)} %bitcast.28), custom_call_target="tpu_custom_call" | custom-call | flops 1048576 | bytes 4194304 | tf_op jit(solution)/shard_map/pallas_call | solution.py:214
  (1 shorter events, 0.0 us)
Async XLA Ops:
  7.2 15.1 %copy-start.3 = (bf16[8,16,256]{2,1,0:T(8,128)(2,1)S(1)}, bf16[8,16,256]{2,1,0:T(8,128)(2,1)}, u32[]{:S(2)}) copy-start(bf16[8,16,256]{2,1,0:T(8,128)(2,1)} %param.10) | copy-start | bytes 196612
  7.2 15.1 %copy-start.4 = (bf16[8,16,256]{2,1,0:T(8,128)(2,1)S(1)}, bf16[8,16,256]{2,1,0:T(8,128)(2,1)}, u32[]{:S(2)}) copy-start(bf16[8,16,256]{2,1,0:T(8,128)(2,1)} %param.9) | copy-start | bytes 196612
  10.9 60.4 %all-to-all-start = ((bf16[32,128,256]{2,1,0:T(8,128)(2,1)}), bf16[32,128,256]{2,1,0:T(8,128)(2,1)S(1)}, u32[]{:S(2)}, u32[]{:S(2)}) async-start(bf16[32,128,256]{2,1,0:T(8,128)(2,1)} %bitcast.30), calls=%async_computation | async-start | bytes 4194304 | tf_op jit(solution)/shard_map/all_to_all | solution.py:182
  71.3 4.0 %copy-start = (bf16[32,128,256]{2,1,0:T(8,128)(2,1)}, bf16[32,128,256]{2,1,0:T(8,128)(2,1)S(1)}, u32[]{:S(2)}) copy-start(bf16[32,128,256]{2,1,0:T(8,128)(2,1)S(1)} %all-to-all-done) | copy-start | bytes 6291460
  71.3 9.9 %all-to-all-start.2 = ((bf16[4,2,2,16,256]{4,3,2,1,0:T(8,128)(2,1)}), bf16[4,2,2,16,256]{4,3,2,1,0:T(8,128)(2,1)S(1)}, u32[]{:S(2)}, u32[]{:S(2)}) async-start(bf16[4,2,2,16,256]{4,3,2,1,0:T(8,128)(2,1)} %pad_maximum_fusion), calls=%async_computation.2 | async-start | bytes 262144 | tf_op jit(solution)/shard_map/all_to_all | solution.py:165
  81.3 0.7 copy-start.2
  81.9 60.4 %all-to-all-start.1 = ((bf16[32,2,2,16,1024]{4,3,2,1,0:T(8,128)(2,1)}), bf16[32,2,2,16,1024]{4,3,2,1,0:T(8,128)(2,1)}, u32[]{:S(2)}, u32[]{:S(2)}) async-start(bf16[32,2,2,16,1024]{4,3,2,1,0:T(8,128)(2,1)} %bitcast.29), calls=%async_computation.1 | async-start | bytes 8388608 | tf_op jit(solution)/shard_map/all_to_all | solution.py:187
  89.4 41.6 %all-gather.3.cloned.1.call-start = ((), (), s32[]{:S(2)}) async-start(), calls=%async_computation.8 | async-start | bytes 1179648 | tf_op jit(solution)/shard_map/all_gather | solution.py:166
  151.5 62.7 %all-to-all-start.3 = ((bf16[32,2,2,16,1024]{4,3,2,1,0:T(8,128)(2,1)}), bf16[32,2,2,16,1024]{4,3,2,1,0:T(8,128)(2,1)}, u32[]{:S(2)}, u32[]{:S(2)}) async-start(bf16[32,2,2,16,1024]{4,3,2,1,0:T(8,128)(2,1)} %get-tuple-element.12), calls=%async_computation.3 | async-start | bytes 8388608 | tf_op jit(solution)/shard_map/all_to_all | solution.py:197
  161.2 41.7 %reduce-scatter.2.cloned.1.call-start = ((), (), s32[]{:S(2)}) async-start(), calls=%async_computation.7 | async-start | bytes 1179648 | tf_op jit(solution)/shard_map/reduce_scatter | solution.py:198
  214.1 14.6 %all-to-all-start.5 = ((bf16[4,2,2,16,256]{4,3,2,1,0:T(8,128)(2,1)}), bf16[4,2,2,16,256]{4,3,2,1,0:T(8,128)(2,1)S(1)}, u32[]{:S(2)}, u32[]{:S(2)}) async-start(bf16[4,2,2,16,256]{4,3,2,1,0:T(8,128)(2,1)} %bitcast.33), calls=%async_computation.6 | async-start | bytes 262144 | tf_op jit(solution)/shard_map/all_to_all | solution.py:199
  228.8 57.3 %all-to-all-start.4 = ((bf16[32,128,256]{2,1,0:T(8,128)(2,1)}), bf16[32,128,256]{2,1,0:T(8,128)(2,1)S(1)}, u32[]{:S(2)}, u32[]{:S(2)}) async-start(bf16[32,128,256]{2,1,0:T(8,128)(2,1)} %bitcast.31), calls=%async_computation.4 | async-start | bytes 4194304 | tf_op jit(solution)/shard_map/all_to_all | solution.py:213
  286.1 1.3 copy-start.1
Sparse Core Ops, SparseCore 0:
  92.6 38.3 all-gather.2
  164.6 38.2 reduce-scatter.1

commit v3 on v2

v3 whole, which is shorter than its diff:
```python
import jax
import jax.numpy as jnp
from jax import lax
from jax.experimental import pallas as pl
from jax.experimental.pallas import tpu as pltpu
from jax.sharding import Mesh
from jax.sharding import PartitionSpec as P

BS = 256
NA = 32
RR = 8
ROWS = 1024
HALF = 512
AXES = ("zl", "x1", "x0", "zh", "y", "c")
WAYS = ("x1", "y", "c", "x0")
COPIES = ("zh", "zl")
SIDE = ("x1", "x0")
FAR = ("zl", "x1", "x0", "zh")
bf16 = jnp.bfloat16
f32 = jnp.float32
C0 = 0.7978845608028654
C1 = 0.044715
VMEM = 60 * 1024 * 1024
ONE = 2 * 1024 * 1024 * 256
S = jax.ShapeDtypeStruct


def dot(a, b, ca, cb):
    return lax.dot_general(a, b, (((ca,), (cb,)), ((), ())), preferred_element_type=f32)


def pack_weights_kernel(zh_ref, first_ref, second_ref, third_ref, fourth_ref, out_ref):
    zh = zh_ref[0]
    for p in range(2):
        for b in range(2):
            x = 2 * p + b
            first = jnp.concatenate([first_ref[b, :, q * BS : q * BS + BS] for q in range(4)], axis=0)
            out_ref[x, :64] = jnp.where(zh == p, first, fourth_ref[b])
            for m in range(2):
                out_ref[x, 64 + m * 16 : 80 + m * 16] = second_ref[2 * x + m]
                out_ref[x, 96 + m * 16 : 112 + m * 16] = third_ref[2 * x + m]


def unpack_weights_kernel(zh_ref, in_ref, sum1_ref, sum2_ref, sum3_ref, sum4_ref):
    zh = zh_ref[0]
    for b in range(2):
        low, high = in_ref[b, :64].astype(f32), in_ref[2 + b, :64].astype(f32)
        first = jnp.where(zh == 0, low, high)
        for q in range(4):
            sum1_ref[b, :, q * BS : q * BS + BS] = first[q * 16 : q * 16 + 16]
        sum4_ref[b] = jnp.where(zh == 0, high, low)
    for x in range(4):
        for m in range(2):
            sum2_ref[2 * x + m] = in_ref[x, 64 + m * 16 : 80 + m * 16].astype(f32)
            sum3_ref[2 * x + m] = in_ref[x, 96 + m * 16 : 112 + m * 16].astype(f32)


def pack_kernel(zh_ref, x_ref, g_ref, out_ref):
    zh = zh_ref[0]
    for p in range(2):
        acts = jnp.where(zh == p, x_ref[...], g_ref[...])
        for b in range(2):
            for t in range(2):
                out_ref[0, p, b, t] = acts[t * 64 : t * 64 + 64, b * BS : b * BS + BS]


def unpack_kernel(zh_ref, in_ref, out_side_ref, g_in_ref, out_ref):
    for b in range(2):
        for t in range(2):
            g_in_ref[t * 64 : t * 64 + 64, b * BS : b * BS + BS] = in_ref[0, 0, b, t]
            out_ref[t * 64 : t * 64 + 64, b * BS : b * BS + BS] = out_side_ref[0, 0, b, t]


def up_kernel(x1_ref, x_ref, g_ref, first_ref, fourth_ref, out_ref):
    first = first_ref[...].reshape(16, 4, 16, BS)
    first = jnp.concatenate([first[:, q].reshape(BS, BS).T for q in range(4)], axis=0)
    mid = dot(first, x_ref[...].reshape(HALF, BS), 1, 1).astype(bf16)
    g_back = dot(fourth_ref[...].reshape(ROWS, BS), g_ref[...].reshape(HALF, BS), 1, 1).astype(bf16)
    for which, values in enumerate((mid, g_back)):
        values = values.reshape(2, 4, 2, 2, 2, 16, HALF)
        for k in range(2):
            for a in range(2):
                out_ref[a, :, :, :, which, k] = values[k, :, :, a]


def group_kernel(in_ref, w_ref, out_ref, grad_ref):
    def rows_of(which, m):
        rows = in_ref[:, which, 0].astype(f32).reshape(NA, 2, RR, ROWS)
        return rows[:, m].reshape(NA * RR, ROWS).astype(bf16)

    def both(values):
        rows = [v.astype(bf16).astype(f32).reshape(NA, 1, RR, ROWS) for v in values]
        return jnp.concatenate(rows, axis=1).reshape(NA, 2 * RR, ROWS).astype(bf16)

    def swapped(values):
        return jnp.concatenate([values[:, 128:], values[:, :128]], axis=1)

    backs, g_mids = [], []
    for m in range(2):
        second = w_ref[0, :, :, m * 16 : m * 16 + 16].reshape(BS, BS)
        third = swapped(w_ref[0, :, :, 32 + m * 16 : 48 + m * 16].reshape(BS, BS))
        mid = rows_of(0, m)
        g_back = rows_of(1, m)
        pre = dot(second.T, mid, 1, 0)
        sq = pre * pre
        th = jnp.tanh(pre * (C0 + (C0 * C1) * sq))
        half = 0.5 * pre
        part = half * th
        hidden = (half + part).astype(bf16)
        backs.append(dot(third.T, hidden, 1, 0))
        slope = (0.5 + 0.5 * th) + (half - part * th) * (C0 + (3.0 * C0 * C1) * sq)
        g_pre = (dot(third, g_back, 1, 0) * slope).astype(bf16)
        g_mids.append(dot(second, g_pre, 1, 0))
        grad_ref[0, :, :, m * 16 : m * 16 + 16] = dot(mid, g_pre, 1, 1).astype(bf16).reshape(4, 4, 16, BS)
        grad3 = swapped(dot(hidden, g_back, 1, 1)).astype(bf16)
        grad_ref[0, :, :, 32 + m * 16 : 48 + m * 16] = grad3.reshape(4, 4, 16, BS)
    out_ref[:, 0, 0] = both(g_mids)
    out_ref[:, 1, 0] = both(backs)


def down_kernel(x1_ref, in_ref, x_ref, g_ref, first_ref, fourth_ref, out_ref, grad_ref, acc1, acc4):
    step = pl.program_id(0)
    x1 = x1_ref[0]
    g_mid, back = (
        jnp.stack(
            [jnp.stack([in_ref[a, :, :, :, which, k] for a in range(2)], axis=2) for k in range(2)], axis=0
        ).reshape(ROWS, HALF)
        for which in range(2)
    )
    first = first_ref[...].reshape(16, 4, 16, BS)
    first = jnp.concatenate([first[:, q].reshape(BS, BS) for q in range(4)], axis=1)
    g_in = dot(first, g_mid, 1, 0)
    out = dot(fourth_ref[...].reshape(ROWS, BS).T, back, 1, 0)
    out_ref[:, x1] = g_in.T.astype(bf16).reshape(8, 64, BS)
    out_ref[:, 1 - x1] = out.T.astype(bf16).reshape(8, 64, BS)
    grad1 = dot(g_mid, x_ref[...].reshape(HALF, BS), 1, 0)
    grad4 = dot(back, g_ref[...].reshape(HALF, BS), 1, 0)

    @pl.when(step == 0)
    def _():
        acc1[...] = grad1
        acc4[...] = grad4

    @pl.when(step == 1)
    def _():
        for q in range(4):
            rows = slice(q * BS, q * BS + BS)
            grad = (acc1[rows] + grad1[rows]).T.astype(bf16)
            grad_ref[x1, :, :, q * 16 : q * 16 + 16, :] = grad.reshape(4, 4, 16, BS)
        grad_ref[1 - x1] = (acc4[...] + grad4).astype(bf16).reshape(4, 4, 64, BS)


def call(kernel, grid, in_specs, out_specs, out_shape, flops, nbytes, trans=0, scratch=()):
    return pl.pallas_call(
        kernel,
        grid_spec=pltpu.PrefetchScalarGridSpec(
            num_scalar_prefetch=1,
            grid=grid,
            in_specs=in_specs,
            out_specs=out_specs,
            scratch_shapes=scratch,
        ),
        out_shape=out_shape,
        compiler_params=pltpu.CompilerParams(vmem_limit_bytes=VMEM),
        cost_estimate=pl.CostEstimate(flops=flops, bytes_accessed=nbytes, transcendentals=trans),
    )


SPEC_X = pl.BlockSpec((8, 1, 64, BS), lambda t, x1: (t, x1[0], 0, 0))
SPEC_G = pl.BlockSpec((8, 1, 64, BS), lambda t, x1: (t, 1 - x1[0], 0, 0))
SPEC_1 = pl.BlockSpec((1, 4, 4, 64, BS), lambda t, x1: (x1[0], 0, 0, 0, 0))
SPEC_4 = pl.BlockSpec((1, 4, 4, 64, BS), lambda t, x1: (1 - x1[0], 0, 0, 0, 0))
SPEC_Q = pl.BlockSpec((2, 4, 2, 2, 2, 2, 16, HALF), lambda t, x1: (0, 0, 0, 0, 0, 0, 0, t))
SPEC_J = pl.BlockSpec((NA, 2, 1, 16, ROWS), lambda k: (0, 0, k, 0, 0))
SPEC_W = pl.BlockSpec((1, 4, 4, 64, BS), lambda k: (k, 0, 0, 1, 0))
SPEC_GRAD = pl.BlockSpec((1, 4, 4, 64, BS), lambda k: (k, 0, 0, 0, 0))
SPEC_T = pl.BlockSpec((128, 512), lambda z, zh: (z, 0))
WIRE = (2, 4, 2, 2, 2, 2, 16, ROWS)
PAIRS = (NA, 2, 2, 16, ROWS)


def whole(shape):
    return pl.BlockSpec(shape, lambda *_: (0,) * len(shape))


FACTORS = [S((2, 16, 1024), f32), S((8, 16, BS), f32), S((8, 16, BS), f32), S((2, 64, BS), f32)]
SPEC_FACTORS = [whole(factor.shape) for factor in FACTORS]
SLOTS = (4, 2, 2, 2, 64, BS)


def body(tokens, cotangent, w_first, w_second, w_third, w_fourth):
    x1, zh = (lax.axis_index(n).astype(jnp.int32).reshape(1) for n in ("x1", "zh"))
    w = call(pack_weights_kernel, (1,), SPEC_FACTORS, whole((4, 128, BS)), S((4, 128, BS), bf16), 0, 1 << 19)(
        zh, w_first, w_second, w_third, w_fourth
    )
    w = lax.all_to_all(w, SIDE, 0, 0, tiled=True)
    acts = call(
        pack_kernel,
        (4,),
        [SPEC_T, SPEC_T],
        pl.BlockSpec((1, 2, 2, 2, 64, BS), lambda z, zh: (z, 0, 0, 0, 0, 0)),
        S(SLOTS, bf16),
        0,
        2 << 20,
    )(zh, tokens, cotangent)
    w, acts = lax.optimization_barrier((w, acts))
    w = lax.all_gather(w[None], COPIES, axis=0, tiled=True).reshape(2, 4, 4, 128, BS)
    acts = lax.all_to_all(acts.reshape(32, 64, BS), FAR, 0, 0, tiled=True).reshape(16, 2, 64, BS)

    wire = call(up_kernel, (2,), [SPEC_X, SPEC_G, SPEC_1, SPEC_4], SPEC_Q, S(WIRE, bf16), 2 * ONE, 6 << 20)(
        x1, acts, acts, w, w
    )
    wire = lax.all_to_all(wire.reshape(PAIRS), WAYS, 0, 0, tiled=True)
    wire, grads23 = pl.pallas_call(
        group_kernel,
        grid=(2,),
        in_specs=[SPEC_J, SPEC_W],
        out_specs=[SPEC_J, SPEC_GRAD],
        out_shape=[S(PAIRS, bf16), S((2, 4, 4, 64, BS), bf16)],
        compiler_params=pltpu.CompilerParams(vmem_limit_bytes=VMEM),
        cost_estimate=pl.CostEstimate(flops=6 * ONE, bytes_accessed=10 << 20, transcendentals=1 << 20),
    )(wire, w)
    wire = lax.all_to_all(wire, WAYS, 0, 0, tiled=True)
    sums23 = lax.psum_scatter(grads23.reshape(8, 4, 64, BS), COPIES, scatter_dimension=0, tiled=True)[0]

    acc = pltpu.VMEM((ROWS, BS), f32)
    acts, grads14 = call(
        down_kernel,
        (2,),
        [SPEC_Q, SPEC_X, SPEC_G, SPEC_1, SPEC_4],
        [pl.BlockSpec((8, 2, 64, BS), lambda t, x1: (t, 0, 0, 0)), whole((2, 4, 4, 64, BS))],
        [S((16, 2, 64, BS), bf16), S((2, 4, 4, 64, BS), bf16)],
        4 * ONE,
        8 << 20,
        scratch=[acc, acc],
    )(x1, wire.reshape(WIRE), acts, acts, w, w)

    sums14 = lax.psum_scatter(grads14.reshape(8, 4, 64, BS), COPIES, scatter_dimension=0, tiled=True)[0]
    acts = lax.all_to_all(acts.reshape(32, 64, BS), FAR, 0, 0, tiled=True).reshape(SLOTS)
    g_in, out = call(
        unpack_kernel,
        (4,),
        [
            pl.BlockSpec((1, 1, 2, 2, 64, BS), lambda z, zh: (z, zh[0], 0, 0, 0, 0)),
            pl.BlockSpec((1, 1, 2, 2, 64, BS), lambda z, zh: (z, 1 - zh[0], 0, 0, 0, 0)),
        ],
        [SPEC_T, SPEC_T],
        [S((512, 512), bf16), S((512, 512), bf16)],
        0,
        2 << 20,
    )(zh, acts, acts)
    sums = lax.all_to_all(jnp.concatenate([sums14, sums23], axis=1), SIDE, 0, 0, tiled=True)
    sum1, sum2, sum3, sum4 = call(
        unpack_weights_kernel, (1,), [whole((4, 128, BS))], SPEC_FACTORS, FACTORS, 0, 1 << 20
    )(zh, sums)
    return out, g_in, sum1, sum2, sum3, sum4


def solution(mesh):
    fine = Mesh(mesh.devices.reshape(4, 2, 2, 2, 4, 2), AXES)
    dp, tensor = ("zl", "x1", "x0"), ("zh", "y", "c")
    acts, weights = P(dp, tensor), P(tensor, dp, None)
    return jax.shard_map(
        body,
        mesh=fine,
        in_specs=(acts, acts, weights, weights, weights, weights),
        out_specs=(acts, acts, weights, weights, weights, weights),
        check_vma=False,
    )
```

time: 301 us -> 286 us (0.950)
  blocking collectives: 0 us -> 56.5 us
  waiting for transfers between devices: 202 us -> 146 us
  starting transfers between devices: 48 us -> 35.6 us
    all_to_all x5 -> x4, waiting for transfers between devices: 108 us -> 39.9 us  [the longest x2 33.4 us: body(): lax.all_to_all(acts.reshape(32, 64, BS), FAR, 0, 0, tiled=True)]
    all_to_all x0 -> x1, blocking collectives: none -> 56.5 us  [body(): wire = lax.all_to_all(wire.reshape(PAIRS), WAYS, 0, 0, tiled=True)]
    all_to_all x1, waiting for transfers between devices: 11.2 us -> 52.2 us  [body(): wire = lax.all_to_all(wire, WAYS, 0, 0, tiled=True)]
    all_gather x1, waiting for transfers between devices: 40.9 us -> 14.5 us  [body(): lax.all_gather(w[None], COPIES, axis=0, tiled=True)]
    all_to_all x5 -> x4, starting transfers between devices: 38.1 us -> 29 us  [the longest x2 18.8 us: body(): lax.all_to_all(acts.reshape(32, 64, BS), FAR, 0, 0, tiled=True)]
    all_to_all x1, starting transfers between devices: 9.77 us -> 6.53 us  [body(): wire = lax.all_to_all(wire, WAYS, 0, 0, tiled=True)]
    reduce_scatter x1 -> x2, waiting for transfers between devices: 40.9 us -> 38.7 us  [the longest x1 38.7 us: body(): lax.psum_scatter(grads14.reshape(8, 4, 64, BS), COPIES, scatter_dimension...]
    pallas_call x4 -> x6, Pallas kernels: 21 us -> 20.8 us  [the longest x1 6.19 us: body(): call(down_kernel, (2,), [SPEC_Q, SPEC_X, SPEC_G, SPEC_1, SPEC_4], [pl.Blo...]
  transfers between devices with their start and end apart: 8 -> 8, of which waited for: 7 -> 6; matrix products, arithmetic and copies ran while one was open for 0% -> 1% of each run, Pallas kernels for 5% -> 5%
where the time goes in v3:
time: 286 us; the launch traced here: 285 us
  waiting for transfers between devices  146 us (51%)
  blocking collectives  56.5 us (20%)
  starting transfers between devices  35.6 us (12%)
  Pallas kernels  29.8 us (10%)
  between operations  13.8 us (5%)
    all_to_all x1, blocking collectives, body(): wire = lax.all_to_all(wire.reshape(PAIRS), WAYS, 0, 0, tiled=True)  56.5 us
    all_to_all x1, waiting for transfers between devices, body(): wire = lax.all_to_all(wire, WAYS, 0, 0, tiled=True)  52.2 us
    reduce_scatter x1, waiting for transfers between devices, body(): lax.psum_scatter(grads14.reshape(8, 4, 64, BS), COPIES, scatter_dimension...  38.7 us
    all_to_all x2, waiting for transfers between devices, body(): lax.all_to_all(acts.reshape(32, 64, BS), FAR, 0, 0, tiled=True)  33.4 us
    all_to_all x2, starting transfers between devices, body(): lax.all_to_all(acts.reshape(32, 64, BS), FAR, 0, 0, tiled=True)  18.8 us
    all_gather x1, waiting for transfers between devices, body(): lax.all_gather(w[None], COPIES, axis=0, tiled=True)  14.5 us
    pallas_call x1, Pallas kernels, body(): pl.pallas_call(group_kernel, grid=(2,), in_specs=[SPEC_J, SPEC_W], out_sp...  9.04 us
    all_to_all x1, starting transfers between devices, body(): wire = lax.all_to_all(wire, WAYS, 0, 0, tiled=True)  6.53 us
  transfers between devices with their start and end apart: 8, of which 6 were waited for; matrix products, arithmetic and copies ran while one was open for 1% of the time, Pallas kernels for 5%

profile of v3, /device:TPU:16, one launch (start us, length us, event | category | flops | bytes accessed | tf_op | source)
XLA Modules:
  0.0 284.8 jit_solution(7923792155078325672)
XLA Ops:
  7.2 1.7 shard_map.109
  8.8 4.3 %all-to-all-start = ((bf16[4,128,256]{2,1,0:T(8,128)(2,1)}), bf16[4,128,256]{2,1,0:T(8,128)(2,1)S(1)}, u32[]{:S(2)}, u32[]{:S(2)}) async-start(bf16[4,128,256]{2,1,0:T(8,128)(2,1)} %shard_map.109), calls=%async_computation | async-start | bytes 524288 | tf_op jit(solution)/shard_map/all_to_all | solution.py:196
  13.1 0.0 all-gather.3.cloned.1.call-start
  13.1 3.4 %shard_map.110 = bf16[4,2,2,2,64,256]{5,4,3,2,1,0:T(8,128)(2,1)} custom-call(s32[1]{0:T(128)} %bitcast.zh_ref, bf16[512,512]{1,0:T(8,128)(2,1)} %x_ref.1, bf16[512,512]{1,0:T(8,128)(2,1)} %g_ref.1), custom_call_target="tpu_custom_call" | custom-call | bytes 2097152 | tf_op jit(solution)/shard_map/pallas_call | solution.py:197
  16.5 3.3 %all-to-all-done = bf16[4,128,256]{2,1,0:T(8,128)(2,1)S(1)} async-done(((bf16[4,128,256]{2,1,0:T(8,128)(2,1)}), bf16[4,128,256]{2,1,0:T(8,128)(2,1)S(1)}, u32[]{:S(2)}, u32[]{:S(2)}) %all-to-all-start) | async-done | bytes 262176 | tf_op jit(solution)/shard_map/all_to_all | solution.py:196
  19.8 0.0 copy-start.2
  19.8 0.7 copy-done.2
  20.5 0.0 all-gather.3.cloned.1.call-update
  20.5 9.5 %all-to-all-start.1 = ((bf16[32,64,256]{2,1,0:T(8,128)(2,1)}), bf16[32,64,256]{2,1,0:T(8,128)(2,1)S(1)}, u32[]{:S(2)}, u32[]{:S(2)}) async-start(bf16[32,64,256]{2,1,0:T(8,128)(2,1)} %bitcast.25), calls=%async_computation.1 | async-start | bytes 2097152 | tf_op jit(solution)/shard_map/all_to_all | solution.py:208
  30.0 33.4 %all-to-all-done.1 = bf16[32,64,256]{2,1,0:T(8,128)(2,1)S(1)} async-done(((bf16[32,64,256]{2,1,0:T(8,128)(2,1)}), bf16[32,64,256]{2,1,0:T(8,128)(2,1)S(1)}, u32[]{:S(2)}, u32[]{:S(2)}) %all-to-all-start.1) | async-done | bytes 1048608 | tf_op jit(solution)/shard_map/all_to_all | solution.py:208
  63.4 0.0 copy-start
  63.4 14.5 %all-gather.3.cloned.1.call-done = bf16[32,128,256]{2,1,0:T(8,128)(2,1)} async-done(((bf16[4,128,256]{2,1,0:T(8,128)(2,1)}), bf16[32,128,256]{2,1,0:T(8,128)(2,1)}) %all-gather.3.cloned.1.call-update) | async-done | bytes 2097168 | tf_op jit(solution)/shard_map/all_gather | solution.py:207
  77.9 0.0 copy-done
  77.9 4.3 %shard_map.111 = bf16[2,4,2,2,2,2,16,1024]{7,6,5,4,3,2,1,0:T(8,128)(2,1)} custom-call(s32[1]{0:T(128)} %bitcast.1.x1_ref, bf16[16,2,64,256]{3,2,1,0:T(8,128)(2,1)} %bitcast.18, bf16[16,2,64,256]{3,2,1,0:T(8,128)(2,1)} %bitcast.19, bf16[2,4,4,128,256]{4,3,2,1,0:T(8,128)(2,1)} %bitcast.13, bf16[2,4,4,128,256]{4,3,2,1,0:T(8,128)(2,1)} %bitcast.14), custom_call_target="tpu_custom_call" | custom-call | flops 1073741824 | bytes 6291456 | tf_op jit(solution)/shard_map/pallas_call | solution.py:210
  82.3 56.5 %all_to_all.30.in_ref = bf16[32,2,2,16,1024]{4,3,2,1,0:T(8,128)(2,1)} all-to-all(bf16[32,2,2,16,1024]{4,3,2,1,0:T(8,128)(2,1)} %bitcast.22), channel_id=1, replica_groups=mesh['zl'=4,'x1'=2,'x0'=2,'zh'=2,'y'=4,'c'=2] {'x1','y','c','x0'}, dimensions={0} | all-to-all | bytes 8388608 | tf_op jit(solution)/shard_map/all_to_all | solution.py:213
  138.8 9.0 %shard_map.112 = (bf16[32,2,2,16,1024]{4,3,2,1,0:T(8,128)(2,1)}, bf16[2,4,4,64,256]{4,3,2,1,0:T(8,128)(2,1)}) custom-call(bf16[32,2,2,16,1024]{4,3,2,1,0:T(8,128)(2,1)} %all_to_all.30.in_ref, bf16[2,4,4,128,256]{4,3,2,1,0:T(8,128)(2,1)} %bitcast.15), custom_call_target="tpu_custom_call" | custom-call | flops 3221225472 | bytes 10485760 | tf_op jit(solution)/shard_map/pallas_call | solution.py:214
  147.8 6.5 %all-to-all-start.3 = ((bf16[32,2,2,16,1024]{4,3,2,1,0:T(8,128)(2,1)}), bf16[32,2,2,16,1024]{4,3,2,1,0:T(8,128)(2,1)}, u32[]{:S(2)}, u32[]{:S(2)}) async-start(bf16[32,2,2,16,1024]{4,3,2,1,0:T(8,128)(2,1)} %get-tuple-element.20), calls=%async_computation.3 | async-start | bytes 8388608 | tf_op jit(solution)/shard_map/all_to_all | solution.py:223
  154.4 0.0 reduce-scatter.5.cloned.1.call-start
  154.4 0.7 reduce-scatter.5.cloned.1.call-update
  155.1 0.0 reduce-scatter.3.cloned.1.call-start
  155.2 52.2 %all-to-all-done.3 = bf16[32,2,2,16,1024]{4,3,2,1,0:T(8,128)(2,1)} async-done(((bf16[32,2,2,16,1024]{4,3,2,1,0:T(8,128)(2,1)}), bf16[32,2,2,16,1024]{4,3,2,1,0:T(8,128)(2,1)}, u32[]{:S(2)}, u32[]{:S(2)}) %all-to-all-start.3) | async-done | bytes 4194336 | tf_op jit(solution)/shard_map/all_to_all | solution.py:223
  207.3 6.2 %shard_map.113 = (bf16[16,2,64,256]{3,2,1,0:T(8,128)(2,1)}, bf16[2,4,4,64,256]{4,3,2,1,0:T(8,128)(2,1)}) custom-call(s32[1]{0:T(128)} %bitcast.1.x1_ref, bf16[2,4,2,2,2,2,16,1024]{7,6,5,4,3,2,1,0:T(8,128)(2,1)} %bitcast.6.in_ref, bf16[16,2,64,256]{3,2,1,0:T(8,128)(2,1)} %bitcast.20, bf16[16,2,64,256]{3,2,1,0:T(8,128)(2,1)} %bitcast.21, ...), custom_call_target="tpu_custom_call" | custom-call | flops 2147483648 | bytes 8388608 | tf_op jit(solution)/shard_map/pallas_call | solution.py:227
  213.5 0.0 reduce-scatter.3.cloned.1.call-update
  213.5 9.3 %all-to-all-start.4 = ((bf16[32,64,256]{2,1,0:T(8,128)(2,1)}), bf16[32,64,256]{2,1,0:T(8,128)(2,1)S(1)}, u32[]{:S(2)}, u32[]{:S(2)}) async-start(bf16[32,64,256]{2,1,0:T(8,128)(2,1)} %bitcast.27), calls=%async_computation.4 | async-start | bytes 2097152 | tf_op jit(solution)/shard_map/all_to_all | solution.py:239
  222.9 0.0 reduce-scatter.5.cloned.1.call-done
  222.9 38.7 %reduce-scatter.3.cloned.1.call-done = bf16[1,4,64,256]{3,2,1,0:T(8,128)(2,1)} async-done(((bf16[8,4,64,256]{3,2,1,0:T(8,128)(2,1)}), bf16[1,4,64,256]{3,2,1,0:T(8,128)(2,1)}) %reduce-scatter.3.cloned.1.call-update) | async-done | bytes 131088 | tf_op jit(solution)/shard_map/reduce_scatter | solution.py:238
  261.6 1.7 pad_maximum_fusion
  263.3 0.0 all-to-all-done.4
  263.3 0.0 copy-start.1
  263.3 5.9 %all-to-all-start.5 = ((bf16[4,128,256]{2,1,0:T(8,128)(2,1)}), bf16[4,128,256]{2,1,0:T(8,128)(2,1)S(1)}, u32[]{:S(2)}, u32[]{:S(2)}) async-start(bf16[4,128,256]{2,1,0:T(8,128)(2,1)} %pad_maximum_fusion), calls=%async_computation.7 | async-start | bytes 524288 | tf_op jit(solution)/shard_map/all_to_all | solution.py:252
  269.2 0.0 copy-done.1
  269.2 3.4 %shard_map.114 = (bf16[512,512]{1,0:T(8,128)(2,1)}, bf16[512,512]{1,0:T(8,128)(2,1)}) custom-call(s32[1]{0:T(128)} %bitcast.zh_ref, bf16[4,2,2,2,64,256]{5,4,3,2,1,0:T(8,128)(2,1)} %bitcast.23, bf16[4,2,2,2,64,256]{5,4,3,2,1,0:T(8,128)(2,1)} %bitcast.24), custom_call_target="tpu_custom_call" | custom-call | bytes 2097152 | tf_op jit(solution)/shard_map/pallas_call | solution.py:240
  272.6 3.3 %all-to-all-done.5.in_ref = bf16[4,128,256]{2,1,0:T(8,128)(2,1)S(1)} async-done(((bf16[4,128,256]{2,1,0:T(8,128)(2,1)}), bf16[4,128,256]{2,1,0:T(8,128)(2,1)S(1)}, u32[]{:S(2)}, u32[]{:S(2)}) %all-to-all-start.5) | async-done | bytes 262176 | tf_op jit(solution)/shard_map/all_to_all | solution.py:252
  275.9 0.0 copy-start.3
  275.9 0.7 copy-done.3
  276.6 1.7 shard_map.115
Async XLA Ops:
  8.8 11.0 %all-to-all-start = ((bf16[4,128,256]{2,1,0:T(8,128)(2,1)}), bf16[4,128,256]{2,1,0:T(8,128)(2,1)S(1)}, u32[]{:S(2)}, u32[]{:S(2)}) async-start(bf16[4,128,256]{2,1,0:T(8,128)(2,1)} %shard_map.109), calls=%async_computation | async-start | bytes 524288 | tf_op jit(solution)/shard_map/all_to_all | solution.py:196
  13.1 64.8 %all-gather.3.cloned.1.call-start = ((), (), s32[]{:S(2)}) async-start(), calls=%async_computation.10 | async-start | bytes 2359296 | tf_op jit(solution)/shard_map/all_gather | solution.py:207
  19.8 0.7 copy-start.2
  20.5 42.9 %all-to-all-start.1 = ((bf16[32,64,256]{2,1,0:T(8,128)(2,1)}), bf16[32,64,256]{2,1,0:T(8,128)(2,1)S(1)}, u32[]{:S(2)}, u32[]{:S(2)}) async-start(bf16[32,64,256]{2,1,0:T(8,128)(2,1)} %bitcast.25), calls=%async_computation.1 | async-start | bytes 2097152 | tf_op jit(solution)/shard_map/all_to_all | solution.py:208
  63.4 14.5 %copy-start = (bf16[32,64,256]{2,1,0:T(8,128)(2,1)}, bf16[32,64,256]{2,1,0:T(8,128)(2,1)S(1)}, u32[]{:S(2)}) copy-start(bf16[32,64,256]{2,1,0:T(8,128)(2,1)S(1)} %all-to-all-done.1) | copy-start | bytes 3145732
  147.8 59.5 %all-to-all-start.3 = ((bf16[32,2,2,16,1024]{4,3,2,1,0:T(8,128)(2,1)}), bf16[32,2,2,16,1024]{4,3,2,1,0:T(8,128)(2,1)}, u32[]{:S(2)}, u32[]{:S(2)}) async-start(bf16[32,2,2,16,1024]{4,3,2,1,0:T(8,128)(2,1)} %get-tuple-element.20), calls=%async_computation.3 | async-start | bytes 8388608 | tf_op jit(solution)/shard_map/all_to_all | solution.py:223
  154.4 68.5 %reduce-scatter.5.cloned.1.call-start = ((), (), s32[]{:S(2)}) async-start(), calls=%async_computation.9 | async-start | bytes 1179648 | tf_op jit(solution)/shard_map/reduce_scatter | solution.py:224
  155.1 106.5 %reduce-scatter.3.cloned.1.call-start = ((), (), s32[]{:S(2)}) async-start(), calls=%async_computation.8 | async-start | bytes 1179648 | tf_op jit(solution)/shard_map/reduce_scatter | solution.py:238
  213.5 49.8 %all-to-all-start.4 = ((bf16[32,64,256]{2,1,0:T(8,128)(2,1)}), bf16[32,64,256]{2,1,0:T(8,128)(2,1)S(1)}, u32[]{:S(2)}, u32[]{:S(2)}) async-start(bf16[32,64,256]{2,1,0:T(8,128)(2,1)} %bitcast.27), calls=%async_computation.4 | async-start | bytes 2097152 | tf_op jit(solution)/shard_map/all_to_all | solution.py:239
  263.3 5.9 %copy-start.1 = (bf16[32,64,256]{2,1,0:T(8,128)(2,1)}, bf16[32,64,256]{2,1,0:T(8,128)(2,1)S(1)}, u32[]{:S(2)}) copy-start(bf16[32,64,256]{2,1,0:T(8,128)(2,1)S(1)} %all-to-all-done.4) | copy-start | bytes 3145732
  263.3 12.5 %all-to-all-start.5 = ((bf16[4,128,256]{2,1,0:T(8,128)(2,1)}), bf16[4,128,256]{2,1,0:T(8,128)(2,1)S(1)}, u32[]{:S(2)}, u32[]{:S(2)}) async-start(bf16[4,128,256]{2,1,0:T(8,128)(2,1)} %pad_maximum_fusion), calls=%async_computation.7 | async-start | bytes 524288 | tf_op jit(solution)/shard_map/all_to_all | solution.py:252
  275.9 0.7 copy-start.3
Sparse Core Ops, SparseCore 0:
  20.7 57.2 all-gather.2
  157.7 37.1 reduce-scatter.4
  213.6 47.9 reduce-scatter.2

commit v4 on v2

v4 whole, which is shorter than its diff:
```python
import jax
import jax.numpy as jnp
from jax import lax
from jax.experimental import pallas as pl
from jax.experimental.pallas import tpu as pltpu
from jax.sharding import Mesh
from jax.sharding import PartitionSpec as P

BS = 256
NA = 32
RR = 8
ROWS = 1024
HALF = 512
AXES = ("zl", "x1", "x0", "zh", "y", "c")
WAYS = ("x1", "y", "c", "x0")
COPIES = ("zh", "zl")
SIDE = ("x1", "x0")
FAR = ("zl", "x1", "x0", "zh")
bf16 = jnp.bfloat16
f32 = jnp.float32
C0 = 0.7978845608028654
C1 = 0.044715
VMEM = 63 * 1024 * 1024 + 512 * 1024
ONE = 2 * 1024 * 1024 * 256
S = jax.ShapeDtypeStruct


def dot(a, b, ca, cb):
    return lax.dot_general(a, b, (((ca,), (cb,)), ((), ())), preferred_element_type=f32)


def pack_kernel(zh_ref, x_ref, g_ref, first_ref, fourth_ref, out_ref):
    zh = zh_ref[0]
    for p in range(2):
        acts = jnp.where(zh == p, x_ref[...], g_ref[...])
        for b in range(2):
            first = jnp.concatenate([first_ref[b, :, q * BS : q * BS + BS] for q in range(4)], axis=0)
            rows = jnp.where(zh == p, first, fourth_ref[b])
            for t in range(2):
                out_ref[0, p, b, t, :64, :] = acts[t * 64 : t * 64 + 64, b * BS : b * BS + BS]
                out_ref[0, p, b, t, 64:, :] = rows


def pack_inner_kernel(x_ref, second_ref, third_ref, *out_refs):
    for d in range(4):
        at = 2 * lax.rem(x_ref[0] + d, 4)
        for m in range(2):
            out_refs[d][m * 16 : 16 + m * 16] = second_ref[at + m]
            out_refs[d][32 + m * 16 : 48 + m * 16] = third_ref[at + m]


def unpack_inner_kernel(x_ref, *refs):
    sum2_ref, sum3_ref = refs[4:]
    for d in range(4):
        at = 2 * lax.rem(x_ref[0] + 4 - d, 4)
        for m in range(2):
            sum2_ref[at + m] = refs[d][m * 16 : 16 + m * 16].astype(f32)
            sum3_ref[at + m] = refs[d][32 + m * 16 : 48 + m * 16].astype(f32)


def arrange_kernel(at_ref, *refs):
    n = len(refs) - 1
    for d in range(n):
        refs[n][lax.rem(at_ref[0] + n - d, n)] = refs[d][...]


def add_kernel(at_ref, *refs):
    total = refs[0][0].astype(f32)
    for ref in refs[1:8]:
        total += ref[...].astype(f32)
    refs[8][...] = total.astype(bf16)


def up_kernel(x1_ref, x_ref, g_ref, first_ref, fourth_ref, out_ref):
    first = first_ref[...].reshape(16, 4, 16, BS)
    first = jnp.concatenate([first[:, q].reshape(BS, BS).T for q in range(4)], axis=0)
    mid = dot(first, x_ref[...].reshape(HALF, BS), 1, 1).astype(bf16)
    g_back = dot(fourth_ref[...].reshape(ROWS, BS), g_ref[...].reshape(HALF, BS), 1, 1).astype(bf16)
    for which, values in enumerate((mid, g_back)):
        values = values.reshape(2, 4, 2, 2, 2, 16, HALF)
        for k in range(2):
            for a in range(2):
                out_ref[a, :, :, :, which, k] = values[k, :, :, a]


def group_kernel(in_ref, w_ref, out_ref, grad_ref):
    def rows_of(which, m):
        rows = in_ref[:, which, 0].astype(f32).reshape(NA, 2, RR, ROWS)
        return rows[:, m].reshape(NA * RR, ROWS).astype(bf16)

    def both(values):
        rows = [v.astype(bf16).astype(f32).reshape(NA, 1, RR, ROWS) for v in values]
        return jnp.concatenate(rows, axis=1).reshape(NA, 2 * RR, ROWS).astype(bf16)

    def swapped(values):
        return jnp.concatenate([values[:, 128:], values[:, :128]], axis=1)

    backs, g_mids = [], []
    for m in range(2):
        second = w_ref[0, :, :, m * 16 : m * 16 + 16].reshape(BS, BS)
        third = swapped(w_ref[0, :, :, 32 + m * 16 : 48 + m * 16].reshape(BS, BS))
        mid = rows_of(0, m)
        g_back = rows_of(1, m)
        pre = dot(second.T, mid, 1, 0)
        sq = pre * pre
        th = jnp.tanh(pre * (C0 + (C0 * C1) * sq))
        half = 0.5 * pre
        part = half * th
        hidden = (half + part).astype(bf16)
        backs.append(dot(third.T, hidden, 1, 0))
        slope = (0.5 + 0.5 * th) + (half - part * th) * (C0 + (3.0 * C0 * C1) * sq)
        g_pre = (dot(third, g_back, 1, 0) * slope).astype(bf16)
        g_mids.append(dot(second, g_pre, 1, 0))
        grad_ref[0, :, :, m * 16 : m * 16 + 16] = dot(mid, g_pre, 1, 1).astype(bf16).reshape(4, 4, 16, BS)
        grad3 = swapped(dot(hidden, g_back, 1, 1)).astype(bf16)
        grad_ref[0, :, :, 32 + m * 16 : 48 + m * 16] = grad3.reshape(4, 4, 16, BS)
    out_ref[:, 0, 0] = both(g_mids)
    out_ref[:, 1, 0] = both(backs)


def down_kernel(x1_ref, in_ref, x_ref, g_ref, first_ref, fourth_ref, out_ref, acc1, acc4):
    step = pl.program_id(0)
    x1 = x1_ref[0]
    g_mid, back = (
        jnp.stack(
            [jnp.stack([in_ref[a, :, :, :, which, k] for a in range(2)], axis=2) for k in range(2)], axis=0
        ).reshape(ROWS, HALF)
        for which in range(2)
    )
    first = first_ref[...].reshape(16, 4, 16, BS)
    first = jnp.concatenate([first[:, q].reshape(BS, BS) for q in range(4)], axis=1)
    g_in = dot(first, g_mid, 1, 0)
    out = dot(fourth_ref[...].reshape(ROWS, BS).T, back, 1, 0)
    here = pl.ds(step * 8, 8)
    out_ref[here, x1, :64, :] = g_in.T.astype(bf16).reshape(8, 64, BS)
    out_ref[here, 1 - x1, :64, :] = out.T.astype(bf16).reshape(8, 64, BS)
    grad1 = dot(g_mid, x_ref[...].reshape(HALF, BS), 1, 0)
    grad4 = dot(back, g_ref[...].reshape(HALF, BS), 1, 0)

    @pl.when(step == 0)
    def _():
        acc1[...] = grad1
        acc4[...] = grad4

    @pl.when(step == 1)
    def _():
        for q in range(4):
            rows = slice(q * BS, q * BS + BS)
            grad = (acc1[rows] + grad1[rows]).T.astype(bf16)
            out_ref[:, x1, 64 + q * 16 : 80 + q * 16, :] = grad.reshape(16, 16, BS)
        out_ref[:, 1 - x1, 64:, :] = (acc4[...] + grad4).astype(bf16).reshape(16, 64, BS)


def unpack_kernel(zh_ref, in_ref, out_side_ref, g_in_ref, out_ref, sum1_ref, sum4_ref):
    step = pl.program_id(0)

    @pl.when(step == 0)
    def _():
        sum1_ref[...] = jnp.zeros_like(sum1_ref)
        sum4_ref[...] = jnp.zeros_like(sum4_ref)

    for b in range(2):
        for t in range(2):
            g_in_ref[t * 64 : t * 64 + 64, b * BS : b * BS + BS] = in_ref[0, 0, b, t, :64, :]
            out_ref[t * 64 : t * 64 + 64, b * BS : b * BS + BS] = out_side_ref[0, 0, b, t, :64, :]
        grad1 = in_ref[0, 0, b, 0, 64:, :].astype(f32) + in_ref[0, 0, b, 1, 64:, :].astype(f32)
        for q in range(4):
            sum1_ref[b, :, q * BS : q * BS + BS] += grad1[q * 16 : q * 16 + 16]
        sum4_ref[b] += out_side_ref[0, 0, b, 0, 64:, :].astype(f32) + out_side_ref[0, 0, b, 1, 64:, :].astype(f32)


def call(kernel, grid, in_specs, out_specs, out_shape, flops, nbytes, trans=0, scratch=()):
    return pl.pallas_call(
        kernel,
        grid_spec=pltpu.PrefetchScalarGridSpec(
            num_scalar_prefetch=1,
            grid=grid,
            in_specs=in_specs,
            out_specs=out_specs,
            scratch_shapes=scratch,
        ),
        out_shape=out_shape,
        compiler_params=pltpu.CompilerParams(vmem_limit_bytes=VMEM),
        cost_estimate=pl.CostEstimate(flops=flops, bytes_accessed=nbytes, transcendentals=trans),
    )


SPEC_X = pl.BlockSpec((8, 1, 64, BS), lambda t, x1: (t, x1[0], 0, 0))
SPEC_G = pl.BlockSpec((8, 1, 64, BS), lambda t, x1: (t, 1 - x1[0], 0, 0))
SPEC_1 = pl.BlockSpec((16, 1, 64, BS), lambda t, x1: (0, x1[0], 1, 0))
SPEC_4 = pl.BlockSpec((16, 1, 64, BS), lambda t, x1: (0, 1 - x1[0], 1, 0))
SPEC_Q = pl.BlockSpec((2, 4, 2, 2, 2, 2, 16, HALF), lambda t, x1: (0, 0, 0, 0, 0, 0, 0, t))
SPEC_J = pl.BlockSpec((NA, 2, 1, 16, ROWS), lambda k: (0, 0, k, 0, 0))
SPEC_W = pl.BlockSpec((1, 4, 4, 64, BS), lambda k: (k, 0, 0, 0, 0))
SPEC_T = pl.BlockSpec((128, 512), lambda z, zh: (z, 0))
WIRE = (2, 4, 2, 2, 2, 2, 16, ROWS)
PAIRS = (NA, 2, 2, 16, ROWS)


def whole(shape):
    return pl.BlockSpec(shape, lambda *_: (0,) * len(shape))


SLOTS = (4, 2, 2, 2, 128, BS)
PIECE = S((64, BS), bf16)
PIECES = S((4, 64, BS), bf16)
INNER = S((8, 16, BS), f32)


def along_x(values, d):
    return lax.ppermute(values, SIDE, [(i, (i + d) % 4) for i in range(4)])


def along_z(values, d):
    place = [z % 4 * 2 + z // 4 for z in range(8)]
    return lax.ppermute(values, ("zl", "zh"), [(place[z], place[(z + d) % 8]) for z in range(8)])


def body(tokens, cotangent, w_first, w_second, w_third, w_fourth):
    x1, zh = (lax.axis_index(n).astype(jnp.int32).reshape(1) for n in ("x1", "zh"))
    at_x, at_z = (lax.axis_index(n).astype(jnp.int32).reshape(1) for n in (SIDE, COPIES))
    inner = call(
        pack_inner_kernel, (1,), [whole((8, 16, BS))] * 2, [whole(PIECE.shape)] * 4, [PIECE] * 4, 0, 1 << 18
    )(at_x, w_second, w_third)
    inner = [inner[0]] + [along_x(inner[d], d) for d in (1, 2, 3)]
    inner = call(arrange_kernel, (1,), [whole(PIECE.shape)] * 4, whole(PIECES.shape), PIECES, 0, 1 << 18)(at_x, *inner)

    outer = call(
        pack_kernel,
        (4,),
        [SPEC_T, SPEC_T, whole((2, 16, 1024)), whole((2, 64, BS))],
        pl.BlockSpec((1, 2, 2, 2, 128, BS), lambda z, zh: (z, 0, 0, 0, 0, 0)),
        S(SLOTS, bf16),
        0,
        3 << 20,
    )(zh, tokens, cotangent, w_first, w_fourth)
    outer = lax.all_to_all(outer.reshape(32, 128, BS), FAR, 0, 0, tiled=True).reshape(16, 2, 128, BS)
    outer, inner = lax.optimization_barrier((outer, inner))

    wire = call(up_kernel, (2,), [SPEC_X, SPEC_G, SPEC_1, SPEC_4], SPEC_Q, S(WIRE, bf16), 2 * ONE, 6 << 20)(
        x1, outer, outer, outer, outer
    )
    wire, inner = lax.optimization_barrier((wire, inner))
    inner = [inner] + [along_z(inner, d) for d in range(1, 8)]
    inner = call(
        arrange_kernel, (1,), [whole(PIECES.shape)] * 8, whole((8, 4, 64, BS)), S((8, 4, 64, BS), bf16), 0, 2 << 20
    )(at_z, *inner)
    wire = lax.all_to_all(wire.reshape(PAIRS), WAYS, 0, 0, tiled=True)
    wire, grads = pl.pallas_call(
        group_kernel,
        grid=(2,),
        in_specs=[SPEC_J, SPEC_W],
        out_specs=[SPEC_J, SPEC_W],
        out_shape=[S(PAIRS, bf16), S((2, 4, 4, 64, BS), bf16)],
        compiler_params=pltpu.CompilerParams(vmem_limit_bytes=VMEM),
        cost_estimate=pl.CostEstimate(flops=6 * ONE, bytes_accessed=10 << 20, transcendentals=1 << 20),
    )(wire, inner.reshape(2, 4, 4, 64, BS))
    wire = lax.all_to_all(wire, WAYS, 0, 0, tiled=True)
    grads = grads.reshape(8, 4, 64, BS)
    sums = [
        along_z(lax.dynamic_index_in_dim(grads, lax.rem(at_z[0] + d, 8), keepdims=False), d) for d in range(1, 8)
    ]
    sums = call(
        add_kernel,
        (1,),
        [pl.BlockSpec((1, 4, 64, BS), lambda i, z: (z[0], 0, 0, 0))] + [whole(PIECES.shape)] * 7,
        whole(PIECES.shape),
        PIECES,
        1 << 20,
        2 << 20,
    )(at_z, grads, *sums)
    wire, sums = lax.optimization_barrier((wire, sums))

    acc = pltpu.VMEM((ROWS, BS), f32)
    outer = call(
        down_kernel,
        (2,),
        [SPEC_Q, SPEC_X, SPEC_G, SPEC_1, SPEC_4],
        whole((16, 2, 128, BS)),
        S((16, 2, 128, BS), bf16),
        4 * ONE,
        8 << 20,
        scratch=[acc, acc],
    )(x1, wire.reshape(WIRE), outer, outer, outer, outer)

    outer, sums = lax.optimization_barrier((outer, sums))
    sums = [lax.dynamic_index_in_dim(sums, lax.rem(at_x[0] + d, 4), keepdims=False) for d in range(4)]
    sums = [sums[0]] + [along_x(sums[d], d) for d in (1, 2, 3)]
    sum2, sum3 = call(
        unpack_inner_kernel, (1,), [whole(PIECE.shape)] * 4, [whole(INNER.shape)] * 2, [INNER] * 2, 0, 1 << 19
    )(at_x, *sums)
    outer = lax.all_to_all(outer.reshape(32, 128, BS), FAR, 0, 0, tiled=True).reshape(SLOTS)
    outer, sum2, sum3 = lax.optimization_barrier((outer, sum2, sum3))
    g_in, out, sum1, sum4 = call(
        unpack_kernel,
        (4,),
        [
            pl.BlockSpec((1, 1, 2, 2, 128, BS), lambda z, zh: (z, zh[0], 0, 0, 0, 0)),
            pl.BlockSpec((1, 1, 2, 2, 128, BS), lambda z, zh: (z, 1 - zh[0], 0, 0, 0, 0)),
        ],
        [SPEC_T, SPEC_T, whole((2, 16, 1024)), whole((2, 64, BS))],
        [S((512, 512), bf16), S((512, 512), bf16), S((2, 16, 1024), f32), S((2, 64, BS), f32)],
        1 << 20,
        4 << 20,
    )(zh, outer, outer)
    return out, g_in, sum1, sum2, sum3, sum4


def solution(mesh):
    fine = Mesh(mesh.devices.reshape(4, 2, 2, 2, 4, 2), AXES)
    dp, tensor = ("zl", "x1", "x0"), ("zh", "y", "c")
    acts, weights = P(dp, tensor), P(tensor, dp, None)
    return jax.shard_map(
        body,
        mesh=fine,
        in_specs=(acts, acts, weights, weights, weights, weights),
        out_specs=(acts, acts, weights, weights, weights, weights),
        check_vma=False,
    )
```

time: 301 us -> 274 us (0.910)
  waiting for transfers between devices: 202 us -> 148 us
  starting transfers between devices: 48 us -> 81 us
  between operations: 14.1 us -> 0.99 us
  Pallas kernels: 30.1 us -> 36.1 us
    ppermute x0 -> x20, waiting for transfers between devices: none -> 45.2 us  [the longest x14 34.6 us: along_z(): lax.ppermute(values, ('zl', 'zh'), [(place[z], place[(z + d) % 8]) for z...]
    ppermute x0 -> x20, starting transfers between devices: none -> 42.2 us  [the longest x14 30.5 us: along_z(): lax.ppermute(values, ('zl', 'zh'), [(place[z], place[(z + d) % 8]) for z...]
    all_gather x1 -> x0, waiting for transfers between devices: 40.9 us -> none  [body(): lax.all_gather(inner[None], COPIES, axis=0, tiled=True)]
    reduce_scatter x1 -> x0, waiting for transfers between devices: 40.9 us -> none  [body(): lax.psum_scatter(grads.reshape(8, 4, 2, 2, 16, BS), COPIES, scatter_dimen...]
    all_to_all x2, waiting for transfers between devices: 96.2 us -> 69.2 us  [body(): lax.all_to_all(outer.reshape(32, 128, BS), FAR, 0, 0, tiled=True)]
    all_to_all x2 -> x0, starting transfers between devices: 10.5 us -> none  [the longest x1 6.58 us: body(): sums = lax.all_to_all(sums, SIDE, 0, 0, tiled=True)]
    all_to_all x1, waiting for transfers between devices: 11.2 us -> 17.4 us  [body(): wire = lax.all_to_all(wire, WAYS, 0, 0, tiled=True)]
    pallas_call x3 -> x8, Pallas kernels: 17.3 us -> 23.4 us  [the longest x1 6.34 us: body(): call(down_kernel, (2,), [SPEC_Q, SPEC_X, SPEC_G, SPEC_1, SPEC_4], whole((...]
  transfers between devices with their start and end apart: 8 -> 24, of which waited for: 7 -> 18; matrix products, arithmetic and copies ran while one was open for 0% -> 0% of each run, Pallas kernels for 5% -> 3%
where the time goes in v4:
time: 274 us; the launch traced here: 270 us
  waiting for transfers between devices  148 us (54%)
  starting transfers between devices  81 us (30%)
  Pallas kernels  36.1 us (13%)
  local copies, waits for them, and re-layouts  3.91 us (1%)
    all_to_all x2, waiting for transfers between devices, body(): lax.all_to_all(outer.reshape(32, 128, BS), FAR, 0, 0, tiled=True)  69.2 us
    ppermute x14, waiting for transfers between devices, along_z(): lax.ppermute(values, ('zl', 'zh'), [(place[z], place[(z + d) % 8]) for z...  34.6 us
    ppermute x14, starting transfers between devices, along_z(): lax.ppermute(values, ('zl', 'zh'), [(place[z], place[(z + d) % 8]) for z...  30.5 us
    all_to_all x2, starting transfers between devices, body(): lax.all_to_all(outer.reshape(32, 128, BS), FAR, 0, 0, tiled=True)  21.4 us
    all_to_all x1, waiting for transfers between devices, body(): wire = lax.all_to_all(wire, WAYS, 0, 0, tiled=True)  17.4 us
    all_to_all x1, waiting for transfers between devices, body(): wire = lax.all_to_all(wire.reshape(PAIRS), WAYS, 0, 0, tiled=True)  16.6 us
    ppermute x6, starting transfers between devices, along_x(): return lax.ppermute(values, SIDE, [(i, (i + d) % 4) for i in range(4)])  11.7 us
    ppermute x6, waiting for transfers between devices, along_x(): return lax.ppermute(values, SIDE, [(i, (i + d) % 4) for i in range(4)])  10.5 us
  transfers between devices with their start and end apart: 24, of which 18 were waited for; matrix products, arithmetic and copies ran while one was open for 0% of the time, Pallas kernels for 3%

profile of v4, /device:TPU:16, one launch (start us, length us, event | category | flops | bytes accessed | tf_op | source)
XLA Modules:
  0.0 270.4 jit_solution(4522749330873601231)
XLA Ops:
  0.6 3.7 %shard_map.109 = bf16[4,2,2,2,128,256]{5,4,3,2,1,0:T(8,128)(2,1)} custom-call(s32[1]{0:T(128)} %bitcast.zh_ref, bf16[512,512]{1,0:T(8,128)(2,1)} %x_ref.1, bf16[512,512]{1,0:T(8,128)(2,1)} %g_ref.1, bf16[2,16,1024]{2,1,0:T(8,128)(2,1)} %first_ref.1, bf16[2,64,256]{2,1,0:T(8,128)(2,1)} %fourth_ref.1), custom_call_target="tpu_custom_call" | custom-call | bytes 3145728 | tf_op jit(solution)/shard_map/pallas_call | solution.py:228
  4.3 11.4 %all-to-all-start = ((bf16[32,128,256]{2,1,0:T(8,128)(2,1)}), bf16[32,128,256]{2,1,0:T(8,128)(2,1)}, u32[]{:S(2)}, u32[]{:S(2)}) async-start(bf16[32,128,256]{2,1,0:T(8,128)(2,1)} %bitcast.35), calls=%async_computation | async-start | bytes 4194304 | tf_op jit(solution)/shard_map/all_to_all | solution.py:237
  15.8 1.5 shard_map.110
  17.3 1.7 collective-permute-start
  19.0 2.7 collective-permute-start.1
  21.7 1.5 collective-permute-start.2
  23.2 0.2 collective-permute-done.refs_1_
  23.3 1.4 collective-permute-done.1.refs_2_
  24.7 3.2 %collective-permute-done.2.refs_3_ = bf16[64,256]{1,0:T(8,128)(2,1)S(1)} collective-permute-done((bf16[64,256]{1,0:T(8,128)(2,1)}, bf16[64,256]{1,0:T(8,128)(2,1)S(1)}, u32[]{:S(2)}, u32[]{:S(2)}) %collective-permute-start.2) | collective-permute-done | bytes 32800 | tf_op jit(solution)/shard_map/ppermute | solution.py:211
  27.9 0.6 copy-done.21
  28.5 1.5 shard_map.111.refs_0_
  30.0 34.8 %all-to-all-done = bf16[32,128,256]{2,1,0:T(8,128)(2,1)} async-done(((bf16[32,128,256]{2,1,0:T(8,128)(2,1)}), bf16[32,128,256]{2,1,0:T(8,128)(2,1)}, u32[]{:S(2)}, u32[]{:S(2)}) %all-to-all-start) | async-done | bytes 2097184 | tf_op jit(solution)/shard_map/all_to_all | solution.py:237
  64.8 4.4 %shard_map.112 = bf16[2,4,2,2,2,2,16,1024]{7,6,5,4,3,2,1,0:T(8,128)(2,1)} custom-call(s32[1]{0:T(128)} %bitcast.1.x1_ref, bf16[16,2,128,256]{3,2,1,0:T(8,128)(2,1)} %bitcast.3.x_ref.g_ref.first_ref.fourth_ref, bf16[16,2,128,256]{3,2,1,0:T(8,128)(2,1)} %bitcast.3.x_ref.g_ref.first_ref.fourth_ref, ...), custom_call_target="tpu_custom_call" | custom-call | flops 1073741824 | bytes 6291456 | tf_op jit(solution)/shard_map/pallas_call | solution.py:240
  69.2 7.3 %all-to-all-start.1 = ((bf16[32,2,2,16,1024]{4,3,2,1,0:T(8,128)(2,1)}), bf16[32,2,2,16,1024]{4,3,2,1,0:T(8,128)(2,1)}, u32[]{:S(2)}, u32[]{:S(2)}) async-start(bf16[32,2,2,16,1024]{4,3,2,1,0:T(8,128)(2,1)} %bitcast.34), calls=%async_computation.1 | async-start | bytes 8388608 | tf_op jit(solution)/shard_map/all_to_all | solution.py:248
  76.5 3.3 %collective-permute-start.3 = (bf16[4,64,256]{2,1,0:T(8,128)(2,1)S(1)}, bf16[4,64,256]{2,1,0:T(8,128)(2,1)S(1)}, u32[]{:S(2)}, u32[]{:S(2)}) collective-permute-start(bf16[4,64,256]{2,1,0:T(8,128)(2,1)S(1)} %copy-done.2), channel_id=1, source_target_pairs={{0,64},{64,128},{128,192},{192,8},{8,72},{72,136},{136,200},{200,0... | collective-permute-start | bytes 393224 | tf_op jit(solution)/shard_map/ppermute | solution.py:216
  79.8 0.1 collective-permute-start.4
  79.9 2.2 collective-permute-start.5
  82.1 4.2 %collective-permute-start.6 = (bf16[4,64,256]{2,1,0:T(8,128)(2,1)S(1)}, bf16[4,64,256]{2,1,0:T(8,128)(2,1)S(1)}, u32[]{:S(2)}, u32[]{:S(2)}) collective-permute-start(bf16[4,64,256]{2,1,0:T(8,128)(2,1)S(1)} %copy-done.2), channel_id=1, source_target_pairs={{0,8},{64,72},{128,136},{192,200},{8,0},{72,64},{136,128},{200,192... | collective-permute-start | bytes 393224 | tf_op jit(solution)/shard_map/ppermute | solution.py:216
  86.3 0.4 collective-permute-start.7
  86.7 0.0 collective-permute-done.3.refs_1_
  86.7 3.8 %collective-permute-start.8 = (bf16[4,64,256]{2,1,0:T(8,128)(2,1)S(1)}, bf16[4,64,256]{2,1,0:T(8,128)(2,1)S(1)}, u32[]{:S(2)}, u32[]{:S(2)}) collective-permute-start(bf16[4,64,256]{2,1,0:T(8,128)(2,1)S(1)} %copy-done.2), channel_id=1, source_target_pairs={{0,136},{64,200},{128,0},{192,64},{8,128},{72,192},{136,8},{200,72... | collective-permute-start | bytes 393224 | tf_op jit(solution)/shard_map/ppermute | solution.py:216
  90.5 1.2 collective-permute-done.4.refs_2_
  91.7 1.2 collective-permute-start.9
  92.9 5.4 %collective-permute-done.5.refs_3_ = bf16[4,64,256]{2,1,0:T(8,128)(2,1)S(1)} collective-permute-done((bf16[4,64,256]{2,1,0:T(8,128)(2,1)S(1)}, bf16[4,64,256]{2,1,0:T(8,128)(2,1)S(1)}, u32[]{:S(2)}, u32[]{:S(2)}) %collective-permute-start.5) | collective-permute-done | bytes 131104 | tf_op jit(solution)/shard_map/ppermute | solution.py:216
  98.3 6.2 %collective-permute-done.6.refs_4_ = bf16[4,64,256]{2,1,0:T(8,128)(2,1)S(1)} collective-permute-done((bf16[4,64,256]{2,1,0:T(8,128)(2,1)S(1)}, bf16[4,64,256]{2,1,0:T(8,128)(2,1)S(1)}, u32[]{:S(2)}, u32[]{:S(2)}) %collective-permute-start.6) | collective-permute-done | bytes 131104 | tf_op jit(solution)/shard_map/ppermute | solution.py:216
  104.5 0.0 collective-permute-done.7.refs_5_
  104.5 4.5 %collective-permute-done.8.refs_6_ = bf16[4,64,256]{2,1,0:T(8,128)(2,1)S(1)} collective-permute-done((bf16[4,64,256]{2,1,0:T(8,128)(2,1)S(1)}, bf16[4,64,256]{2,1,0:T(8,128)(2,1)S(1)}, u32[]{:S(2)}, u32[]{:S(2)}) %collective-permute-start.8) | collective-permute-done | bytes 131104 | tf_op jit(solution)/shard_map/ppermute | solution.py:216
  109.1 0.0 collective-permute-done.9.refs_7_
  109.1 0.6 copy-done.13
  109.7 0.6 copy-done.15
  110.3 2.4 shard_map.113
  112.7 16.6 %all-to-all-done.1.in_ref = bf16[32,2,2,16,1024]{4,3,2,1,0:T(8,128)(2,1)} async-done(((bf16[32,2,2,16,1024]{4,3,2,1,0:T(8,128)(2,1)}), bf16[32,2,2,16,1024]{4,3,2,1,0:T(8,128)(2,1)}, u32[]{:S(2)}, u32[]{:S(2)}) %all-to-all-start.1) | async-done | bytes 4194336 | tf_op jit(solution)/shard_map/all_to_all | solution.py:248
  129.4 9.0 %shard_map.114 = (bf16[32,2,2,16,1024]{4,3,2,1,0:T(8,128)(2,1)}, bf16[2,4,4,64,256]{4,3,2,1,0:T(8,128)(2,1)}) custom-call(bf16[32,2,2,16,1024]{4,3,2,1,0:T(8,128)(2,1)} %all-to-all-done.1.in_ref, bf16[2,4,4,64,256]{4,3,2,1,0:T(8,128)(2,1)} %bitcast.39), custom_call_target="tpu_custom_call" | custom-call | flops 3221225472 | bytes 10485760 | tf_op jit(solution)/shard_map/pallas_call | solution.py:249
  138.4 10.1 %all-to-all-start.2 = ((bf16[32,2,2,16,1024]{4,3,2,1,0:T(8,128)(2,1)}), bf16[32,2,2,16,1024]{4,3,2,1,0:T(8,128)(2,1)}, u32[]{:S(2)}, u32[]{:S(2)}) async-start(bf16[32,2,2,16,1024]{4,3,2,1,0:T(8,128)(2,1)} %get-tuple-element.37), calls=%async_computation.2 | async-start | bytes 8388608 | tf_op jit(solution)/shard_map/all_to_all | solution.py:258
  148.6 0.1 dynamic-slice_bitcast_fusion
  148.6 3.3 %collective-permute-start.10 = (bf16[4,64,256]{2,1,0:T(8,128)(2,1)S(1)}, bf16[4,64,256]{2,1,0:T(8,128)(2,1)S(1)}, u32[]{:S(2)}, u32[]{:S(2)}) collective-permute-start(bf16[4,64,256]{2,1,0:T(8,128)(2,1)S(1)} %get-tuple-element.58), channel_id=1, source_target_pairs={{0,64},{64,128},{128,192},{192,8},{8,72},{72,136},{136,200},{200,0... | collective-permute-start | bytes 393224 | tf_op jit(solution)/shard_map/ppermute | solution.py:216
  152.0 0.1 collective-permute-start.11
  152.1 2.2 collective-permute-start.12
  154.3 4.2 %collective-permute-start.13 = (bf16[4,64,256]{2,1,0:T(8,128)(2,1)S(1)}, bf16[4,64,256]{2,1,0:T(8,128)(2,1)S(1)}, u32[]{:S(2)}, u32[]{:S(2)}) collective-permute-start(bf16[4,64,256]{2,1,0:T(8,128)(2,1)S(1)} %get-tuple-element.55), channel_id=1, source_target_pairs={{0,8},{64,72},{128,136},{192,200},{8,0},{72,64},{136,128},{200,192... | collective-permute-start | bytes 393224 | tf_op jit(solution)/shard_map/ppermute | solution.py:216
  158.5 0.4 collective-permute-start.14
  158.8 3.8 %collective-permute-start.15 = (bf16[4,64,256]{2,1,0:T(8,128)(2,1)S(1)}, bf16[4,64,256]{2,1,0:T(8,128)(2,1)S(1)}, u32[]{:S(2)}, u32[]{:S(2)}) collective-permute-start(bf16[4,64,256]{2,1,0:T(8,128)(2,1)S(1)} %get-tuple-element.53), channel_id=1, source_target_pairs={{0,136},{64,200},{128,0},{192,64},{8,128},{72,192},{136,8},{200,72... | collective-permute-start | bytes 393224 | tf_op jit(solution)/shard_map/ppermute | solution.py:216
  162.7 1.2 collective-permute-done.11.refs_2_
  163.8 1.2 collective-permute-start.16
  165.1 5.4 %collective-permute-done.12.refs_3_ = bf16[4,64,256]{2,1,0:T(8,128)(2,1)S(1)} collective-permute-done((bf16[4,64,256]{2,1,0:T(8,128)(2,1)S(1)}, bf16[4,64,256]{2,1,0:T(8,128)(2,1)S(1)}, u32[]{:S(2)}, u32[]{:S(2)}) %collective-permute-start.12) | collective-permute-done | bytes 131104 | tf_op jit(solution)/shard_map/ppermute | solution.py:216
  170.5 6.2 %collective-permute-done.13.refs_4_ = bf16[4,64,256]{2,1,0:T(8,128)(2,1)S(1)} collective-permute-done((bf16[4,64,256]{2,1,0:T(8,128)(2,1)S(1)}, bf16[4,64,256]{2,1,0:T(8,128)(2,1)S(1)}, u32[]{:S(2)}, u32[]{:S(2)}) %collective-permute-start.13) | collective-permute-done | bytes 131104 | tf_op jit(solution)/shard_map/ppermute | solution.py:216
  176.7 0.0 collective-permute-done.14.refs_5_
  176.7 4.5 %collective-permute-done.15.refs_6_ = bf16[4,64,256]{2,1,0:T(8,128)(2,1)S(1)} collective-permute-done((bf16[4,64,256]{2,1,0:T(8,128)(2,1)S(1)}, bf16[4,64,256]{2,1,0:T(8,128)(2,1)S(1)}, u32[]{:S(2)}, u32[]{:S(2)}) %collective-permute-start.15) | collective-permute-done | bytes 131104 | tf_op jit(solution)/shard_map/ppermute | solution.py:216
  181.2 0.7 copy-done.14
  181.9 0.0 collective-permute-done.16.refs_7_
  181.9 2.1 shard_map.115
  184.0 17.4 %all-to-all-done.2 = bf16[32,2,2,16,1024]{4,3,2,1,0:T(8,128)(2,1)} async-done(((bf16[32,2,2,16,1024]{4,3,2,1,0:T(8,128)(2,1)}), bf16[32,2,2,16,1024]{4,3,2,1,0:T(8,128)(2,1)}, u32[]{:S(2)}, u32[]{:S(2)}) %all-to-all-start.2) | async-done | bytes 4194336 | tf_op jit(solution)/shard_map/all_to_all | solution.py:258
  201.4 6.3 %shard_map.116 = bf16[16,2,128,256]{3,2,1,0:T(8,128)(2,1)} custom-call(s32[1]{0:T(128)} %bitcast.1.x1_ref, bf16[2,4,2,2,2,2,16,1024]{7,6,5,4,3,2,1,0:T(8,128)(2,1)} %bitcast.16.in_ref, bf16[16,2,128,256]{3,2,1,0:T(8,128)(2,1)} %bitcast.3.x_ref.g_ref.first_ref.fourth_ref, bf16[16,2,128,256]{3,2,1,0:T(8,128)(2,1)} %bitcast.3.x_ref.g_ref.first_ref.fourth_ref, ...), custom_call_target="tpu_custom_call" | custom-call | flops 2147483648 | bytes 8388608 | tf_op jit(solution)/shard_map/pallas_call | solution.py:275
  207.7 10.0 %all-to-all-start.3 = ((bf16[32,128,256]{2,1,0:T(8,128)(2,1)}), bf16[32,128,256]{2,1,0:T(8,128)(2,1)}, u32[]{:S(2)}, u32[]{:S(2)}) async-start(bf16[32,128,256]{2,1,0:T(8,128)(2,1)} %bitcast.36), calls=%async_computation.3 | async-start | bytes 4194304 | tf_op jit(solution)/shard_map/all_to_all | solution.py:292
  217.8 0.6 dynamic-slice_bitcast_fusion.7
  218.4 1.7 collective-permute-start.17
  220.1 2.7 collective-permute-start.18
  222.8 1.5 collective-permute-start.19
  224.2 0.5 collective-permute-done.17.refs_1_
  224.7 1.5 collective-permute-done.18.refs_2_
  226.2 3.8 %collective-permute-done.19.refs_3_ = bf16[64,256]{1,0:T(8,128)(2,1)S(1)} collective-permute-done((bf16[64,256]{1,0:T(8,128)(2,1)S(1)}, bf16[64,256]{1,0:T(8,128)(2,1)S(1)}, u32[]{:S(2)}, u32[]{:S(2)}) %collective-permute-start.19) | collective-permute-done | bytes 32800 | tf_op jit(solution)/shard_map/ppermute | solution.py:211
  230.1 0.6 copy-done.18
  230.7 1.5 shard_map.117
  232.2 34.4 %all-to-all-done.3 = bf16[32,128,256]{2,1,0:T(8,128)(2,1)} async-done(((bf16[32,128,256]{2,1,0:T(8,128)(2,1)}), bf16[32,128,256]{2,1,0:T(8,128)(2,1)}, u32[]{:S(2)}, u32[]{:S(2)}) %all-to-all-start.3) | async-done | bytes 2097184 | tf_op jit(solution)/shard_map/all_to_all | solution.py:292
  266.6 3.7 %shard_map.118 = (bf16[512,512]{1,0:T(8,128)(2,1)}, bf16[512,512]{1,0:T(8,128)(2,1)}, f32[2,16,1024]{2,1,0:T(8,128)}, f32[2,64,256]{2,1,0:T(8,128)}) custom-call(s32[1]{0:T(128)} %bitcast.zh_ref, bf16[4,2,2,2,128,256]{5,4,3,2,1,0:T(8,128)(2,1)} %bitcast.18.in_ref.out_side_ref, bf16[4,2,2,2,128,256]{5,4,3,2,1,0:T(8,128)(2,1)} %bitcast.18.in_ref.out_side_ref), custom_call_target="tpu_custom_call" | custom-call | flops 1048576 | bytes 4194304 | tf_op jit(solution)/shard_map/pallas_call | solution.py:294
  (40 shorter events, 0.1 us)
Async XLA Ops:
  4.3 60.5 %all-to-all-start = ((bf16[32,128,256]{2,1,0:T(8,128)(2,1)}), bf16[32,128,256]{2,1,0:T(8,128)(2,1)}, u32[]{:S(2)}, u32[]{:S(2)}) async-start(bf16[32,128,256]{2,1,0:T(8,128)(2,1)} %bitcast.35), calls=%async_computation | async-start | bytes 4194304 | tf_op jit(solution)/shard_map/all_to_all | solution.py:237
  17.3 6.0 %collective-permute-start = (bf16[64,256]{1,0:T(8,128)(2,1)}, bf16[64,256]{1,0:T(8,128)(2,1)S(1)}, u32[]{:S(2)}, u32[]{:S(2)}) collective-permute-start(bf16[64,256]{1,0:T(8,128)(2,1)} %get-tuple-element.30), channel_id=1, source_target_pairs={{0,16},{16,32},{32,48},{48,0},{1,17},{17,33},{33,49},{49,1},{2,18}... | collective-permute-start | bytes 98312 | tf_op jit(solution)/shard_map/ppermute | solution.py:211
  19.0 5.7 %collective-permute-start.1 = (bf16[64,256]{1,0:T(8,128)(2,1)}, bf16[64,256]{1,0:T(8,128)(2,1)S(1)}, u32[]{:S(2)}, u32[]{:S(2)}) collective-permute-start(bf16[64,256]{1,0:T(8,128)(2,1)} %get-tuple-element.31), channel_id=1, source_target_pairs={{0,32},{16,48},{32,0},{48,16},{1,33},{17,49},{33,1},{49,17},{2,34}... | collective-permute-start | bytes 98312 | tf_op jit(solution)/shard_map/ppermute | solution.py:211
  21.7 6.2 %collective-permute-start.2 = (bf16[64,256]{1,0:T(8,128)(2,1)}, bf16[64,256]{1,0:T(8,128)(2,1)S(1)}, u32[]{:S(2)}, u32[]{:S(2)}) collective-permute-start(bf16[64,256]{1,0:T(8,128)(2,1)} %get-tuple-element.32), channel_id=1, source_target_pairs={{0,48},{16,0},{32,16},{48,32},{1,49},{17,1},{33,17},{49,33},{2,50}... | collective-permute-start | bytes 98312 | tf_op jit(solution)/shard_map/ppermute | solution.py:211
  23.3 4.6 %copy-start.19 = (bf16[64,256]{1,0:T(8,128)(2,1)}, bf16[64,256]{1,0:T(8,128)(2,1)S(1)}, u32[]{:S(2)}) copy-start(bf16[64,256]{1,0:T(8,128)(2,1)S(1)} %collective-permute-done.refs_1_) | copy-start | bytes 98308
  24.7 3.2 %copy-start.20 = (bf16[64,256]{1,0:T(8,128)(2,1)}, bf16[64,256]{1,0:T(8,128)(2,1)S(1)}, u32[]{:S(2)}) copy-start(bf16[64,256]{1,0:T(8,128)(2,1)S(1)} %collective-permute-done.1.refs_2_) | copy-start | bytes 98308
  27.9 0.6 copy-start.21
  69.2 7.3 %copy-start.2 = (bf16[4,64,256]{2,1,0:T(8,128)(2,1)S(1)}, bf16[4,64,256]{2,1,0:T(8,128)(2,1)}, u32[]{:S(2)}) copy-start(bf16[4,64,256]{2,1,0:T(8,128)(2,1)} %shard_map.111.refs_0_) | copy-start | bytes 393220
  69.2 60.2 %all-to-all-start.1 = ((bf16[32,2,2,16,1024]{4,3,2,1,0:T(8,128)(2,1)}), bf16[32,2,2,16,1024]{4,3,2,1,0:T(8,128)(2,1)}, u32[]{:S(2)}, u32[]{:S(2)}) async-start(bf16[32,2,2,16,1024]{4,3,2,1,0:T(8,128)(2,1)} %bitcast.34), calls=%async_computation.1 | async-start | bytes 8388608 | tf_op jit(solution)/shard_map/all_to_all | solution.py:248
  76.5 10.2 %collective-permute-start.3 = (bf16[4,64,256]{2,1,0:T(8,128)(2,1)S(1)}, bf16[4,64,256]{2,1,0:T(8,128)(2,1)S(1)}, u32[]{:S(2)}, u32[]{:S(2)}) collective-permute-start(bf16[4,64,256]{2,1,0:T(8,128)(2,1)S(1)} %copy-done.2), channel_id=1, source_target_pairs={{0,64},{64,128},{128,192},{192,8},{8,72},{72,136},{136,200},{200,0... | collective-permute-start | bytes 393224 | tf_op jit(solution)/shard_map/ppermute | solution.py:216
  79.8 11.9 %collective-permute-start.4 = (bf16[4,64,256]{2,1,0:T(8,128)(2,1)S(1)}, bf16[4,64,256]{2,1,0:T(8,128)(2,1)S(1)}, u32[]{:S(2)}, u32[]{:S(2)}) collective-permute-start(bf16[4,64,256]{2,1,0:T(8,128)(2,1)S(1)} %copy-done.2), channel_id=1, source_target_pairs={{0,128},{64,192},{128,8},{192,72},{8,136},{72,200},{136,0},{200,64... | collective-permute-start | bytes 393224 | tf_op jit(solution)/shard_map/ppermute | solution.py:216
  79.9 18.4 %collective-permute-start.5 = (bf16[4,64,256]{2,1,0:T(8,128)(2,1)S(1)}, bf16[4,64,256]{2,1,0:T(8,128)(2,1)S(1)}, u32[]{:S(2)}, u32[]{:S(2)}) collective-permute-start(bf16[4,64,256]{2,1,0:T(8,128)(2,1)S(1)} %copy-done.2), channel_id=1, source_target_pairs={{0,192},{64,8},{128,72},{192,136},{8,200},{72,0},{136,64},{200,128... | collective-permute-start | bytes 393224 | tf_op jit(solution)/shard_map/ppermute | solution.py:216
  82.1 22.4 %collective-permute-start.6 = (bf16[4,64,256]{2,1,0:T(8,128)(2,1)S(1)}, bf16[4,64,256]{2,1,0:T(8,128)(2,1)S(1)}, u32[]{:S(2)}, u32[]{:S(2)}) collective-permute-start(bf16[4,64,256]{2,1,0:T(8,128)(2,1)S(1)} %copy-done.2), channel_id=1, source_target_pairs={{0,8},{64,72},{128,136},{192,200},{8,0},{72,64},{136,128},{200,192... | collective-permute-start | bytes 393224 | tf_op jit(solution)/shard_map/ppermute | solution.py:216
  86.3 18.2 %collective-permute-start.7 = (bf16[4,64,256]{2,1,0:T(8,128)(2,1)S(1)}, bf16[4,64,256]{2,1,0:T(8,128)(2,1)S(1)}, u32[]{:S(2)}, u32[]{:S(2)}) collective-permute-start(bf16[4,64,256]{2,1,0:T(8,128)(2,1)S(1)} %copy-done.2), channel_id=1, source_target_pairs={{0,72},{64,136},{128,200},{192,0},{8,64},{72,128},{136,192},{200,8... | collective-permute-start | bytes 393224 | tf_op jit(solution)/shard_map/ppermute | solution.py:216
  86.7 23.6 %copy-start.3 = (bf16[4,64,256]{2,1,0:T(8,128)(2,1)}, bf16[4,64,256]{2,1,0:T(8,128)(2,1)S(1)}, u32[]{:S(2)}) copy-start(bf16[4,64,256]{2,1,0:T(8,128)(2,1)S(1)} %collective-permute-done.3.refs_1_) | copy-start | bytes 393220
  86.7 22.4 %collective-permute-start.8 = (bf16[4,64,256]{2,1,0:T(8,128)(2,1)S(1)}, bf16[4,64,256]{2,1,0:T(8,128)(2,1)S(1)}, u32[]{:S(2)}, u32[]{:S(2)}) collective-permute-start(bf16[4,64,256]{2,1,0:T(8,128)(2,1)S(1)} %copy-done.2), channel_id=1, source_target_pairs={{0,136},{64,200},{128,0},{192,64},{8,128},{72,192},{136,8},{200,72... | collective-permute-start | bytes 393224 | tf_op jit(solution)/shard_map/ppermute | solution.py:216
  91.7 18.7 %copy-start.4 = (bf16[4,64,256]{2,1,0:T(8,128)(2,1)}, bf16[4,64,256]{2,1,0:T(8,128)(2,1)S(1)}, u32[]{:S(2)}) copy-start(bf16[4,64,256]{2,1,0:T(8,128)(2,1)S(1)} %collective-permute-done.4.refs_2_) | copy-start | bytes 393220
  91.7 17.4 %collective-permute-start.9 = (bf16[4,64,256]{2,1,0:T(8,128)(2,1)S(1)}, bf16[4,64,256]{2,1,0:T(8,128)(2,1)S(1)}, u32[]{:S(2)}, u32[]{:S(2)}) collective-permute-start(bf16[4,64,256]{2,1,0:T(8,128)(2,1)S(1)} %copy-done.2), channel_id=1, source_target_pairs={{0,200},{64,0},{128,64},{192,128},{8,192},{72,8},{136,72},{200,136... | collective-permute-start | bytes 393224 | tf_op jit(solution)/shard_map/ppermute | solution.py:216
  98.3 10.7 %copy-start.6 = (bf16[4,64,256]{2,1,0:T(8,128)(2,1)}, bf16[4,64,256]{2,1,0:T(8,128)(2,1)S(1)}, u32[]{:S(2)}) copy-start(bf16[4,64,256]{2,1,0:T(8,128)(2,1)S(1)} %collective-permute-done.5.refs_3_) | copy-start | bytes 393220
  104.5 4.6 %copy-start.8 = (bf16[4,64,256]{2,1,0:T(8,128)(2,1)}, bf16[4,64,256]{2,1,0:T(8,128)(2,1)S(1)}, u32[]{:S(2)}) copy-start(bf16[4,64,256]{2,1,0:T(8,128)(2,1)S(1)} %collective-permute-done.6.refs_4_) | copy-start | bytes 393220
  104.5 4.6 %copy-start.10 = (bf16[4,64,256]{2,1,0:T(8,128)(2,1)}, bf16[4,64,256]{2,1,0:T(8,128)(2,1)S(1)}, u32[]{:S(2)}) copy-start(bf16[4,64,256]{2,1,0:T(8,128)(2,1)S(1)} %collective-permute-done.7.refs_5_) | copy-start | bytes 393220
  109.1 0.6 copy-start.13
  109.7 0.6 copy-start.15
  138.4 10.1 %copy-start = (bf16[2,4,4,64,256]{4,3,2,1,0:T(8,128)(2,1)S(1)}, bf16[2,4,4,64,256]{4,3,2,1,0:T(8,128)(2,1)}, u32[]{:S(2)}) copy-start(bf16[2,4,4,64,256]{4,3,2,1,0:T(8,128)(2,1)} %get-tuple-element.38) | copy-start | bytes 3145732
  138.4 63.0 %all-to-all-start.2 = ((bf16[32,2,2,16,1024]{4,3,2,1,0:T(8,128)(2,1)}), bf16[32,2,2,16,1024]{4,3,2,1,0:T(8,128)(2,1)}, u32[]{:S(2)}, u32[]{:S(2)}) async-start(bf16[32,2,2,16,1024]{4,3,2,1,0:T(8,128)(2,1)} %get-tuple-element.37), calls=%async_computation.2 | async-start | bytes 8388608 | tf_op jit(solution)/shard_map/all_to_all | solution.py:258
  148.6 10.2 %collective-permute-start.10 = (bf16[4,64,256]{2,1,0:T(8,128)(2,1)S(1)}, bf16[4,64,256]{2,1,0:T(8,128)(2,1)S(1)}, u32[]{:S(2)}, u32[]{:S(2)}) collective-permute-start(bf16[4,64,256]{2,1,0:T(8,128)(2,1)S(1)} %get-tuple-element.58), channel_id=1, source_target_pairs={{0,64},{64,128},{128,192},{192,8},{8,72},{72,136},{136,200},{200,0... | collective-permute-start | bytes 393224 | tf_op jit(solution)/shard_map/ppermute | solution.py:216
  152.0 11.9 %collective-permute-start.11 = (bf16[4,64,256]{2,1,0:T(8,128)(2,1)S(1)}, bf16[4,64,256]{2,1,0:T(8,128)(2,1)S(1)}, u32[]{:S(2)}, u32[]{:S(2)}) collective-permute-start(bf16[4,64,256]{2,1,0:T(8,128)(2,1)S(1)} %get-tuple-element.57), channel_id=1, source_target_pairs={{0,128},{64,192},{128,8},{192,72},{8,136},{72,200},{136,0},{200,64... | collective-permute-start | bytes 393224 | tf_op jit(solution)/shard_map/ppermute | solution.py:216
  152.1 18.4 %collective-permute-start.12 = (bf16[4,64,256]{2,1,0:T(8,128)(2,1)S(1)}, bf16[4,64,256]{2,1,0:T(8,128)(2,1)S(1)}, u32[]{:S(2)}, u32[]{:S(2)}) collective-permute-start(bf16[4,64,256]{2,1,0:T(8,128)(2,1)S(1)} %get-tuple-element.56), channel_id=1, source_target_pairs={{0,192},{64,8},{128,72},{192,136},{8,200},{72,0},{136,64},{200,128... | collective-permute-start | bytes 393224 | tf_op jit(solution)/shard_map/ppermute | solution.py:216
  154.3 22.4 %collective-permute-start.13 = (bf16[4,64,256]{2,1,0:T(8,128)(2,1)S(1)}, bf16[4,64,256]{2,1,0:T(8,128)(2,1)S(1)}, u32[]{:S(2)}, u32[]{:S(2)}) collective-permute-start(bf16[4,64,256]{2,1,0:T(8,128)(2,1)S(1)} %get-tuple-element.55), channel_id=1, source_target_pairs={{0,8},{64,72},{128,136},{192,200},{8,0},{72,64},{136,128},{200,192... | collective-permute-start | bytes 393224 | tf_op jit(solution)/shard_map/ppermute | solution.py:216
  158.5 18.2 %collective-permute-start.14 = (bf16[4,64,256]{2,1,0:T(8,128)(2,1)S(1)}, bf16[4,64,256]{2,1,0:T(8,128)(2,1)S(1)}, u32[]{:S(2)}, u32[]{:S(2)}) collective-permute-start(bf16[4,64,256]{2,1,0:T(8,128)(2,1)S(1)} %get-tuple-element.54), channel_id=1, source_target_pairs={{0,72},{64,136},{128,200},{192,0},{8,64},{72,128},{136,192},{200,8... | collective-permute-start | bytes 393224 | tf_op jit(solution)/shard_map/ppermute | solution.py:216
  158.8 23.0 %copy-start.5 = (bf16[4,64,256]{2,1,0:T(8,128)(2,1)}, bf16[4,64,256]{2,1,0:T(8,128)(2,1)S(1)}, u32[]{:S(2)}) copy-start(bf16[4,64,256]{2,1,0:T(8,128)(2,1)S(1)} %collective-permute-done.10.refs_1_) | copy-start | bytes 393220
  158.8 22.4 %collective-permute-start.15 = (bf16[4,64,256]{2,1,0:T(8,128)(2,1)S(1)}, bf16[4,64,256]{2,1,0:T(8,128)(2,1)S(1)}, u32[]{:S(2)}, u32[]{:S(2)}) collective-permute-start(bf16[4,64,256]{2,1,0:T(8,128)(2,1)S(1)} %get-tuple-element.53), channel_id=1, source_target_pairs={{0,136},{64,200},{128,0},{192,64},{8,128},{72,192},{136,8},{200,72... | collective-permute-start | bytes 393224 | tf_op jit(solution)/shard_map/ppermute | solution.py:216
  163.8 18.0 %copy-start.7 = (bf16[4,64,256]{2,1,0:T(8,128)(2,1)}, bf16[4,64,256]{2,1,0:T(8,128)(2,1)S(1)}, u32[]{:S(2)}) copy-start(bf16[4,64,256]{2,1,0:T(8,128)(2,1)S(1)} %collective-permute-done.11.refs_2_) | copy-start | bytes 393220
  163.8 18.0 %collective-permute-start.16 = (bf16[4,64,256]{2,1,0:T(8,128)(2,1)S(1)}, bf16[4,64,256]{2,1,0:T(8,128)(2,1)}, u32[]{:S(2)}, u32[]{:S(2)}) collective-permute-start(bf16[4,64,256]{2,1,0:T(8,128)(2,1)S(1)} %get-tuple-element.52), channel_id=1, source_target_pairs={{0,200},{64,0},{128,64},{192,128},{8,192},{72,8},{136,72},{200,136... | collective-permute-start | bytes 393224 | tf_op jit(solution)/shard_map/ppermute | solution.py:216
  170.5 11.4 %copy-start.9 = (bf16[4,64,256]{2,1,0:T(8,128)(2,1)}, bf16[4,64,256]{2,1,0:T(8,128)(2,1)S(1)}, u32[]{:S(2)}) copy-start(bf16[4,64,256]{2,1,0:T(8,128)(2,1)S(1)} %collective-permute-done.12.refs_3_) | copy-start | bytes 393220
  176.7 4.5 %copy-start.11 = (bf16[4,64,256]{2,1,0:T(8,128)(2,1)}, bf16[4,64,256]{2,1,0:T(8,128)(2,1)S(1)}, u32[]{:S(2)}) copy-start(bf16[4,64,256]{2,1,0:T(8,128)(2,1)S(1)} %collective-permute-done.13.refs_4_) | copy-start | bytes 393220
  176.7 4.5 %copy-start.12 = (bf16[4,64,256]{2,1,0:T(8,128)(2,1)}, bf16[4,64,256]{2,1,0:T(8,128)(2,1)S(1)}, u32[]{:S(2)}) copy-start(bf16[4,64,256]{2,1,0:T(8,128)(2,1)S(1)} %collective-permute-done.14.refs_5_) | copy-start | bytes 393220
  181.2 0.7 copy-start.14
  207.7 10.0 %copy-start.1 = (bf16[4,64,256]{2,1,0:T(8,128)(2,1)S(1)}, bf16[4,64,256]{2,1,0:T(8,128)(2,1)}, u32[]{:S(2)}) copy-start(bf16[4,64,256]{2,1,0:T(8,128)(2,1)} %shard_map.115) | copy-start | bytes 393220
  207.7 58.8 %all-to-all-start.3 = ((bf16[32,128,256]{2,1,0:T(8,128)(2,1)}), bf16[32,128,256]{2,1,0:T(8,128)(2,1)}, u32[]{:S(2)}, u32[]{:S(2)}) async-start(bf16[32,128,256]{2,1,0:T(8,128)(2,1)} %bitcast.36), calls=%async_computation.3 | async-start | bytes 4194304 | tf_op jit(solution)/shard_map/all_to_all | solution.py:292
  218.4 6.3 %collective-permute-start.17 = (bf16[64,256]{1,0:T(8,128)(2,1)S(1)}, bf16[64,256]{1,0:T(8,128)(2,1)S(1)}, u32[]{:S(2)}, u32[]{:S(2)}) collective-permute-start(bf16[64,256]{1,0:T(8,128)(2,1)S(1)} %get-tuple-element.61), channel_id=1, source_target_pairs={{0,16},{16,32},{32,48},{48,0},{1,17},{17,33},{33,49},{49,1},{2,18}... | collective-permute-start | bytes 98312 | tf_op jit(solution)/shard_map/ppermute | solution.py:211
  220.1 6.1 %collective-permute-start.18 = (bf16[64,256]{1,0:T(8,128)(2,1)S(1)}, bf16[64,256]{1,0:T(8,128)(2,1)S(1)}, u32[]{:S(2)}, u32[]{:S(2)}) collective-permute-start(bf16[64,256]{1,0:T(8,128)(2,1)S(1)} %get-tuple-element.60), channel_id=1, source_target_pairs={{0,32},{16,48},{32,0},{48,16},{1,33},{17,49},{33,1},{49,17},{2,34}... | collective-permute-start | bytes 98312 | tf_op jit(solution)/shard_map/ppermute | solution.py:211
  222.8 7.3 %collective-permute-start.19 = (bf16[64,256]{1,0:T(8,128)(2,1)S(1)}, bf16[64,256]{1,0:T(8,128)(2,1)S(1)}, u32[]{:S(2)}, u32[]{:S(2)}) collective-permute-start(bf16[64,256]{1,0:T(8,128)(2,1)S(1)} %get-tuple-element.59), channel_id=1, source_target_pairs={{0,48},{16,0},{32,16},{48,32},{1,49},{17,1},{33,17},{49,33},{2,50}... | collective-permute-start | bytes 98312 | tf_op jit(solution)/shard_map/ppermute | solution.py:211
  224.7 5.3 %copy-start.16 = (bf16[64,256]{1,0:T(8,128)(2,1)}, bf16[64,256]{1,0:T(8,128)(2,1)S(1)}, u32[]{:S(2)}) copy-start(bf16[64,256]{1,0:T(8,128)(2,1)S(1)} %collective-permute-done.17.refs_1_) | copy-start | bytes 98308
  226.2 3.8 %copy-start.17 = (bf16[64,256]{1,0:T(8,128)(2,1)}, bf16[64,256]{1,0:T(8,128)(2,1)S(1)}, u32[]{:S(2)}) copy-start(bf16[64,256]{1,0:T(8,128)(2,1)S(1)} %collective-permute-done.18.refs_2_) | copy-start | bytes 98308
  230.0 0.6 copy-start.18

commit v5 on v4

--- a/solution.py
+++ b/solution.py
@@ -36,9 +36,11 @@
         for b in range(2):
             first = jnp.concatenate([first_ref[b, :, q * BS : q * BS + BS] for q in range(4)], axis=0)
             rows = jnp.where(zh == p, first, fourth_ref[b])
-            for t in range(2):
-                out_ref[0, p, b, t, :64, :] = acts[t * 64 : t * 64 + 64, b * BS : b * BS + BS]
-                out_ref[0, p, b, t, 64:, :] = rows
+            for z in range(2):
+                for t in range(2):
+                    at = z * 128 + t * 64
+                    out_ref[z, p, b, t, :64, :] = acts[at : at + 64, b * BS : b * BS + BS]
+                    out_ref[z, p, b, t, 64:, :] = rows
 
 
 def pack_inner_kernel(x_ref, second_ref, third_ref, *out_refs):
@@ -160,13 +162,17 @@
         sum4_ref[...] = jnp.zeros_like(sum4_ref)
 
     for b in range(2):
-        for t in range(2):
-            g_in_ref[t * 64 : t * 64 + 64, b * BS : b * BS + BS] = in_ref[0, 0, b, t, :64, :]
-            out_ref[t * 64 : t * 64 + 64, b * BS : b * BS + BS] = out_side_ref[0, 0, b, t, :64, :]
-        grad1 = in_ref[0, 0, b, 0, 64:, :].astype(f32) + in_ref[0, 0, b, 1, 64:, :].astype(f32)
+        grad1, grad4 = jnp.zeros((64, BS), f32), jnp.zeros((64, BS), f32)
+        for z in range(2):
+            for t in range(2):
+                at = z * 128 + t * 64
+                g_in_ref[at : at + 64, b * BS : b * BS + BS] = in_ref[z, 0, b, t, :64, :]
+                out_ref[at : at + 64, b * BS : b * BS + BS] = out_side_ref[z, 0, b, t, :64, :]
+                grad1 += in_ref[z, 0, b, t, 64:, :].astype(f32)
+                grad4 += out_side_ref[z, 0, b, t, 64:, :].astype(f32)
         for q in range(4):
             sum1_ref[b, :, q * BS : q * BS + BS] += grad1[q * 16 : q * 16 + 16]
-        sum4_ref[b] += out_side_ref[0, 0, b, 0, 64:, :].astype(f32) + out_side_ref[0, 0, b, 1, 64:, :].astype(f32)
+        sum4_ref[b] += grad4
 
 
 def call(kernel, grid, in_specs, out_specs, out_shape, flops, nbytes, trans=0, scratch=()):
@@ -192,7 +198,7 @@
 SPEC_Q = pl.BlockSpec((2, 4, 2, 2, 2, 2, 16, HALF), lambda t, x1: (0, 0, 0, 0, 0, 0, 0, t))
 SPEC_J = pl.BlockSpec((NA, 2, 1, 16, ROWS), lambda k: (0, 0, k, 0, 0))
 SPEC_W = pl.BlockSpec((1, 4, 4, 64, BS), lambda k: (k, 0, 0, 0, 0))
-SPEC_T = pl.BlockSpec((128, 512), lambda z, zh: (z, 0))
+SPEC_T = pl.BlockSpec((256, 512), lambda z, zh: (z, 0))
 WIRE = (2, 4, 2, 2, 2, 2, 16, ROWS)
 PAIRS = (NA, 2, 2, 16, ROWS)
 
@@ -227,9 +233,9 @@
 
     outer = call(
         pack_kernel,
-        (4,),
+        (2,),
         [SPEC_T, SPEC_T, whole((2, 16, 1024)), whole((2, 64, BS))],
-        pl.BlockSpec((1, 2, 2, 2, 128, BS), lambda z, zh: (z, 0, 0, 0, 0, 0)),
+        pl.BlockSpec((2, 2, 2, 2, 128, BS), lambda z, zh: (z, 0, 0, 0, 0, 0)),
         S(SLOTS, bf16),
         0,
         3 << 20,
@@ -293,10 +299,10 @@
     outer, sum2, sum3 = lax.optimization_barrier((outer, sum2, sum3))
     g_in, out, sum1, sum4 = call(
         unpack_kernel,
-        (4,),
+        (2,),
         [
-            pl.BlockSpec((1, 1, 2, 2, 128, BS), lambda z, zh: (z, zh[0], 0, 0, 0, 0)),
-            pl.BlockSpec((1, 1, 2, 2, 128, BS), lambda z, zh: (z, 1 - zh[0], 0, 0, 0, 0)),
+            pl.BlockSpec((2, 1, 2, 2, 128, BS), lambda z, zh: (z, zh[0], 0, 0, 0, 0)),
+            pl.BlockSpec((2, 1, 2, 2, 128, BS), lambda z, zh: (z, 1 - zh[0], 0, 0, 0, 0)),
         ],
         [SPEC_T, SPEC_T, whole((2, 16, 1024)), whole((2, 64, BS))],
         [S((512, 512), bf16), S((512, 512), bf16), S((2, 16, 1024), f32), S((2, 64, BS), f32)],

time: 274 us -> 271 us (0.989)
  no operation moved by 1% of the time
where the time goes in v5:
time: 271 us; the launch traced here: 268 us
  waiting for transfers between devices  148 us (55%)
  starting transfers between devices  80.8 us (30%)
  Pallas kernels  33.7 us (12%)
  local copies, waits for them, and re-layouts  3.91 us (1%)
    all_to_all x2, waiting for transfers between devices, body(): lax.all_to_all(outer.reshape(32, 128, BS), FAR, 0, 0, tiled=True)  69.2 us
    ppermute x14, waiting for transfers between devices, along_z(): lax.ppermute(values, ('zl', 'zh'), [(place[z], place[(z + d) % 8]) for z...  34.6 us
    ppermute x14, starting transfers between devices, along_z(): lax.ppermute(values, ('zl', 'zh'), [(place[z], place[(z + d) % 8]) for z...  30.5 us
    all_to_all x2, starting transfers between devices, body(): lax.all_to_all(outer.reshape(32, 128, BS), FAR, 0, 0, tiled=True)  21.4 us
    all_to_all x1, waiting for transfers between devices, body(): wire = lax.all_to_all(wire, WAYS, 0, 0, tiled=True)  17.4 us
    all_to_all x1, waiting for transfers between devices, body(): wire = lax.all_to_all(wire.reshape(PAIRS), WAYS, 0, 0, tiled=True)  16.6 us
    ppermute x6, starting transfers between devices, along_x(): return lax.ppermute(values, SIDE, [(i, (i + d) % 4) for i in range(4)])  11.7 us
    ppermute x6, waiting for transfers between devices, along_x(): return lax.ppermute(values, SIDE, [(i, (i + d) % 4) for i in range(4)])  10.5 us
  transfers between devices with their start and end apart: 24, of which 18 were waited for; matrix products, arithmetic and copies ran while one was open for 0% of the time, Pallas kernels for 3%

profile of v5, /device:TPU:16, one launch (start us, length us, event | category | flops | bytes accessed | tf_op | source)
XLA Modules:
  0.0 267.8 jit_solution(17139127753307613985)
XLA Ops:
  0.6 2.5 shard_map.109
  3.1 11.4 %all-to-all-start = ((bf16[32,128,256]{2,1,0:T(8,128)(2,1)}), bf16[32,128,256]{2,1,0:T(8,128)(2,1)}, u32[]{:S(2)}, u32[]{:S(2)}) async-start(bf16[32,128,256]{2,1,0:T(8,128)(2,1)} %bitcast.35), calls=%async_computation | async-start | bytes 4194304 | tf_op jit(solution)/shard_map/all_to_all | solution.py:243
  14.6 1.5 shard_map.110
  16.1 1.7 collective-permute-start
  17.8 2.7 collective-permute-start.1
  20.5 1.5 collective-permute-start.2
  22.0 0.2 collective-permute-done.refs_1_
  22.1 1.4 collective-permute-done.1.refs_2_
  23.5 3.2 %collective-permute-done.2.refs_3_ = bf16[64,256]{1,0:T(8,128)(2,1)S(1)} collective-permute-done((bf16[64,256]{1,0:T(8,128)(2,1)}, bf16[64,256]{1,0:T(8,128)(2,1)S(1)}, u32[]{:S(2)}, u32[]{:S(2)}) %collective-permute-start.2) | collective-permute-done | bytes 32800 | tf_op jit(solution)/shard_map/ppermute | solution.py:217
  26.7 0.6 copy-done.21
  27.3 1.5 shard_map.111.refs_0_
  28.8 34.8 %all-to-all-done = bf16[32,128,256]{2,1,0:T(8,128)(2,1)} async-done(((bf16[32,128,256]{2,1,0:T(8,128)(2,1)}), bf16[32,128,256]{2,1,0:T(8,128)(2,1)}, u32[]{:S(2)}, u32[]{:S(2)}) %all-to-all-start) | async-done | bytes 2097184 | tf_op jit(solution)/shard_map/all_to_all | solution.py:243
  63.6 4.4 %shard_map.112 = bf16[2,4,2,2,2,2,16,1024]{7,6,5,4,3,2,1,0:T(8,128)(2,1)} custom-call(s32[1]{0:T(128)} %bitcast.1.x1_ref, bf16[16,2,128,256]{3,2,1,0:T(8,128)(2,1)} %bitcast.3.x_ref.g_ref.first_ref.fourth_ref, bf16[16,2,128,256]{3,2,1,0:T(8,128)(2,1)} %bitcast.3.x_ref.g_ref.first_ref.fourth_ref, ...), custom_call_target="tpu_custom_call" | custom-call | flops 1073741824 | bytes 6291456 | tf_op jit(solution)/shard_map/pallas_call | solution.py:246
  68.0 7.3 %all-to-all-start.1 = ((bf16[32,2,2,16,1024]{4,3,2,1,0:T(8,128)(2,1)}), bf16[32,2,2,16,1024]{4,3,2,1,0:T(8,128)(2,1)}, u32[]{:S(2)}, u32[]{:S(2)}) async-start(bf16[32,2,2,16,1024]{4,3,2,1,0:T(8,128)(2,1)} %bitcast.34), calls=%async_computation.1 | async-start | bytes 8388608 | tf_op jit(solution)/shard_map/all_to_all | solution.py:254
  75.3 3.3 %collective-permute-start.3 = (bf16[4,64,256]{2,1,0:T(8,128)(2,1)S(1)}, bf16[4,64,256]{2,1,0:T(8,128)(2,1)S(1)}, u32[]{:S(2)}, u32[]{:S(2)}) collective-permute-start(bf16[4,64,256]{2,1,0:T(8,128)(2,1)S(1)} %copy-done.2), channel_id=1, source_target_pairs={{0,64},{64,128},{128,192},{192,8},{8,72},{72,136},{136,200},{200,0... | collective-permute-start | bytes 393224 | tf_op jit(solution)/shard_map/ppermute | solution.py:222
  78.6 0.1 collective-permute-start.4
  78.7 2.2 collective-permute-start.5
  80.9 4.2 %collective-permute-start.6 = (bf16[4,64,256]{2,1,0:T(8,128)(2,1)S(1)}, bf16[4,64,256]{2,1,0:T(8,128)(2,1)S(1)}, u32[]{:S(2)}, u32[]{:S(2)}) collective-permute-start(bf16[4,64,256]{2,1,0:T(8,128)(2,1)S(1)} %copy-done.2), channel_id=1, source_target_pairs={{0,8},{64,72},{128,136},{192,200},{8,0},{72,64},{136,128},{200,192... | collective-permute-start | bytes 393224 | tf_op jit(solution)/shard_map/ppermute | solution.py:222
  85.1 0.4 collective-permute-start.7
  85.5 3.8 %collective-permute-start.8 = (bf16[4,64,256]{2,1,0:T(8,128)(2,1)S(1)}, bf16[4,64,256]{2,1,0:T(8,128)(2,1)S(1)}, u32[]{:S(2)}, u32[]{:S(2)}) collective-permute-start(bf16[4,64,256]{2,1,0:T(8,128)(2,1)S(1)} %copy-done.2), channel_id=1, source_target_pairs={{0,136},{64,200},{128,0},{192,64},{8,128},{72,192},{136,8},{200,72... | collective-permute-start | bytes 393224 | tf_op jit(solution)/shard_map/ppermute | solution.py:222
  89.3 1.2 collective-permute-done.4.refs_2_
  90.5 1.2 collective-permute-start.9
  91.7 5.4 %collective-permute-done.5.refs_3_ = bf16[4,64,256]{2,1,0:T(8,128)(2,1)S(1)} collective-permute-done((bf16[4,64,256]{2,1,0:T(8,128)(2,1)S(1)}, bf16[4,64,256]{2,1,0:T(8,128)(2,1)S(1)}, u32[]{:S(2)}, u32[]{:S(2)}) %collective-permute-start.5) | collective-permute-done | bytes 131104 | tf_op jit(solution)/shard_map/ppermute | solution.py:222
  97.1 6.2 %collective-permute-done.6.refs_4_ = bf16[4,64,256]{2,1,0:T(8,128)(2,1)S(1)} collective-permute-done((bf16[4,64,256]{2,1,0:T(8,128)(2,1)S(1)}, bf16[4,64,256]{2,1,0:T(8,128)(2,1)S(1)}, u32[]{:S(2)}, u32[]{:S(2)}) %collective-permute-start.6) | collective-permute-done | bytes 131104 | tf_op jit(solution)/shard_map/ppermute | solution.py:222
  103.3 0.0 collective-permute-done.7.refs_5_
  103.3 4.5 %collective-permute-done.8.refs_6_ = bf16[4,64,256]{2,1,0:T(8,128)(2,1)S(1)} collective-permute-done((bf16[4,64,256]{2,1,0:T(8,128)(2,1)S(1)}, bf16[4,64,256]{2,1,0:T(8,128)(2,1)S(1)}, u32[]{:S(2)}, u32[]{:S(2)}) %collective-permute-start.8) | collective-permute-done | bytes 131104 | tf_op jit(solution)/shard_map/ppermute | solution.py:222
  107.9 0.0 collective-permute-done.9.refs_7_
  107.9 0.6 copy-done.13
  108.5 0.6 copy-done.15
  109.1 2.4 shard_map.113
  111.5 16.6 %all-to-all-done.1.in_ref = bf16[32,2,2,16,1024]{4,3,2,1,0:T(8,128)(2,1)} async-done(((bf16[32,2,2,16,1024]{4,3,2,1,0:T(8,128)(2,1)}), bf16[32,2,2,16,1024]{4,3,2,1,0:T(8,128)(2,1)}, u32[]{:S(2)}, u32[]{:S(2)}) %all-to-all-start.1) | async-done | bytes 4194336 | tf_op jit(solution)/shard_map/all_to_all | solution.py:254
  128.2 9.0 %shard_map.114 = (bf16[32,2,2,16,1024]{4,3,2,1,0:T(8,128)(2,1)}, bf16[2,4,4,64,256]{4,3,2,1,0:T(8,128)(2,1)}) custom-call(bf16[32,2,2,16,1024]{4,3,2,1,0:T(8,128)(2,1)} %all-to-all-done.1.in_ref, bf16[2,4,4,64,256]{4,3,2,1,0:T(8,128)(2,1)} %bitcast.39), custom_call_target="tpu_custom_call" | custom-call | flops 3221225472 | bytes 10485760 | tf_op jit(solution)/shard_map/pallas_call | solution.py:255
  137.2 9.9 %all-to-all-start.2 = ((bf16[32,2,2,16,1024]{4,3,2,1,0:T(8,128)(2,1)}), bf16[32,2,2,16,1024]{4,3,2,1,0:T(8,128)(2,1)}, u32[]{:S(2)}, u32[]{:S(2)}) async-start(bf16[32,2,2,16,1024]{4,3,2,1,0:T(8,128)(2,1)} %get-tuple-element.37), calls=%async_computation.2 | async-start | bytes 8388608 | tf_op jit(solution)/shard_map/all_to_all | solution.py:264
  147.2 0.1 dynamic-slice_bitcast_fusion
  147.3 3.3 %collective-permute-start.10 = (bf16[4,64,256]{2,1,0:T(8,128)(2,1)S(1)}, bf16[4,64,256]{2,1,0:T(8,128)(2,1)S(1)}, u32[]{:S(2)}, u32[]{:S(2)}) collective-permute-start(bf16[4,64,256]{2,1,0:T(8,128)(2,1)S(1)} %get-tuple-element.58), channel_id=1, source_target_pairs={{0,64},{64,128},{128,192},{192,8},{8,72},{72,136},{136,200},{200,0... | collective-permute-start | bytes 393224 | tf_op jit(solution)/shard_map/ppermute | solution.py:222
  150.6 0.1 collective-permute-start.11
  150.7 2.2 collective-permute-start.12
  152.9 4.2 %collective-permute-start.13 = (bf16[4,64,256]{2,1,0:T(8,128)(2,1)S(1)}, bf16[4,64,256]{2,1,0:T(8,128)(2,1)S(1)}, u32[]{:S(2)}, u32[]{:S(2)}) collective-permute-start(bf16[4,64,256]{2,1,0:T(8,128)(2,1)S(1)} %get-tuple-element.55), channel_id=1, source_target_pairs={{0,8},{64,72},{128,136},{192,200},{8,0},{72,64},{136,128},{200,192... | collective-permute-start | bytes 393224 | tf_op jit(solution)/shard_map/ppermute | solution.py:222
  157.1 0.4 collective-permute-start.14
  157.5 0.0 collective-permute-done.10.refs_1_
  157.5 3.8 %collective-permute-start.15 = (bf16[4,64,256]{2,1,0:T(8,128)(2,1)S(1)}, bf16[4,64,256]{2,1,0:T(8,128)(2,1)S(1)}, u32[]{:S(2)}, u32[]{:S(2)}) collective-permute-start(bf16[4,64,256]{2,1,0:T(8,128)(2,1)S(1)} %get-tuple-element.53), channel_id=1, source_target_pairs={{0,136},{64,200},{128,0},{192,64},{8,128},{72,192},{136,8},{200,72... | collective-permute-start | bytes 393224 | tf_op jit(solution)/shard_map/ppermute | solution.py:222
  161.3 1.2 collective-permute-done.11.refs_2_
  162.4 1.3 collective-permute-start.16
  163.7 5.4 %collective-permute-done.12.refs_3_ = bf16[4,64,256]{2,1,0:T(8,128)(2,1)S(1)} collective-permute-done((bf16[4,64,256]{2,1,0:T(8,128)(2,1)S(1)}, bf16[4,64,256]{2,1,0:T(8,128)(2,1)S(1)}, u32[]{:S(2)}, u32[]{:S(2)}) %collective-permute-start.12) | collective-permute-done | bytes 131104 | tf_op jit(solution)/shard_map/ppermute | solution.py:222
  169.1 6.2 %collective-permute-done.13.refs_4_ = bf16[4,64,256]{2,1,0:T(8,128)(2,1)S(1)} collective-permute-done((bf16[4,64,256]{2,1,0:T(8,128)(2,1)S(1)}, bf16[4,64,256]{2,1,0:T(8,128)(2,1)S(1)}, u32[]{:S(2)}, u32[]{:S(2)}) %collective-permute-start.13) | collective-permute-done | bytes 131104 | tf_op jit(solution)/shard_map/ppermute | solution.py:222
  175.3 0.0 collective-permute-done.14.refs_5_
  175.3 4.5 %collective-permute-done.15.refs_6_ = bf16[4,64,256]{2,1,0:T(8,128)(2,1)S(1)} collective-permute-done((bf16[4,64,256]{2,1,0:T(8,128)(2,1)S(1)}, bf16[4,64,256]{2,1,0:T(8,128)(2,1)S(1)}, u32[]{:S(2)}, u32[]{:S(2)}) %collective-permute-start.15) | collective-permute-done | bytes 131104 | tf_op jit(solution)/shard_map/ppermute | solution.py:222
  179.8 0.7 copy-done.14
  180.5 0.0 collective-permute-done.16.refs_7_
  180.5 2.1 shard_map.115
  182.6 17.4 %all-to-all-done.2 = bf16[32,2,2,16,1024]{4,3,2,1,0:T(8,128)(2,1)} async-done(((bf16[32,2,2,16,1024]{4,3,2,1,0:T(8,128)(2,1)}), bf16[32,2,2,16,1024]{4,3,2,1,0:T(8,128)(2,1)}, u32[]{:S(2)}, u32[]{:S(2)}) %all-to-all-start.2) | async-done | bytes 4194336 | tf_op jit(solution)/shard_map/all_to_all | solution.py:264
  200.0 6.3 %shard_map.116 = bf16[16,2,128,256]{3,2,1,0:T(8,128)(2,1)} custom-call(s32[1]{0:T(128)} %bitcast.1.x1_ref, bf16[2,4,2,2,2,2,16,1024]{7,6,5,4,3,2,1,0:T(8,128)(2,1)} %bitcast.16.in_ref, bf16[16,2,128,256]{3,2,1,0:T(8,128)(2,1)} %bitcast.3.x_ref.g_ref.first_ref.fourth_ref, bf16[16,2,128,256]{3,2,1,0:T(8,128)(2,1)} %bitcast.3.x_ref.g_ref.first_ref.fourth_ref, ...), custom_call_target="tpu_custom_call" | custom-call | flops 2147483648 | bytes 8388608 | tf_op jit(solution)/shard_map/pallas_call | solution.py:281
  206.4 10.0 %all-to-all-start.3 = ((bf16[32,128,256]{2,1,0:T(8,128)(2,1)}), bf16[32,128,256]{2,1,0:T(8,128)(2,1)}, u32[]{:S(2)}, u32[]{:S(2)}) async-start(bf16[32,128,256]{2,1,0:T(8,128)(2,1)} %bitcast.36), calls=%async_computation.3 | async-start | bytes 4194304 | tf_op jit(solution)/shard_map/all_to_all | solution.py:298
  216.4 0.6 dynamic-slice_bitcast_fusion.7
  217.0 1.7 collective-permute-start.17
  218.7 2.7 collective-permute-start.18
  221.4 1.5 collective-permute-start.19
  222.9 0.5 collective-permute-done.17.refs_1_
  223.3 1.5 collective-permute-done.18.refs_2_
  224.8 3.8 %collective-permute-done.19.refs_3_ = bf16[64,256]{1,0:T(8,128)(2,1)S(1)} collective-permute-done((bf16[64,256]{1,0:T(8,128)(2,1)S(1)}, bf16[64,256]{1,0:T(8,128)(2,1)S(1)}, u32[]{:S(2)}, u32[]{:S(2)}) %collective-permute-start.19) | collective-permute-done | bytes 32800 | tf_op jit(solution)/shard_map/ppermute | solution.py:217
  228.7 0.6 copy-done.18
  229.3 1.5 shard_map.117
  230.8 34.4 %all-to-all-done.3 = bf16[32,128,256]{2,1,0:T(8,128)(2,1)} async-done(((bf16[32,128,256]{2,1,0:T(8,128)(2,1)}), bf16[32,128,256]{2,1,0:T(8,128)(2,1)}, u32[]{:S(2)}, u32[]{:S(2)}) %all-to-all-start.3) | async-done | bytes 2097184 | tf_op jit(solution)/shard_map/all_to_all | solution.py:298
  265.2 2.5 shard_map.118
  (40 shorter events, 0.1 us)
Async XLA Ops:
  3.1 60.5 %all-to-all-start = ((bf16[32,128,256]{2,1,0:T(8,128)(2,1)}), bf16[32,128,256]{2,1,0:T(8,128)(2,1)}, u32[]{:S(2)}, u32[]{:S(2)}) async-start(bf16[32,128,256]{2,1,0:T(8,128)(2,1)} %bitcast.35), calls=%async_computation | async-start | bytes 4194304 | tf_op jit(solution)/shard_map/all_to_all | solution.py:243
  16.1 6.0 %collective-permute-start = (bf16[64,256]{1,0:T(8,128)(2,1)}, bf16[64,256]{1,0:T(8,128)(2,1)S(1)}, u32[]{:S(2)}, u32[]{:S(2)}) collective-permute-start(bf16[64,256]{1,0:T(8,128)(2,1)} %get-tuple-element.30), channel_id=1, source_target_pairs={{0,16},{16,32},{32,48},{48,0},{1,17},{17,33},{33,49},{49,1},{2,18}... | collective-permute-start | bytes 98312 | tf_op jit(solution)/shard_map/ppermute | solution.py:217
  17.8 5.7 %collective-permute-start.1 = (bf16[64,256]{1,0:T(8,128)(2,1)}, bf16[64,256]{1,0:T(8,128)(2,1)S(1)}, u32[]{:S(2)}, u32[]{:S(2)}) collective-permute-start(bf16[64,256]{1,0:T(8,128)(2,1)} %get-tuple-element.31), channel_id=1, source_target_pairs={{0,32},{16,48},{32,0},{48,16},{1,33},{17,49},{33,1},{49,17},{2,34}... | collective-permute-start | bytes 98312 | tf_op jit(solution)/shard_map/ppermute | solution.py:217
  20.5 6.2 %collective-permute-start.2 = (bf16[64,256]{1,0:T(8,128)(2,1)}, bf16[64,256]{1,0:T(8,128)(2,1)S(1)}, u32[]{:S(2)}, u32[]{:S(2)}) collective-permute-start(bf16[64,256]{1,0:T(8,128)(2,1)} %get-tuple-element.32), channel_id=1, source_target_pairs={{0,48},{16,0},{32,16},{48,32},{1,49},{17,1},{33,17},{49,33},{2,50}... | collective-permute-start | bytes 98312 | tf_op jit(solution)/shard_map/ppermute | solution.py:217
  22.1 4.6 %copy-start.19 = (bf16[64,256]{1,0:T(8,128)(2,1)}, bf16[64,256]{1,0:T(8,128)(2,1)S(1)}, u32[]{:S(2)}) copy-start(bf16[64,256]{1,0:T(8,128)(2,1)S(1)} %collective-permute-done.refs_1_) | copy-start | bytes 98308
  23.5 3.2 %copy-start.20 = (bf16[64,256]{1,0:T(8,128)(2,1)}, bf16[64,256]{1,0:T(8,128)(2,1)S(1)}, u32[]{:S(2)}) copy-start(bf16[64,256]{1,0:T(8,128)(2,1)S(1)} %collective-permute-done.1.refs_2_) | copy-start | bytes 98308
  26.7 0.6 copy-start.21
  68.0 7.3 %copy-start.2 = (bf16[4,64,256]{2,1,0:T(8,128)(2,1)S(1)}, bf16[4,64,256]{2,1,0:T(8,128)(2,1)}, u32[]{:S(2)}) copy-start(bf16[4,64,256]{2,1,0:T(8,128)(2,1)} %shard_map.111.refs_0_) | copy-start | bytes 393220
  68.0 60.2 %all-to-all-start.1 = ((bf16[32,2,2,16,1024]{4,3,2,1,0:T(8,128)(2,1)}), bf16[32,2,2,16,1024]{4,3,2,1,0:T(8,128)(2,1)}, u32[]{:S(2)}, u32[]{:S(2)}) async-start(bf16[32,2,2,16,1024]{4,3,2,1,0:T(8,128)(2,1)} %bitcast.34), calls=%async_computation.1 | async-start | bytes 8388608 | tf_op jit(solution)/shard_map/all_to_all | solution.py:254
  75.3 10.2 %collective-permute-start.3 = (bf16[4,64,256]{2,1,0:T(8,128)(2,1)S(1)}, bf16[4,64,256]{2,1,0:T(8,128)(2,1)S(1)}, u32[]{:S(2)}, u32[]{:S(2)}) collective-permute-start(bf16[4,64,256]{2,1,0:T(8,128)(2,1)S(1)} %copy-done.2), channel_id=1, source_target_pairs={{0,64},{64,128},{128,192},{192,8},{8,72},{72,136},{136,200},{200,0... | collective-permute-start | bytes 393224 | tf_op jit(solution)/shard_map/ppermute | solution.py:222
  78.6 11.9 %collective-permute-start.4 = (bf16[4,64,256]{2,1,0:T(8,128)(2,1)S(1)}, bf16[4,64,256]{2,1,0:T(8,128)(2,1)S(1)}, u32[]{:S(2)}, u32[]{:S(2)}) collective-permute-start(bf16[4,64,256]{2,1,0:T(8,128)(2,1)S(1)} %copy-done.2), channel_id=1, source_target_pairs={{0,128},{64,192},{128,8},{192,72},{8,136},{72,200},{136,0},{200,64... | collective-permute-start | bytes 393224 | tf_op jit(solution)/shard_map/ppermute | solution.py:222
  78.7 18.4 %collective-permute-start.5 = (bf16[4,64,256]{2,1,0:T(8,128)(2,1)S(1)}, bf16[4,64,256]{2,1,0:T(8,128)(2,1)S(1)}, u32[]{:S(2)}, u32[]{:S(2)}) collective-permute-start(bf16[4,64,256]{2,1,0:T(8,128)(2,1)S(1)} %copy-done.2), channel_id=1, source_target_pairs={{0,192},{64,8},{128,72},{192,136},{8,200},{72,0},{136,64},{200,128... | collective-permute-start | bytes 393224 | tf_op jit(solution)/shard_map/ppermute | solution.py:222
  80.9 22.4 %collective-permute-start.6 = (bf16[4,64,256]{2,1,0:T(8,128)(2,1)S(1)}, bf16[4,64,256]{2,1,0:T(8,128)(2,1)S(1)}, u32[]{:S(2)}, u32[]{:S(2)}) collective-permute-start(bf16[4,64,256]{2,1,0:T(8,128)(2,1)S(1)} %copy-done.2), channel_id=1, source_target_pairs={{0,8},{64,72},{128,136},{192,200},{8,0},{72,64},{136,128},{200,192... | collective-permute-start | bytes 393224 | tf_op jit(solution)/shard_map/ppermute | solution.py:222
  85.1 18.2 %collective-permute-start.7 = (bf16[4,64,256]{2,1,0:T(8,128)(2,1)S(1)}, bf16[4,64,256]{2,1,0:T(8,128)(2,1)S(1)}, u32[]{:S(2)}, u32[]{:S(2)}) collective-permute-start(bf16[4,64,256]{2,1,0:T(8,128)(2,1)S(1)} %copy-done.2), channel_id=1, source_target_pairs={{0,72},{64,136},{128,200},{192,0},{8,64},{72,128},{136,192},{200,8... | collective-permute-start | bytes 393224 | tf_op jit(solution)/shard_map/ppermute | solution.py:222
  85.5 23.6 %copy-start.3 = (bf16[4,64,256]{2,1,0:T(8,128)(2,1)}, bf16[4,64,256]{2,1,0:T(8,128)(2,1)S(1)}, u32[]{:S(2)}) copy-start(bf16[4,64,256]{2,1,0:T(8,128)(2,1)S(1)} %collective-permute-done.3.refs_1_) | copy-start | bytes 393220
  85.5 22.4 %collective-permute-start.8 = (bf16[4,64,256]{2,1,0:T(8,128)(2,1)S(1)}, bf16[4,64,256]{2,1,0:T(8,128)(2,1)S(1)}, u32[]{:S(2)}, u32[]{:S(2)}) collective-permute-start(bf16[4,64,256]{2,1,0:T(8,128)(2,1)S(1)} %copy-done.2), channel_id=1, source_target_pairs={{0,136},{64,200},{128,0},{192,64},{8,128},{72,192},{136,8},{200,72... | collective-permute-start | bytes 393224 | tf_op jit(solution)/shard_map/ppermute | solution.py:222
  90.5 18.6 %copy-start.4 = (bf16[4,64,256]{2,1,0:T(8,128)(2,1)}, bf16[4,64,256]{2,1,0:T(8,128)(2,1)S(1)}, u32[]{:S(2)}) copy-start(bf16[4,64,256]{2,1,0:T(8,128)(2,1)S(1)} %collective-permute-done.4.refs_2_) | copy-start | bytes 393220
  90.5 17.4 %collective-permute-start.9 = (bf16[4,64,256]{2,1,0:T(8,128)(2,1)S(1)}, bf16[4,64,256]{2,1,0:T(8,128)(2,1)S(1)}, u32[]{:S(2)}, u32[]{:S(2)}) collective-permute-start(bf16[4,64,256]{2,1,0:T(8,128)(2,1)S(1)} %copy-done.2), channel_id=1, source_target_pairs={{0,200},{64,0},{128,64},{192,128},{8,192},{72,8},{136,72},{200,136... | collective-permute-start | bytes 393224 | tf_op jit(solution)/shard_map/ppermute | solution.py:222
  97.1 10.7 %copy-start.6 = (bf16[4,64,256]{2,1,0:T(8,128)(2,1)}, bf16[4,64,256]{2,1,0:T(8,128)(2,1)S(1)}, u32[]{:S(2)}) copy-start(bf16[4,64,256]{2,1,0:T(8,128)(2,1)S(1)} %collective-permute-done.5.refs_3_) | copy-start | bytes 393220
  103.3 4.6 %copy-start.8 = (bf16[4,64,256]{2,1,0:T(8,128)(2,1)}, bf16[4,64,256]{2,1,0:T(8,128)(2,1)S(1)}, u32[]{:S(2)}) copy-start(bf16[4,64,256]{2,1,0:T(8,128)(2,1)S(1)} %collective-permute-done.6.refs_4_) | copy-start | bytes 393220
  103.3 4.6 %copy-start.10 = (bf16[4,64,256]{2,1,0:T(8,128)(2,1)}, bf16[4,64,256]{2,1,0:T(8,128)(2,1)S(1)}, u32[]{:S(2)}) copy-start(bf16[4,64,256]{2,1,0:T(8,128)(2,1)S(1)} %collective-permute-done.7.refs_5_) | copy-start | bytes 393220
  107.8 0.6 copy-start.13
  108.5 0.6 copy-start.15
  137.2 10.0 %copy-start = (bf16[2,4,4,64,256]{4,3,2,1,0:T(8,128)(2,1)S(1)}, bf16[2,4,4,64,256]{4,3,2,1,0:T(8,128)(2,1)}, u32[]{:S(2)}) copy-start(bf16[2,4,4,64,256]{4,3,2,1,0:T(8,128)(2,1)} %get-tuple-element.38) | copy-start | bytes 3145732
  137.2 62.8 %all-to-all-start.2 = ((bf16[32,2,2,16,1024]{4,3,2,1,0:T(8,128)(2,1)}), bf16[32,2,2,16,1024]{4,3,2,1,0:T(8,128)(2,1)}, u32[]{:S(2)}, u32[]{:S(2)}) async-start(bf16[32,2,2,16,1024]{4,3,2,1,0:T(8,128)(2,1)} %get-tuple-element.37), calls=%async_computation.2 | async-start | bytes 8388608 | tf_op jit(solution)/shard_map/all_to_all | solution.py:264
  147.3 10.2 %collective-permute-start.10 = (bf16[4,64,256]{2,1,0:T(8,128)(2,1)S(1)}, bf16[4,64,256]{2,1,0:T(8,128)(2,1)S(1)}, u32[]{:S(2)}, u32[]{:S(2)}) collective-permute-start(bf16[4,64,256]{2,1,0:T(8,128)(2,1)S(1)} %get-tuple-element.58), channel_id=1, source_target_pairs={{0,64},{64,128},{128,192},{192,8},{8,72},{72,136},{136,200},{200,0... | collective-permute-start | bytes 393224 | tf_op jit(solution)/shard_map/ppermute | solution.py:222
  150.6 11.9 %collective-permute-start.11 = (bf16[4,64,256]{2,1,0:T(8,128)(2,1)S(1)}, bf16[4,64,256]{2,1,0:T(8,128)(2,1)S(1)}, u32[]{:S(2)}, u32[]{:S(2)}) collective-permute-start(bf16[4,64,256]{2,1,0:T(8,128)(2,1)S(1)} %get-tuple-element.57), channel_id=1, source_target_pairs={{0,128},{64,192},{128,8},{192,72},{8,136},{72,200},{136,0},{200,64... | collective-permute-start | bytes 393224 | tf_op jit(solution)/shard_map/ppermute | solution.py:222
  150.7 18.4 %collective-permute-start.12 = (bf16[4,64,256]{2,1,0:T(8,128)(2,1)S(1)}, bf16[4,64,256]{2,1,0:T(8,128)(2,1)S(1)}, u32[]{:S(2)}, u32[]{:S(2)}) collective-permute-start(bf16[4,64,256]{2,1,0:T(8,128)(2,1)S(1)} %get-tuple-element.56), channel_id=1, source_target_pairs={{0,192},{64,8},{128,72},{192,136},{8,200},{72,0},{136,64},{200,128... | collective-permute-start | bytes 393224 | tf_op jit(solution)/shard_map/ppermute | solution.py:222
  152.9 22.4 %collective-permute-start.13 = (bf16[4,64,256]{2,1,0:T(8,128)(2,1)S(1)}, bf16[4,64,256]{2,1,0:T(8,128)(2,1)S(1)}, u32[]{:S(2)}, u32[]{:S(2)}) collective-permute-start(bf16[4,64,256]{2,1,0:T(8,128)(2,1)S(1)} %get-tuple-element.55), channel_id=1, source_target_pairs={{0,8},{64,72},{128,136},{192,200},{8,0},{72,64},{136,128},{200,192... | collective-permute-start | bytes 393224 | tf_op jit(solution)/shard_map/ppermute | solution.py:222
  157.1 18.2 %collective-permute-start.14 = (bf16[4,64,256]{2,1,0:T(8,128)(2,1)S(1)}, bf16[4,64,256]{2,1,0:T(8,128)(2,1)S(1)}, u32[]{:S(2)}, u32[]{:S(2)}) collective-permute-start(bf16[4,64,256]{2,1,0:T(8,128)(2,1)S(1)} %get-tuple-element.54), channel_id=1, source_target_pairs={{0,72},{64,136},{128,200},{192,0},{8,64},{72,128},{136,192},{200,8... | collective-permute-start | bytes 393224 | tf_op jit(solution)/shard_map/ppermute | solution.py:222
  157.5 23.0 %copy-start.5 = (bf16[4,64,256]{2,1,0:T(8,128)(2,1)}, bf16[4,64,256]{2,1,0:T(8,128)(2,1)S(1)}, u32[]{:S(2)}) copy-start(bf16[4,64,256]{2,1,0:T(8,128)(2,1)S(1)} %collective-permute-done.10.refs_1_) | copy-start | bytes 393220
  157.5 22.3 %collective-permute-start.15 = (bf16[4,64,256]{2,1,0:T(8,128)(2,1)S(1)}, bf16[4,64,256]{2,1,0:T(8,128)(2,1)S(1)}, u32[]{:S(2)}, u32[]{:S(2)}) collective-permute-start(bf16[4,64,256]{2,1,0:T(8,128)(2,1)S(1)} %get-tuple-element.53), channel_id=1, source_target_pairs={{0,136},{64,200},{128,0},{192,64},{8,128},{72,192},{136,8},{200,72... | collective-permute-start | bytes 393224 | tf_op jit(solution)/shard_map/ppermute | solution.py:222
  162.4 18.0 %copy-start.7 = (bf16[4,64,256]{2,1,0:T(8,128)(2,1)}, bf16[4,64,256]{2,1,0:T(8,128)(2,1)S(1)}, u32[]{:S(2)}) copy-start(bf16[4,64,256]{2,1,0:T(8,128)(2,1)S(1)} %collective-permute-done.11.refs_2_) | copy-start | bytes 393220
  162.4 18.0 %collective-permute-start.16 = (bf16[4,64,256]{2,1,0:T(8,128)(2,1)S(1)}, bf16[4,64,256]{2,1,0:T(8,128)(2,1)}, u32[]{:S(2)}, u32[]{:S(2)}) collective-permute-start(bf16[4,64,256]{2,1,0:T(8,128)(2,1)S(1)} %get-tuple-element.52), channel_id=1, source_target_pairs={{0,200},{64,0},{128,64},{192,128},{8,192},{72,8},{136,72},{200,136... | collective-permute-start | bytes 393224 | tf_op jit(solution)/shard_map/ppermute | solution.py:222
  169.1 11.4 %copy-start.9 = (bf16[4,64,256]{2,1,0:T(8,128)(2,1)}, bf16[4,64,256]{2,1,0:T(8,128)(2,1)S(1)}, u32[]{:S(2)}) copy-start(bf16[4,64,256]{2,1,0:T(8,128)(2,1)S(1)} %collective-permute-done.12.refs_3_) | copy-start | bytes 393220
  175.3 4.5 %copy-start.11 = (bf16[4,64,256]{2,1,0:T(8,128)(2,1)}, bf16[4,64,256]{2,1,0:T(8,128)(2,1)S(1)}, u32[]{:S(2)}) copy-start(bf16[4,64,256]{2,1,0:T(8,128)(2,1)S(1)} %collective-permute-done.13.refs_4_) | copy-start | bytes 393220
  175.3 4.5 %copy-start.12 = (bf16[4,64,256]{2,1,0:T(8,128)(2,1)}, bf16[4,64,256]{2,1,0:T(8,128)(2,1)S(1)}, u32[]{:S(2)}) copy-start(bf16[4,64,256]{2,1,0:T(8,128)(2,1)S(1)} %collective-permute-done.14.refs_5_) | copy-start | bytes 393220
  179.8 0.7 copy-start.14
  206.4 10.0 %copy-start.1 = (bf16[4,64,256]{2,1,0:T(8,128)(2,1)S(1)}, bf16[4,64,256]{2,1,0:T(8,128)(2,1)}, u32[]{:S(2)}) copy-start(bf16[4,64,256]{2,1,0:T(8,128)(2,1)} %shard_map.115) | copy-start | bytes 393220
  206.4 58.8 %all-to-all-start.3 = ((bf16[32,128,256]{2,1,0:T(8,128)(2,1)}), bf16[32,128,256]{2,1,0:T(8,128)(2,1)}, u32[]{:S(2)}, u32[]{:S(2)}) async-start(bf16[32,128,256]{2,1,0:T(8,128)(2,1)} %bitcast.36), calls=%async_computation.3 | async-start | bytes 4194304 | tf_op jit(solution)/shard_map/all_to_all | solution.py:298
  217.0 6.3 %collective-permute-start.17 = (bf16[64,256]{1,0:T(8,128)(2,1)S(1)}, bf16[64,256]{1,0:T(8,128)(2,1)S(1)}, u32[]{:S(2)}, u32[]{:S(2)}) collective-permute-start(bf16[64,256]{1,0:T(8,128)(2,1)S(1)} %get-tuple-element.61), channel_id=1, source_target_pairs={{0,16},{16,32},{32,48},{48,0},{1,17},{17,33},{33,49},{49,1},{2,18}... | collective-permute-start | bytes 98312 | tf_op jit(solution)/shard_map/ppermute | solution.py:217
  218.7 6.1 %collective-permute-start.18 = (bf16[64,256]{1,0:T(8,128)(2,1)S(1)}, bf16[64,256]{1,0:T(8,128)(2,1)S(1)}, u32[]{:S(2)}, u32[]{:S(2)}) collective-permute-start(bf16[64,256]{1,0:T(8,128)(2,1)S(1)} %get-tuple-element.60), channel_id=1, source_target_pairs={{0,32},{16,48},{32,0},{48,16},{1,33},{17,49},{33,1},{49,17},{2,34}... | collective-permute-start | bytes 98312 | tf_op jit(solution)/shard_map/ppermute | solution.py:217
  221.4 7.3 %collective-permute-start.19 = (bf16[64,256]{1,0:T(8,128)(2,1)S(1)}, bf16[64,256]{1,0:T(8,128)(2,1)S(1)}, u32[]{:S(2)}, u32[]{:S(2)}) collective-permute-start(bf16[64,256]{1,0:T(8,128)(2,1)S(1)} %get-tuple-element.59), channel_id=1, source_target_pairs={{0,48},{16,0},{32,16},{48,32},{1,49},{17,1},{33,17},{49,33},{2,50}... | collective-permute-start | bytes 98312 | tf_op jit(solution)/shard_map/ppermute | solution.py:217
  223.3 5.3 %copy-start.16 = (bf16[64,256]{1,0:T(8,128)(2,1)}, bf16[64,256]{1,0:T(8,128)(2,1)S(1)}, u32[]{:S(2)}) copy-start(bf16[64,256]{1,0:T(8,128)(2,1)S(1)} %collective-permute-done.17.refs_1_) | copy-start | bytes 98308
  224.8 3.8 %copy-start.17 = (bf16[64,256]{1,0:T(8,128)(2,1)}, bf16[64,256]{1,0:T(8,128)(2,1)S(1)}, u32[]{:S(2)}) copy-start(bf16[64,256]{1,0:T(8,128)(2,1)S(1)} %collective-permute-done.18.refs_2_) | copy-start | bytes 98308
  228.7 0.6 copy-start.18

commit v6 on v5

--- a/solution.py
+++ b/solution.py
@@ -275,6 +275,8 @@
         1 << 20,
         2 << 20,
     )(at_z, grads, *sums)
+    sums = [lax.dynamic_index_in_dim(sums, lax.rem(at_x[0] + d, 4), keepdims=False) for d in range(4)]
+    sums = [sums[0]] + [along_x(sums[d], d) for d in (1, 2, 3)]
     wire, sums = lax.optimization_barrier((wire, sums))
 
     acc = pltpu.VMEM((ROWS, BS), f32)
@@ -290,8 +292,6 @@
     )(x1, wire.reshape(WIRE), outer, outer, outer, outer)
 
     outer, sums = lax.optimization_barrier((outer, sums))
-    sums = [lax.dynamic_index_in_dim(sums, lax.rem(at_x[0] + d, 4), keepdims=False) for d in range(4)]
-    sums = [sums[0]] + [along_x(sums[d], d) for d in (1, 2, 3)]
     sum2, sum3 = call(
         unpack_inner_kernel, (1,), [whole(PIECE.shape)] * 4, [whole(INNER.shape)] * 2, [INNER] * 2, 0, 1 << 19
     )(at_x, *sums)

time: 271 us -> 272 us (level)
  waiting for transfers between devices: 148 us -> 152 us
  starting transfers between devices: 80.8 us -> 77.5 us
    all_to_all x1, waiting for transfers between devices: 17.4 us -> 0.01 us  [body(): wire = lax.all_to_all(wire, WAYS, 0, 0, tiled=True)]
    all_to_all x2, waiting for transfers between devices: 69.2 us -> 81.9 us  [body(): lax.all_to_all(outer.reshape(32, 128, BS), FAR, 0, 0, tiled=True)]
    ppermute x6, waiting for transfers between devices: 10.5 us -> 19.2 us  [along_x(): return lax.ppermute(values, SIDE, [(i, (i + d) % 4) for i in range(4)])]
    all_to_all x2, starting transfers between devices: 21.4 us -> 18.3 us  [body(): lax.all_to_all(outer.reshape(32, 128, BS), FAR, 0, 0, tiled=True)]
  transfers between devices with their start and end apart: 24 -> 24, of which waited for: 18 -> 17; matrix products, arithmetic and copies ran while one was open for 0% -> 1% of each run, Pallas kernels for 3% -> 3%
where the time goes in v6:
time: 272 us; the launch traced here: 269 us
  waiting for transfers between devices  152 us (56%)
  starting transfers between devices  77.5 us (28%)
  Pallas kernels  33.8 us (12%)
  local copies, waits for them, and re-layouts  4.12 us (2%)
    all_to_all x2, waiting for transfers between devices, body(): lax.all_to_all(outer.reshape(32, 128, BS), FAR, 0, 0, tiled=True)  81.9 us
    ppermute x14, waiting for transfers between devices, along_z(): lax.ppermute(values, ('zl', 'zh'), [(place[z], place[(z + d) % 8]) for z...  34.6 us
    ppermute x14, starting transfers between devices, along_z(): lax.ppermute(values, ('zl', 'zh'), [(place[z], place[(z + d) % 8]) for z...  30.5 us
    ppermute x6, waiting for transfers between devices, along_x(): return lax.ppermute(values, SIDE, [(i, (i + d) % 4) for i in range(4)])  19.2 us
    all_to_all x2, starting transfers between devices, body(): lax.all_to_all(outer.reshape(32, 128, BS), FAR, 0, 0, tiled=True)  18.3 us
    all_to_all x1, waiting for transfers between devices, body(): wire = lax.all_to_all(wire.reshape(PAIRS), WAYS, 0, 0, tiled=True)  16.6 us
    ppermute x6, starting transfers between devices, along_x(): return lax.ppermute(values, SIDE, [(i, (i + d) % 4) for i in range(4)])  11.5 us
    all_to_all x1, starting transfers between devices, body(): wire = lax.all_to_all(wire, WAYS, 0, 0, tiled=True)  9.89 us
  transfers between devices with their start and end apart: 24, of which 17 were waited for; matrix products, arithmetic and copies ran while one was open for 1% of the time, Pallas kernels for 3%

profile of v6, /device:TPU:16, one launch (start us, length us, event | category | flops | bytes accessed | tf_op | source)
XLA Modules:
  0.0 268.8 jit_solution(2603226106530962577)
XLA Ops:
  0.6 2.5 shard_map.109
  3.1 11.4 %all-to-all-start = ((bf16[32,128,256]{2,1,0:T(8,128)(2,1)}), bf16[32,128,256]{2,1,0:T(8,128)(2,1)}, u32[]{:S(2)}, u32[]{:S(2)}) async-start(bf16[32,128,256]{2,1,0:T(8,128)(2,1)} %bitcast.35), calls=%async_computation | async-start | bytes 4194304 | tf_op jit(solution)/shard_map/all_to_all | solution.py:243
  14.6 1.5 shard_map.110
  16.1 1.7 collective-permute-start
  17.8 2.7 collective-permute-start.1
  20.5 1.5 collective-permute-start.2
  22.0 0.2 collective-permute-done.refs_1_
  22.1 1.4 collective-permute-done.1.refs_2_
  23.5 3.2 %collective-permute-done.2.refs_3_ = bf16[64,256]{1,0:T(8,128)(2,1)S(1)} collective-permute-done((bf16[64,256]{1,0:T(8,128)(2,1)}, bf16[64,256]{1,0:T(8,128)(2,1)S(1)}, u32[]{:S(2)}, u32[]{:S(2)}) %collective-permute-start.2) | collective-permute-done | bytes 32800 | tf_op jit(solution)/shard_map/ppermute | solution.py:217
  26.7 0.6 copy-done.20
  27.3 1.5 shard_map.111.refs_0_
  28.8 34.8 %all-to-all-done = bf16[32,128,256]{2,1,0:T(8,128)(2,1)} async-done(((bf16[32,128,256]{2,1,0:T(8,128)(2,1)}), bf16[32,128,256]{2,1,0:T(8,128)(2,1)}, u32[]{:S(2)}, u32[]{:S(2)}) %all-to-all-start) | async-done | bytes 2097184 | tf_op jit(solution)/shard_map/all_to_all | solution.py:243
  63.6 4.4 %shard_map.112 = bf16[2,4,2,2,2,2,16,1024]{7,6,5,4,3,2,1,0:T(8,128)(2,1)} custom-call(s32[1]{0:T(128)} %bitcast.1.x1_ref, bf16[16,2,128,256]{3,2,1,0:T(8,128)(2,1)} %bitcast.3.x_ref.g_ref.first_ref.fourth_ref, bf16[16,2,128,256]{3,2,1,0:T(8,128)(2,1)} %bitcast.3.x_ref.g_ref.first_ref.fourth_ref, ...), custom_call_target="tpu_custom_call" | custom-call | flops 1073741824 | bytes 6291456 | tf_op jit(solution)/shard_map/pallas_call | solution.py:246
  68.0 7.3 %all-to-all-start.1 = ((bf16[32,2,2,16,1024]{4,3,2,1,0:T(8,128)(2,1)}), bf16[32,2,2,16,1024]{4,3,2,1,0:T(8,128)(2,1)}, u32[]{:S(2)}, u32[]{:S(2)}) async-start(bf16[32,2,2,16,1024]{4,3,2,1,0:T(8,128)(2,1)} %bitcast.34), calls=%async_computation.1 | async-start | bytes 8388608 | tf_op jit(solution)/shard_map/all_to_all | solution.py:254
  75.3 3.3 %collective-permute-start.3 = (bf16[4,64,256]{2,1,0:T(8,128)(2,1)S(1)}, bf16[4,64,256]{2,1,0:T(8,128)(2,1)S(1)}, u32[]{:S(2)}, u32[]{:S(2)}) collective-permute-start(bf16[4,64,256]{2,1,0:T(8,128)(2,1)S(1)} %copy-done.1), channel_id=1, source_target_pairs={{0,64},{64,128},{128,192},{192,8},{8,72},{72,136},{136,200},{200,0... | collective-permute-start | bytes 393224 | tf_op jit(solution)/shard_map/ppermute | solution.py:222
  78.6 0.1 collective-permute-start.4
  78.7 2.2 collective-permute-start.5
  80.9 4.2 %collective-permute-start.6 = (bf16[4,64,256]{2,1,0:T(8,128)(2,1)S(1)}, bf16[4,64,256]{2,1,0:T(8,128)(2,1)S(1)}, u32[]{:S(2)}, u32[]{:S(2)}) collective-permute-start(bf16[4,64,256]{2,1,0:T(8,128)(2,1)S(1)} %copy-done.1), channel_id=1, source_target_pairs={{0,8},{64,72},{128,136},{192,200},{8,0},{72,64},{136,128},{200,192... | collective-permute-start | bytes 393224 | tf_op jit(solution)/shard_map/ppermute | solution.py:222
  85.1 0.4 collective-permute-start.7
  85.5 0.0 collective-permute-done.3.refs_1_
  85.5 3.8 %collective-permute-start.8 = (bf16[4,64,256]{2,1,0:T(8,128)(2,1)S(1)}, bf16[4,64,256]{2,1,0:T(8,128)(2,1)S(1)}, u32[]{:S(2)}, u32[]{:S(2)}) collective-permute-start(bf16[4,64,256]{2,1,0:T(8,128)(2,1)S(1)} %copy-done.1), channel_id=1, source_target_pairs={{0,136},{64,200},{128,0},{192,64},{8,128},{72,192},{136,8},{200,72... | collective-permute-start | bytes 393224 | tf_op jit(solution)/shard_map/ppermute | solution.py:222
  89.3 1.2 collective-permute-done.4.refs_2_
  90.5 1.2 collective-permute-start.9
  91.7 5.4 %collective-permute-done.5.refs_3_ = bf16[4,64,256]{2,1,0:T(8,128)(2,1)S(1)} collective-permute-done((bf16[4,64,256]{2,1,0:T(8,128)(2,1)S(1)}, bf16[4,64,256]{2,1,0:T(8,128)(2,1)S(1)}, u32[]{:S(2)}, u32[]{:S(2)}) %collective-permute-start.5) | collective-permute-done | bytes 131104 | tf_op jit(solution)/shard_map/ppermute | solution.py:222
  97.2 6.2 %collective-permute-done.6.refs_4_ = bf16[4,64,256]{2,1,0:T(8,128)(2,1)S(1)} collective-permute-done((bf16[4,64,256]{2,1,0:T(8,128)(2,1)S(1)}, bf16[4,64,256]{2,1,0:T(8,128)(2,1)S(1)}, u32[]{:S(2)}, u32[]{:S(2)}) %collective-permute-start.6) | collective-permute-done | bytes 131104 | tf_op jit(solution)/shard_map/ppermute | solution.py:222
  103.3 0.0 collective-permute-done.7.refs_5_
  103.3 4.5 %collective-permute-done.8.refs_6_ = bf16[4,64,256]{2,1,0:T(8,128)(2,1)S(1)} collective-permute-done((bf16[4,64,256]{2,1,0:T(8,128)(2,1)S(1)}, bf16[4,64,256]{2,1,0:T(8,128)(2,1)S(1)}, u32[]{:S(2)}, u32[]{:S(2)}) %collective-permute-start.8) | collective-permute-done | bytes 131104 | tf_op jit(solution)/shard_map/ppermute | solution.py:222
  107.9 0.0 collective-permute-done.9.refs_7_
  107.9 0.6 copy-done.13
  108.5 0.6 copy-done.14
  109.2 2.4 shard_map.113
  111.6 16.6 %all-to-all-done.1.in_ref = bf16[32,2,2,16,1024]{4,3,2,1,0:T(8,128)(2,1)} async-done(((bf16[32,2,2,16,1024]{4,3,2,1,0:T(8,128)(2,1)}), bf16[32,2,2,16,1024]{4,3,2,1,0:T(8,128)(2,1)}, u32[]{:S(2)}, u32[]{:S(2)}) %all-to-all-start.1) | async-done | bytes 4194336 | tf_op jit(solution)/shard_map/all_to_all | solution.py:254
  128.2 9.1 %shard_map.114 = (bf16[32,2,2,16,1024]{4,3,2,1,0:T(8,128)(2,1)}, bf16[2,4,4,64,256]{4,3,2,1,0:T(8,128)(2,1)}) custom-call(bf16[32,2,2,16,1024]{4,3,2,1,0:T(8,128)(2,1)} %all-to-all-done.1.in_ref, bf16[2,4,4,64,256]{4,3,2,1,0:T(8,128)(2,1)} %bitcast.39), custom_call_target="tpu_custom_call" | custom-call | flops 3221225472 | bytes 10485760 | tf_op jit(solution)/shard_map/pallas_call | solution.py:255
  137.3 9.9 %all-to-all-start.2 = ((bf16[32,2,2,16,1024]{4,3,2,1,0:T(8,128)(2,1)}), bf16[32,2,2,16,1024]{4,3,2,1,0:T(8,128)(2,1)}, u32[]{:S(2)}, u32[]{:S(2)}) async-start(bf16[32,2,2,16,1024]{4,3,2,1,0:T(8,128)(2,1)} %get-tuple-element.43), calls=%async_computation.2 | async-start | bytes 8388608 | tf_op jit(solution)/shard_map/all_to_all | solution.py:264
  147.2 0.1 dynamic-slice_bitcast_fusion
  147.3 3.3 %collective-permute-start.10 = (bf16[4,64,256]{2,1,0:T(8,128)(2,1)S(1)}, bf16[4,64,256]{2,1,0:T(8,128)(2,1)S(1)}, u32[]{:S(2)}, u32[]{:S(2)}) collective-permute-start(bf16[4,64,256]{2,1,0:T(8,128)(2,1)S(1)} %get-tuple-element.70), channel_id=1, source_target_pairs={{0,64},{64,128},{128,192},{192,8},{8,72},{72,136},{136,200},{200,0... | collective-permute-start | bytes 393224 | tf_op jit(solution)/shard_map/ppermute | solution.py:222
  150.7 0.1 collective-permute-start.11
  150.8 2.2 collective-permute-start.12
  153.0 4.2 %collective-permute-start.13 = (bf16[4,64,256]{2,1,0:T(8,128)(2,1)S(1)}, bf16[4,64,256]{2,1,0:T(8,128)(2,1)S(1)}, u32[]{:S(2)}, u32[]{:S(2)}) collective-permute-start(bf16[4,64,256]{2,1,0:T(8,128)(2,1)S(1)} %get-tuple-element.67), channel_id=1, source_target_pairs={{0,8},{64,72},{128,136},{192,200},{8,0},{72,64},{136,128},{200,192... | collective-permute-start | bytes 393224 | tf_op jit(solution)/shard_map/ppermute | solution.py:222
  157.2 0.4 collective-permute-start.14
  157.5 0.0 collective-permute-done.10.refs_1_
  157.6 3.8 %collective-permute-start.15 = (bf16[4,64,256]{2,1,0:T(8,128)(2,1)S(1)}, bf16[4,64,256]{2,1,0:T(8,128)(2,1)S(1)}, u32[]{:S(2)}, u32[]{:S(2)}) collective-permute-start(bf16[4,64,256]{2,1,0:T(8,128)(2,1)S(1)} %get-tuple-element.65), channel_id=1, source_target_pairs={{0,136},{64,200},{128,0},{192,64},{8,128},{72,192},{136,8},{200,72... | collective-permute-start | bytes 393224 | tf_op jit(solution)/shard_map/ppermute | solution.py:222
  161.4 1.2 collective-permute-done.11.refs_2_
  162.6 1.2 collective-permute-start.16
  163.8 5.4 %collective-permute-done.12.refs_3_ = bf16[4,64,256]{2,1,0:T(8,128)(2,1)S(1)} collective-permute-done((bf16[4,64,256]{2,1,0:T(8,128)(2,1)S(1)}, bf16[4,64,256]{2,1,0:T(8,128)(2,1)S(1)}, u32[]{:S(2)}, u32[]{:S(2)}) %collective-permute-start.12) | collective-permute-done | bytes 131104 | tf_op jit(solution)/shard_map/ppermute | solution.py:222
  169.2 6.2 %collective-permute-done.13.refs_4_ = bf16[4,64,256]{2,1,0:T(8,128)(2,1)S(1)} collective-permute-done((bf16[4,64,256]{2,1,0:T(8,128)(2,1)S(1)}, bf16[4,64,256]{2,1,0:T(8,128)(2,1)S(1)}, u32[]{:S(2)}, u32[]{:S(2)}) %collective-permute-start.13) | collective-permute-done | bytes 131104 | tf_op jit(solution)/shard_map/ppermute | solution.py:222
  175.4 0.0 collective-permute-done.14.refs_5_
  175.4 4.5 %collective-permute-done.15.refs_6_ = bf16[4,64,256]{2,1,0:T(8,128)(2,1)S(1)} collective-permute-done((bf16[4,64,256]{2,1,0:T(8,128)(2,1)S(1)}, bf16[4,64,256]{2,1,0:T(8,128)(2,1)S(1)}, u32[]{:S(2)}, u32[]{:S(2)}) %collective-permute-start.15) | collective-permute-done | bytes 131104 | tf_op jit(solution)/shard_map/ppermute | solution.py:222
  179.9 0.7 copy-done.7
  180.6 0.0 collective-permute-done.16.refs_7_
  180.6 2.1 shard_map.115
  182.7 1.4 dynamic-slice_bitcast_fusion.7
  184.1 1.5 collective-permute-start.17
  185.6 2.7 %collective-permute-start.18 = (bf16[64,256]{1,0:T(8,128)(2,1)S(1)}, bf16[64,256]{1,0:T(8,128)(2,1)S(1)}, u32[]{:S(2)}, u32[]{:S(2)}) collective-permute-start(bf16[64,256]{1,0:T(8,128)(2,1)S(1)} %get-tuple-element.72), channel_id=1, source_target_pairs={{0,32},{16,48},{32,0},{48,16},{1,33},{17,49},{33,1},{49,17},{2,34}... | collective-permute-start | bytes 98312 | tf_op jit(solution)/shard_map/ppermute | solution.py:217
  188.3 1.5 collective-permute-start.19
  189.7 8.8 %collective-permute-done.17.refs_1_ = bf16[64,256]{1,0:T(8,128)(2,1)S(1)} collective-permute-done((bf16[64,256]{1,0:T(8,128)(2,1)S(1)}, bf16[64,256]{1,0:T(8,128)(2,1)S(1)}, u32[]{:S(2)}, u32[]{:S(2)}) %collective-permute-start.17) | collective-permute-done | bytes 32800 | tf_op jit(solution)/shard_map/ppermute | solution.py:217
  198.6 2.8 %collective-permute-done.18.refs_2_ = bf16[64,256]{1,0:T(8,128)(2,1)S(1)} collective-permute-done((bf16[64,256]{1,0:T(8,128)(2,1)S(1)}, bf16[64,256]{1,0:T(8,128)(2,1)S(1)}, u32[]{:S(2)}, u32[]{:S(2)}) %collective-permute-start.18) | collective-permute-done | bytes 32800 | tf_op jit(solution)/shard_map/ppermute | solution.py:217
  201.4 2.9 %collective-permute-done.19.refs_3_ = bf16[64,256]{1,0:T(8,128)(2,1)S(1)} collective-permute-done((bf16[64,256]{1,0:T(8,128)(2,1)S(1)}, bf16[64,256]{1,0:T(8,128)(2,1)S(1)}, u32[]{:S(2)}, u32[]{:S(2)}) %collective-permute-start.19) | collective-permute-done | bytes 32800 | tf_op jit(solution)/shard_map/ppermute | solution.py:217
  204.2 0.0 all-to-all-done.2
  204.2 6.4 %shard_map.116 = bf16[16,2,128,256]{3,2,1,0:T(8,128)(2,1)} custom-call(s32[1]{0:T(128)} %bitcast.1.x1_ref, bf16[2,4,2,2,2,2,16,1024]{7,6,5,4,3,2,1,0:T(8,128)(2,1)} %bitcast.20.in_ref, bf16[16,2,128,256]{3,2,1,0:T(8,128)(2,1)} %bitcast.3.x_ref.g_ref.first_ref.fourth_ref, bf16[16,2,128,256]{3,2,1,0:T(8,128)(2,1)} %bitcast.3.x_ref.g_ref.first_ref.fourth_ref, ...), custom_call_target="tpu_custom_call" | custom-call | flops 2147483648 | bytes 8388608 | tf_op jit(solution)/shard_map/pallas_call | solution.py:283
  210.6 6.9 %all-to-all-start.3 = ((bf16[32,128,256]{2,1,0:T(8,128)(2,1)}), bf16[32,128,256]{2,1,0:T(8,128)(2,1)}, u32[]{:S(2)}, u32[]{:S(2)}) async-start(bf16[32,128,256]{2,1,0:T(8,128)(2,1)} %bitcast.36), calls=%async_computation.3 | async-start | bytes 4194304 | tf_op jit(solution)/shard_map/all_to_all | solution.py:298
  217.5 1.5 shard_map.117
  219.0 47.1 %all-to-all-done.3 = bf16[32,128,256]{2,1,0:T(8,128)(2,1)} async-done(((bf16[32,128,256]{2,1,0:T(8,128)(2,1)}), bf16[32,128,256]{2,1,0:T(8,128)(2,1)}, u32[]{:S(2)}, u32[]{:S(2)}) %all-to-all-start.3) | async-done | bytes 2097184 | tf_op jit(solution)/shard_map/all_to_all | solution.py:298
  266.2 2.5 shard_map.118
  (38 shorter events, 0.1 us)
Async XLA Ops:
  3.1 60.5 %all-to-all-start = ((bf16[32,128,256]{2,1,0:T(8,128)(2,1)}), bf16[32,128,256]{2,1,0:T(8,128)(2,1)}, u32[]{:S(2)}, u32[]{:S(2)}) async-start(bf16[32,128,256]{2,1,0:T(8,128)(2,1)} %bitcast.35), calls=%async_computation | async-start | bytes 4194304 | tf_op jit(solution)/shard_map/all_to_all | solution.py:243
  16.1 6.0 %collective-permute-start = (bf16[64,256]{1,0:T(8,128)(2,1)}, bf16[64,256]{1,0:T(8,128)(2,1)S(1)}, u32[]{:S(2)}, u32[]{:S(2)}) collective-permute-start(bf16[64,256]{1,0:T(8,128)(2,1)} %get-tuple-element.36), channel_id=1, source_target_pairs={{0,16},{16,32},{32,48},{48,0},{1,17},{17,33},{33,49},{49,1},{2,18}... | collective-permute-start | bytes 98312 | tf_op jit(solution)/shard_map/ppermute | solution.py:217
  17.8 5.7 %collective-permute-start.1 = (bf16[64,256]{1,0:T(8,128)(2,1)}, bf16[64,256]{1,0:T(8,128)(2,1)S(1)}, u32[]{:S(2)}, u32[]{:S(2)}) collective-permute-start(bf16[64,256]{1,0:T(8,128)(2,1)} %get-tuple-element.37), channel_id=1, source_target_pairs={{0,32},{16,48},{32,0},{48,16},{1,33},{17,49},{33,1},{49,17},{2,34}... | collective-permute-start | bytes 98312 | tf_op jit(solution)/shard_map/ppermute | solution.py:217
  20.5 6.2 %collective-permute-start.2 = (bf16[64,256]{1,0:T(8,128)(2,1)}, bf16[64,256]{1,0:T(8,128)(2,1)S(1)}, u32[]{:S(2)}, u32[]{:S(2)}) collective-permute-start(bf16[64,256]{1,0:T(8,128)(2,1)} %get-tuple-element.38), channel_id=1, source_target_pairs={{0,48},{16,0},{32,16},{48,32},{1,49},{17,1},{33,17},{49,33},{2,50}... | collective-permute-start | bytes 98312 | tf_op jit(solution)/shard_map/ppermute | solution.py:217
  22.1 4.6 %copy-start.18 = (bf16[64,256]{1,0:T(8,128)(2,1)}, bf16[64,256]{1,0:T(8,128)(2,1)S(1)}, u32[]{:S(2)}) copy-start(bf16[64,256]{1,0:T(8,128)(2,1)S(1)} %collective-permute-done.refs_1_) | copy-start | bytes 98308
  23.5 3.2 %copy-start.19 = (bf16[64,256]{1,0:T(8,128)(2,1)}, bf16[64,256]{1,0:T(8,128)(2,1)S(1)}, u32[]{:S(2)}) copy-start(bf16[64,256]{1,0:T(8,128)(2,1)S(1)} %collective-permute-done.1.refs_2_) | copy-start | bytes 98308
  26.7 0.6 copy-start.20
  68.0 7.3 %copy-start.1 = (bf16[4,64,256]{2,1,0:T(8,128)(2,1)S(1)}, bf16[4,64,256]{2,1,0:T(8,128)(2,1)}, u32[]{:S(2)}) copy-start(bf16[4,64,256]{2,1,0:T(8,128)(2,1)} %shard_map.111.refs_0_) | copy-start | bytes 393220
  68.0 60.2 %all-to-all-start.1 = ((bf16[32,2,2,16,1024]{4,3,2,1,0:T(8,128)(2,1)}), bf16[32,2,2,16,1024]{4,3,2,1,0:T(8,128)(2,1)}, u32[]{:S(2)}, u32[]{:S(2)}) async-start(bf16[32,2,2,16,1024]{4,3,2,1,0:T(8,128)(2,1)} %bitcast.34), calls=%async_computation.1 | async-start | bytes 8388608 | tf_op jit(solution)/shard_map/all_to_all | solution.py:254
  75.3 10.2 %collective-permute-start.3 = (bf16[4,64,256]{2,1,0:T(8,128)(2,1)S(1)}, bf16[4,64,256]{2,1,0:T(8,128)(2,1)S(1)}, u32[]{:S(2)}, u32[]{:S(2)}) collective-permute-start(bf16[4,64,256]{2,1,0:T(8,128)(2,1)S(1)} %copy-done.1), channel_id=1, source_target_pairs={{0,64},{64,128},{128,192},{192,8},{8,72},{72,136},{136,200},{200,0... | collective-permute-start | bytes 393224 | tf_op jit(solution)/shard_map/ppermute | solution.py:222
  78.6 11.9 %collective-permute-start.4 = (bf16[4,64,256]{2,1,0:T(8,128)(2,1)S(1)}, bf16[4,64,256]{2,1,0:T(8,128)(2,1)S(1)}, u32[]{:S(2)}, u32[]{:S(2)}) collective-permute-start(bf16[4,64,256]{2,1,0:T(8,128)(2,1)S(1)} %copy-done.1), channel_id=1, source_target_pairs={{0,128},{64,192},{128,8},{192,72},{8,136},{72,200},{136,0},{200,64... | collective-permute-start | bytes 393224 | tf_op jit(solution)/shard_map/ppermute | solution.py:222
  78.7 18.4 %collective-permute-start.5 = (bf16[4,64,256]{2,1,0:T(8,128)(2,1)S(1)}, bf16[4,64,256]{2,1,0:T(8,128)(2,1)S(1)}, u32[]{:S(2)}, u32[]{:S(2)}) collective-permute-start(bf16[4,64,256]{2,1,0:T(8,128)(2,1)S(1)} %copy-done.1), channel_id=1, source_target_pairs={{0,192},{64,8},{128,72},{192,136},{8,200},{72,0},{136,64},{200,128... | collective-permute-start | bytes 393224 | tf_op jit(solution)/shard_map/ppermute | solution.py:222
  80.9 22.4 %collective-permute-start.6 = (bf16[4,64,256]{2,1,0:T(8,128)(2,1)S(1)}, bf16[4,64,256]{2,1,0:T(8,128)(2,1)S(1)}, u32[]{:S(2)}, u32[]{:S(2)}) collective-permute-start(bf16[4,64,256]{2,1,0:T(8,128)(2,1)S(1)} %copy-done.1), channel_id=1, source_target_pairs={{0,8},{64,72},{128,136},{192,200},{8,0},{72,64},{136,128},{200,192... | collective-permute-start | bytes 393224 | tf_op jit(solution)/shard_map/ppermute | solution.py:222
  85.1 18.2 %collective-permute-start.7 = (bf16[4,64,256]{2,1,0:T(8,128)(2,1)S(1)}, bf16[4,64,256]{2,1,0:T(8,128)(2,1)S(1)}, u32[]{:S(2)}, u32[]{:S(2)}) collective-permute-start(bf16[4,64,256]{2,1,0:T(8,128)(2,1)S(1)} %copy-done.1), channel_id=1, source_target_pairs={{0,72},{64,136},{128,200},{192,0},{8,64},{72,128},{136,192},{200,8... | collective-permute-start | bytes 393224 | tf_op jit(solution)/shard_map/ppermute | solution.py:222
  85.5 23.7 %copy-start.8 = (bf16[4,64,256]{2,1,0:T(8,128)(2,1)}, bf16[4,64,256]{2,1,0:T(8,128)(2,1)S(1)}, u32[]{:S(2)}) copy-start(bf16[4,64,256]{2,1,0:T(8,128)(2,1)S(1)} %collective-permute-done.3.refs_1_) | copy-start | bytes 393220
  85.5 22.4 %collective-permute-start.8 = (bf16[4,64,256]{2,1,0:T(8,128)(2,1)S(1)}, bf16[4,64,256]{2,1,0:T(8,128)(2,1)S(1)}, u32[]{:S(2)}, u32[]{:S(2)}) collective-permute-start(bf16[4,64,256]{2,1,0:T(8,128)(2,1)S(1)} %copy-done.1), channel_id=1, source_target_pairs={{0,136},{64,200},{128,0},{192,64},{8,128},{72,192},{136,8},{200,72... | collective-permute-start | bytes 393224 | tf_op jit(solution)/shard_map/ppermute | solution.py:222
  90.5 18.7 %copy-start.9 = (bf16[4,64,256]{2,1,0:T(8,128)(2,1)}, bf16[4,64,256]{2,1,0:T(8,128)(2,1)S(1)}, u32[]{:S(2)}) copy-start(bf16[4,64,256]{2,1,0:T(8,128)(2,1)S(1)} %collective-permute-done.4.refs_2_) | copy-start | bytes 393220
  90.5 17.4 %collective-permute-start.9 = (bf16[4,64,256]{2,1,0:T(8,128)(2,1)S(1)}, bf16[4,64,256]{2,1,0:T(8,128)(2,1)S(1)}, u32[]{:S(2)}, u32[]{:S(2)}) collective-permute-start(bf16[4,64,256]{2,1,0:T(8,128)(2,1)S(1)} %copy-done.1), channel_id=1, source_target_pairs={{0,200},{64,0},{128,64},{192,128},{8,192},{72,8},{136,72},{200,136... | collective-permute-start | bytes 393224 | tf_op jit(solution)/shard_map/ppermute | solution.py:222
  97.2 10.7 %copy-start.10 = (bf16[4,64,256]{2,1,0:T(8,128)(2,1)}, bf16[4,64,256]{2,1,0:T(8,128)(2,1)S(1)}, u32[]{:S(2)}) copy-start(bf16[4,64,256]{2,1,0:T(8,128)(2,1)S(1)} %collective-permute-done.5.refs_3_) | copy-start | bytes 393220
  103.3 4.6 %copy-start.11 = (bf16[4,64,256]{2,1,0:T(8,128)(2,1)}, bf16[4,64,256]{2,1,0:T(8,128)(2,1)S(1)}, u32[]{:S(2)}) copy-start(bf16[4,64,256]{2,1,0:T(8,128)(2,1)S(1)} %collective-permute-done.6.refs_4_) | copy-start | bytes 393220
  103.3 4.6 %copy-start.12 = (bf16[4,64,256]{2,1,0:T(8,128)(2,1)}, bf16[4,64,256]{2,1,0:T(8,128)(2,1)S(1)}, u32[]{:S(2)}) copy-start(bf16[4,64,256]{2,1,0:T(8,128)(2,1)S(1)} %collective-permute-done.7.refs_5_) | copy-start | bytes 393220
  107.9 0.6 copy-start.13
  108.5 0.6 copy-start.14
  137.3 9.9 %copy-start = (bf16[2,4,4,64,256]{4,3,2,1,0:T(8,128)(2,1)S(1)}, bf16[2,4,4,64,256]{4,3,2,1,0:T(8,128)(2,1)}, u32[]{:S(2)}) copy-start(bf16[2,4,4,64,256]{4,3,2,1,0:T(8,128)(2,1)} %get-tuple-element.44) | copy-start | bytes 3145732
  137.3 67.0 %all-to-all-start.2 = ((bf16[32,2,2,16,1024]{4,3,2,1,0:T(8,128)(2,1)}), bf16[32,2,2,16,1024]{4,3,2,1,0:T(8,128)(2,1)}, u32[]{:S(2)}, u32[]{:S(2)}) async-start(bf16[32,2,2,16,1024]{4,3,2,1,0:T(8,128)(2,1)} %get-tuple-element.43), calls=%async_computation.2 | async-start | bytes 8388608 | tf_op jit(solution)/shard_map/all_to_all | solution.py:264
  147.3 10.2 %collective-permute-start.10 = (bf16[4,64,256]{2,1,0:T(8,128)(2,1)S(1)}, bf16[4,64,256]{2,1,0:T(8,128)(2,1)S(1)}, u32[]{:S(2)}, u32[]{:S(2)}) collective-permute-start(bf16[4,64,256]{2,1,0:T(8,128)(2,1)S(1)} %get-tuple-element.70), channel_id=1, source_target_pairs={{0,64},{64,128},{128,192},{192,8},{8,72},{72,136},{136,200},{200,0... | collective-permute-start | bytes 393224 | tf_op jit(solution)/shard_map/ppermute | solution.py:222
  150.7 11.9 %collective-permute-start.11 = (bf16[4,64,256]{2,1,0:T(8,128)(2,1)S(1)}, bf16[4,64,256]{2,1,0:T(8,128)(2,1)S(1)}, u32[]{:S(2)}, u32[]{:S(2)}) collective-permute-start(bf16[4,64,256]{2,1,0:T(8,128)(2,1)S(1)} %get-tuple-element.69), channel_id=1, source_target_pairs={{0,128},{64,192},{128,8},{192,72},{8,136},{72,200},{136,0},{200,64... | collective-permute-start | bytes 393224 | tf_op jit(solution)/shard_map/ppermute | solution.py:222
  150.8 18.4 %collective-permute-start.12 = (bf16[4,64,256]{2,1,0:T(8,128)(2,1)S(1)}, bf16[4,64,256]{2,1,0:T(8,128)(2,1)S(1)}, u32[]{:S(2)}, u32[]{:S(2)}) collective-permute-start(bf16[4,64,256]{2,1,0:T(8,128)(2,1)S(1)} %get-tuple-element.68), channel_id=1, source_target_pairs={{0,192},{64,8},{128,72},{192,136},{8,200},{72,0},{136,64},{200,128... | collective-permute-start | bytes 393224 | tf_op jit(solution)/shard_map/ppermute | solution.py:222
  153.0 22.4 %collective-permute-start.13 = (bf16[4,64,256]{2,1,0:T(8,128)(2,1)S(1)}, bf16[4,64,256]{2,1,0:T(8,128)(2,1)S(1)}, u32[]{:S(2)}, u32[]{:S(2)}) collective-permute-start(bf16[4,64,256]{2,1,0:T(8,128)(2,1)S(1)} %get-tuple-element.67), channel_id=1, source_target_pairs={{0,8},{64,72},{128,136},{192,200},{8,0},{72,64},{136,128},{200,192... | collective-permute-start | bytes 393224 | tf_op jit(solution)/shard_map/ppermute | solution.py:222
  157.2 18.2 %collective-permute-start.14 = (bf16[4,64,256]{2,1,0:T(8,128)(2,1)S(1)}, bf16[4,64,256]{2,1,0:T(8,128)(2,1)S(1)}, u32[]{:S(2)}, u32[]{:S(2)}) collective-permute-start(bf16[4,64,256]{2,1,0:T(8,128)(2,1)S(1)} %get-tuple-element.66), channel_id=1, source_target_pairs={{0,72},{64,136},{128,200},{192,0},{8,64},{72,128},{136,192},{200,8... | collective-permute-start | bytes 393224 | tf_op jit(solution)/shard_map/ppermute | solution.py:222
  157.5 23.0 %copy-start.2 = (bf16[4,64,256]{2,1,0:T(8,128)(2,1)}, bf16[4,64,256]{2,1,0:T(8,128)(2,1)S(1)}, u32[]{:S(2)}) copy-start(bf16[4,64,256]{2,1,0:T(8,128)(2,1)S(1)} %collective-permute-done.10.refs_1_) | copy-start | bytes 393220
  157.6 22.4 %collective-permute-start.15 = (bf16[4,64,256]{2,1,0:T(8,128)(2,1)S(1)}, bf16[4,64,256]{2,1,0:T(8,128)(2,1)S(1)}, u32[]{:S(2)}, u32[]{:S(2)}) collective-permute-start(bf16[4,64,256]{2,1,0:T(8,128)(2,1)S(1)} %get-tuple-element.65), channel_id=1, source_target_pairs={{0,136},{64,200},{128,0},{192,64},{8,128},{72,192},{136,8},{200,72... | collective-permute-start | bytes 393224 | tf_op jit(solution)/shard_map/ppermute | solution.py:222
  162.6 18.0 %copy-start.3 = (bf16[4,64,256]{2,1,0:T(8,128)(2,1)}, bf16[4,64,256]{2,1,0:T(8,128)(2,1)S(1)}, u32[]{:S(2)}) copy-start(bf16[4,64,256]{2,1,0:T(8,128)(2,1)S(1)} %collective-permute-done.11.refs_2_) | copy-start | bytes 393220
  162.6 18.0 %collective-permute-start.16 = (bf16[4,64,256]{2,1,0:T(8,128)(2,1)S(1)}, bf16[4,64,256]{2,1,0:T(8,128)(2,1)}, u32[]{:S(2)}, u32[]{:S(2)}) collective-permute-start(bf16[4,64,256]{2,1,0:T(8,128)(2,1)S(1)} %get-tuple-element.64), channel_id=1, source_target_pairs={{0,200},{64,0},{128,64},{192,128},{8,192},{72,8},{136,72},{200,136... | collective-permute-start | bytes 393224 | tf_op jit(solution)/shard_map/ppermute | solution.py:222
  169.2 11.4 %copy-start.4 = (bf16[4,64,256]{2,1,0:T(8,128)(2,1)}, bf16[4,64,256]{2,1,0:T(8,128)(2,1)S(1)}, u32[]{:S(2)}) copy-start(bf16[4,64,256]{2,1,0:T(8,128)(2,1)S(1)} %collective-permute-done.12.refs_3_) | copy-start | bytes 393220
  175.4 4.5 %copy-start.5 = (bf16[4,64,256]{2,1,0:T(8,128)(2,1)}, bf16[4,64,256]{2,1,0:T(8,128)(2,1)S(1)}, u32[]{:S(2)}) copy-start(bf16[4,64,256]{2,1,0:T(8,128)(2,1)S(1)} %collective-permute-done.13.refs_4_) | copy-start | bytes 393220
  175.4 4.5 %copy-start.6 = (bf16[4,64,256]{2,1,0:T(8,128)(2,1)}, bf16[4,64,256]{2,1,0:T(8,128)(2,1)S(1)}, u32[]{:S(2)}) copy-start(bf16[4,64,256]{2,1,0:T(8,128)(2,1)S(1)} %collective-permute-done.14.refs_5_) | copy-start | bytes 393220
  179.9 0.7 copy-start.7
  184.1 14.5 %collective-permute-start.17 = (bf16[64,256]{1,0:T(8,128)(2,1)S(1)}, bf16[64,256]{1,0:T(8,128)(2,1)S(1)}, u32[]{:S(2)}, u32[]{:S(2)}) collective-permute-start(bf16[64,256]{1,0:T(8,128)(2,1)S(1)} %get-tuple-element.73), channel_id=1, source_target_pairs={{0,16},{16,32},{32,48},{48,0},{1,17},{17,33},{33,49},{49,1},{2,18}... | collective-permute-start | bytes 98312 | tf_op jit(solution)/shard_map/ppermute | solution.py:217
  185.6 15.8 %collective-permute-start.18 = (bf16[64,256]{1,0:T(8,128)(2,1)S(1)}, bf16[64,256]{1,0:T(8,128)(2,1)S(1)}, u32[]{:S(2)}, u32[]{:S(2)}) collective-permute-start(bf16[64,256]{1,0:T(8,128)(2,1)S(1)} %get-tuple-element.72), channel_id=1, source_target_pairs={{0,32},{16,48},{32,0},{48,16},{1,33},{17,49},{33,1},{49,17},{2,34}... | collective-permute-start | bytes 98312 | tf_op jit(solution)/shard_map/ppermute | solution.py:217
  188.3 16.0 %collective-permute-start.19 = (bf16[64,256]{1,0:T(8,128)(2,1)S(1)}, bf16[64,256]{1,0:T(8,128)(2,1)S(1)}, u32[]{:S(2)}, u32[]{:S(2)}) collective-permute-start(bf16[64,256]{1,0:T(8,128)(2,1)S(1)} %get-tuple-element.71), channel_id=1, source_target_pairs={{0,48},{16,0},{32,16},{48,32},{1,49},{17,1},{33,17},{49,33},{2,50}... | collective-permute-start | bytes 98312 | tf_op jit(solution)/shard_map/ppermute | solution.py:217
  198.6 12.0 %copy-start.15 = (bf16[64,256]{1,0:T(8,128)(2,1)}, bf16[64,256]{1,0:T(8,128)(2,1)S(1)}, u32[]{:S(2)}) copy-start(bf16[64,256]{1,0:T(8,128)(2,1)S(1)} %collective-permute-done.17.refs_1_) | copy-start | bytes 98308
  201.4 9.2 %copy-start.16 = (bf16[64,256]{1,0:T(8,128)(2,1)}, bf16[64,256]{1,0:T(8,128)(2,1)S(1)}, u32[]{:S(2)}) copy-start(bf16[64,256]{1,0:T(8,128)(2,1)S(1)} %collective-permute-done.18.refs_2_) | copy-start | bytes 98308
  204.2 6.4 %copy-start.17 = (bf16[64,256]{1,0:T(8,128)(2,1)}, bf16[64,256]{1,0:T(8,128)(2,1)S(1)}, u32[]{:S(2)}) copy-start(bf16[64,256]{1,0:T(8,128)(2,1)S(1)} %collective-permute-done.19.refs_3_) | copy-start | bytes 98308
  210.6 55.5 %all-to-all-start.3 = ((bf16[32,128,256]{2,1,0:T(8,128)(2,1)}), bf16[32,128,256]{2,1,0:T(8,128)(2,1)}, u32[]{:S(2)}, u32[]{:S(2)}) async-start(bf16[32,128,256]{2,1,0:T(8,128)(2,1)} %bitcast.36), calls=%async_computation.3 | async-start | bytes 4194304 | tf_op jit(solution)/shard_map/all_to_all | solution.py:298

commit v7 on v5

--- a/solution.py
+++ b/solution.py
@@ -247,7 +247,8 @@
         x1, outer, outer, outer, outer
     )
     wire, inner = lax.optimization_barrier((wire, inner))
-    inner = [inner] + [along_z(inner, d) for d in range(1, 8)]
+    far_first = {d: along_z(inner, d) for d in (4, 3, 5, 2, 6, 1, 7)}
+    inner = [inner] + [far_first[d] for d in range(1, 8)]
     inner = call(
         arrange_kernel, (1,), [whole(PIECES.shape)] * 8, whole((8, 4, 64, BS)), S((8, 4, 64, BS), bf16), 0, 2 << 20
     )(at_z, *inner)
@@ -264,7 +265,8 @@
     wire = lax.all_to_all(wire, WAYS, 0, 0, tiled=True)
     grads = grads.reshape(8, 4, 64, BS)
     sums = [
-        along_z(lax.dynamic_index_in_dim(grads, lax.rem(at_z[0] + d, 8), keepdims=False), d) for d in range(1, 8)
+        along_z(lax.dynamic_index_in_dim(grads, lax.rem(at_z[0] + d, 8), keepdims=False), d)
+        for d in (4, 3, 5, 2, 6, 1, 7)
     ]
     sums = call(
         add_kernel,

time: 271 us -> 271 us (level)
    ppermute x14, waiting for transfers between devices: 34.6 us -> 30.6 us  [along_z(): lax.ppermute(values, ('zl', 'zh'), [(place[z], place[(z + d) % 8]) for z...]
    all_to_all x1, waiting for transfers between devices: 17.4 us -> 20.8 us  [body(): wire = lax.all_to_all(wire, WAYS, 0, 0, tiled=True)]
where the time goes in v7:
time: 271 us; the launch traced here: 268 us
  waiting for transfers between devices  148 us (55%)
  starting transfers between devices  81.5 us (30%)
  Pallas kernels  33.7 us (12%)
  local copies, waits for them, and re-layouts  3.92 us (1%)
    all_to_all x2, waiting for transfers between devices, body(): lax.all_to_all(outer.reshape(32, 128, BS), FAR, 0, 0, tiled=True)  69.2 us
    ppermute x14, starting transfers between devices, along_z(): lax.ppermute(values, ('zl', 'zh'), [(place[z], place[(z + d) % 8]) for z...  31.2 us
    ppermute x14, waiting for transfers between devices, along_z(): lax.ppermute(values, ('zl', 'zh'), [(place[z], place[(z + d) % 8]) for z...  30.6 us
    all_to_all x2, starting transfers between devices, body(): lax.all_to_all(outer.reshape(32, 128, BS), FAR, 0, 0, tiled=True)  21.4 us
    all_to_all x1, waiting for transfers between devices, body(): wire = lax.all_to_all(wire, WAYS, 0, 0, tiled=True)  20.8 us
    all_to_all x1, waiting for transfers between devices, body(): wire = lax.all_to_all(wire.reshape(PAIRS), WAYS, 0, 0, tiled=True)  16.6 us
    ppermute x6, starting transfers between devices, along_x(): return lax.ppermute(values, SIDE, [(i, (i + d) % 4) for i in range(4)])  11.7 us
    ppermute x6, waiting for transfers between devices, along_x(): return lax.ppermute(values, SIDE, [(i, (i + d) % 4) for i in range(4)])  10.5 us
  transfers between devices with their start and end apart: 24, of which 18 were waited for; matrix products, arithmetic and copies ran while one was open for 0% of the time, Pallas kernels for 3%

profile of v7, /device:TPU:16, one launch (start us, length us, event | category | flops | bytes accessed | tf_op | source)
XLA Modules:
  0.0 267.8 jit_solution(5838381052282326570)
XLA Ops:
  0.6 2.5 shard_map.109
  3.1 11.4 %all-to-all-start = ((bf16[32,128,256]{2,1,0:T(8,128)(2,1)}), bf16[32,128,256]{2,1,0:T(8,128)(2,1)}, u32[]{:S(2)}, u32[]{:S(2)}) async-start(bf16[32,128,256]{2,1,0:T(8,128)(2,1)} %bitcast.35), calls=%async_computation | async-start | bytes 4194304 | tf_op jit(solution)/shard_map/all_to_all | solution.py:243
  14.6 1.5 shard_map.110
  16.1 1.7 collective-permute-start
  17.8 2.7 collective-permute-start.1
  20.5 1.5 collective-permute-start.2
  22.0 0.2 collective-permute-done.refs_1_
  22.1 1.4 collective-permute-done.1.refs_2_
  23.5 3.2 %collective-permute-done.2.refs_3_ = bf16[64,256]{1,0:T(8,128)(2,1)S(1)} collective-permute-done((bf16[64,256]{1,0:T(8,128)(2,1)}, bf16[64,256]{1,0:T(8,128)(2,1)S(1)}, u32[]{:S(2)}, u32[]{:S(2)}) %collective-permute-start.2) | collective-permute-done | bytes 32800 | tf_op jit(solution)/shard_map/ppermute | solution.py:217
  26.7 0.6 copy-done.21
  27.3 1.5 shard_map.111.refs_0_
  28.8 34.8 %all-to-all-done = bf16[32,128,256]{2,1,0:T(8,128)(2,1)} async-done(((bf16[32,128,256]{2,1,0:T(8,128)(2,1)}), bf16[32,128,256]{2,1,0:T(8,128)(2,1)}, u32[]{:S(2)}, u32[]{:S(2)}) %all-to-all-start) | async-done | bytes 2097184 | tf_op jit(solution)/shard_map/all_to_all | solution.py:243
  63.6 4.4 %shard_map.112 = bf16[2,4,2,2,2,2,16,1024]{7,6,5,4,3,2,1,0:T(8,128)(2,1)} custom-call(s32[1]{0:T(128)} %bitcast.1.x1_ref, bf16[16,2,128,256]{3,2,1,0:T(8,128)(2,1)} %bitcast.3.x_ref.g_ref.first_ref.fourth_ref, bf16[16,2,128,256]{3,2,1,0:T(8,128)(2,1)} %bitcast.3.x_ref.g_ref.first_ref.fourth_ref, ...), custom_call_target="tpu_custom_call" | custom-call | flops 1073741824 | bytes 6291456 | tf_op jit(solution)/shard_map/pallas_call | solution.py:246
  68.0 7.3 %all-to-all-start.1 = ((bf16[32,2,2,16,1024]{4,3,2,1,0:T(8,128)(2,1)}), bf16[32,2,2,16,1024]{4,3,2,1,0:T(8,128)(2,1)}, u32[]{:S(2)}, u32[]{:S(2)}) async-start(bf16[32,2,2,16,1024]{4,3,2,1,0:T(8,128)(2,1)} %bitcast.34), calls=%async_computation.1 | async-start | bytes 8388608 | tf_op jit(solution)/shard_map/all_to_all | solution.py:255
  75.3 3.3 %collective-permute-start.3 = (bf16[4,64,256]{2,1,0:T(8,128)(2,1)S(1)}, bf16[4,64,256]{2,1,0:T(8,128)(2,1)S(1)}, u32[]{:S(2)}, u32[]{:S(2)}) collective-permute-start(bf16[4,64,256]{2,1,0:T(8,128)(2,1)S(1)} %copy-done.2), channel_id=1, source_target_pairs={{0,64},{64,128},{128,192},{192,8},{8,72},{72,136},{136,200},{200,0... | collective-permute-start | bytes 393224 | tf_op jit(solution)/shard_map/ppermute | solution.py:222
  78.6 0.1 collective-permute-start.4
  78.7 2.2 collective-permute-start.5
  80.9 4.2 %collective-permute-start.6 = (bf16[4,64,256]{2,1,0:T(8,128)(2,1)S(1)}, bf16[4,64,256]{2,1,0:T(8,128)(2,1)S(1)}, u32[]{:S(2)}, u32[]{:S(2)}) collective-permute-start(bf16[4,64,256]{2,1,0:T(8,128)(2,1)S(1)} %copy-done.2), channel_id=1, source_target_pairs={{0,8},{64,72},{128,136},{192,200},{8,0},{72,64},{136,128},{200,192... | collective-permute-start | bytes 393224 | tf_op jit(solution)/shard_map/ppermute | solution.py:222
  85.1 0.4 collective-permute-start.7
  85.5 3.8 %collective-permute-start.8 = (bf16[4,64,256]{2,1,0:T(8,128)(2,1)S(1)}, bf16[4,64,256]{2,1,0:T(8,128)(2,1)S(1)}, u32[]{:S(2)}, u32[]{:S(2)}) collective-permute-start(bf16[4,64,256]{2,1,0:T(8,128)(2,1)S(1)} %copy-done.2), channel_id=1, source_target_pairs={{0,136},{64,200},{128,0},{192,64},{8,128},{72,192},{136,8},{200,72... | collective-permute-start | bytes 393224 | tf_op jit(solution)/shard_map/ppermute | solution.py:222
  89.3 1.2 collective-permute-done.4.refs_2_
  90.5 1.2 collective-permute-start.9
  91.7 5.4 %collective-permute-done.5.refs_3_ = bf16[4,64,256]{2,1,0:T(8,128)(2,1)S(1)} collective-permute-done((bf16[4,64,256]{2,1,0:T(8,128)(2,1)S(1)}, bf16[4,64,256]{2,1,0:T(8,128)(2,1)S(1)}, u32[]{:S(2)}, u32[]{:S(2)}) %collective-permute-start.5) | collective-permute-done | bytes 131104 | tf_op jit(solution)/shard_map/ppermute | solution.py:222
  97.1 6.2 %collective-permute-done.6.refs_4_ = bf16[4,64,256]{2,1,0:T(8,128)(2,1)S(1)} collective-permute-done((bf16[4,64,256]{2,1,0:T(8,128)(2,1)S(1)}, bf16[4,64,256]{2,1,0:T(8,128)(2,1)S(1)}, u32[]{:S(2)}, u32[]{:S(2)}) %collective-permute-start.6) | collective-permute-done | bytes 131104 | tf_op jit(solution)/shard_map/ppermute | solution.py:222
  103.3 0.0 collective-permute-done.7.refs_5_
  103.3 4.5 %collective-permute-done.8.refs_6_ = bf16[4,64,256]{2,1,0:T(8,128)(2,1)S(1)} collective-permute-done((bf16[4,64,256]{2,1,0:T(8,128)(2,1)S(1)}, bf16[4,64,256]{2,1,0:T(8,128)(2,1)S(1)}, u32[]{:S(2)}, u32[]{:S(2)}) %collective-permute-start.8) | collective-permute-done | bytes 131104 | tf_op jit(solution)/shard_map/ppermute | solution.py:222
  107.9 0.0 collective-permute-done.9.refs_7_
  107.9 0.6 copy-done.13
  108.5 0.6 copy-done.15
  109.1 2.4 shard_map.113
  111.5 16.6 %all-to-all-done.1.in_ref = bf16[32,2,2,16,1024]{4,3,2,1,0:T(8,128)(2,1)} async-done(((bf16[32,2,2,16,1024]{4,3,2,1,0:T(8,128)(2,1)}), bf16[32,2,2,16,1024]{4,3,2,1,0:T(8,128)(2,1)}, u32[]{:S(2)}, u32[]{:S(2)}) %all-to-all-start.1) | async-done | bytes 4194336 | tf_op jit(solution)/shard_map/all_to_all | solution.py:255
  128.2 9.0 %shard_map.114 = (bf16[32,2,2,16,1024]{4,3,2,1,0:T(8,128)(2,1)}, bf16[2,4,4,64,256]{4,3,2,1,0:T(8,128)(2,1)}) custom-call(bf16[32,2,2,16,1024]{4,3,2,1,0:T(8,128)(2,1)} %all-to-all-done.1.in_ref, bf16[2,4,4,64,256]{4,3,2,1,0:T(8,128)(2,1)} %bitcast.39), custom_call_target="tpu_custom_call" | custom-call | flops 3221225472 | bytes 10485760 | tf_op jit(solution)/shard_map/pallas_call | solution.py:256
  137.2 9.9 %all-to-all-start.2 = ((bf16[32,2,2,16,1024]{4,3,2,1,0:T(8,128)(2,1)}), bf16[32,2,2,16,1024]{4,3,2,1,0:T(8,128)(2,1)}, u32[]{:S(2)}, u32[]{:S(2)}) async-start(bf16[32,2,2,16,1024]{4,3,2,1,0:T(8,128)(2,1)} %get-tuple-element.37), calls=%async_computation.2 | async-start | bytes 8388608 | tf_op jit(solution)/shard_map/all_to_all | solution.py:265
  147.2 0.1 dynamic-slice_bitcast_fusion
  147.3 2.5 collective-permute-start.10
  149.7 1.8 collective-permute-start.11
  151.5 3.5 %collective-permute-start.12 = (bf16[4,64,256]{2,1,0:T(8,128)(2,1)S(1)}, bf16[4,64,256]{2,1,0:T(8,128)(2,1)S(1)}, u32[]{:S(2)}, u32[]{:S(2)}) collective-permute-start(bf16[4,64,256]{2,1,0:T(8,128)(2,1)S(1)} %get-tuple-element.56), channel_id=1, source_target_pairs={{0,72},{64,136},{128,200},{192,0},{8,64},{72,128},{136,192},{200,8... | collective-permute-start | bytes 393224 | tf_op jit(solution)/shard_map/ppermute | solution.py:222
  155.1 2.3 collective-permute-start.13
  157.4 1.8 collective-permute-start.14
  159.2 4.0 %collective-permute-start.15 = (bf16[4,64,256]{2,1,0:T(8,128)(2,1)S(1)}, bf16[4,64,256]{2,1,0:T(8,128)(2,1)S(1)}, u32[]{:S(2)}, u32[]{:S(2)}) collective-permute-start(bf16[4,64,256]{2,1,0:T(8,128)(2,1)S(1)} %get-tuple-element.53), channel_id=1, source_target_pairs={{0,64},{64,128},{128,192},{192,8},{8,72},{72,136},{136,200},{200,0... | collective-permute-start | bytes 393224 | tf_op jit(solution)/shard_map/ppermute | solution.py:222
  163.2 7.0 %collective-permute-done.11.refs_2_ = bf16[4,64,256]{2,1,0:T(8,128)(2,1)S(1)} collective-permute-done((bf16[4,64,256]{2,1,0:T(8,128)(2,1)S(1)}, bf16[4,64,256]{2,1,0:T(8,128)(2,1)S(1)}, u32[]{:S(2)}, u32[]{:S(2)}) %collective-permute-start.11) | collective-permute-done | bytes 131104 | tf_op jit(solution)/shard_map/ppermute | solution.py:222
  170.2 0.0 collective-permute-start.16
  170.2 0.0 collective-permute-done.12.refs_3_
  170.2 0.0 copy-start.9
  170.2 3.5 %collective-permute-done.13.refs_4_ = bf16[4,64,256]{2,1,0:T(8,128)(2,1)S(1)} collective-permute-done((bf16[4,64,256]{2,1,0:T(8,128)(2,1)S(1)}, bf16[4,64,256]{2,1,0:T(8,128)(2,1)S(1)}, u32[]{:S(2)}, u32[]{:S(2)}) %collective-permute-start.13) | collective-permute-done | bytes 131104 | tf_op jit(solution)/shard_map/ppermute | solution.py:222
  173.7 0.3 collective-permute-done.14.refs_5_
  173.9 2.5 collective-permute-done.15.refs_6_
  176.5 0.7 copy-done.14
  177.1 0.0 collective-permute-done.16.refs_7_
  177.2 2.1 shard_map.115
  179.2 20.8 %all-to-all-done.2 = bf16[32,2,2,16,1024]{4,3,2,1,0:T(8,128)(2,1)} async-done(((bf16[32,2,2,16,1024]{4,3,2,1,0:T(8,128)(2,1)}), bf16[32,2,2,16,1024]{4,3,2,1,0:T(8,128)(2,1)}, u32[]{:S(2)}, u32[]{:S(2)}) %all-to-all-start.2) | async-done | bytes 4194336 | tf_op jit(solution)/shard_map/all_to_all | solution.py:265
  200.0 6.3 %shard_map.116 = bf16[16,2,128,256]{3,2,1,0:T(8,128)(2,1)} custom-call(s32[1]{0:T(128)} %bitcast.1.x1_ref, bf16[2,4,2,2,2,2,16,1024]{7,6,5,4,3,2,1,0:T(8,128)(2,1)} %bitcast.16.in_ref, bf16[16,2,128,256]{3,2,1,0:T(8,128)(2,1)} %bitcast.3.x_ref.g_ref.first_ref.fourth_ref, bf16[16,2,128,256]{3,2,1,0:T(8,128)(2,1)} %bitcast.3.x_ref.g_ref.first_ref.fourth_ref, ...), custom_call_target="tpu_custom_call" | custom-call | flops 2147483648 | bytes 8388608 | tf_op jit(solution)/shard_map/pallas_call | solution.py:283
  206.4 10.0 %all-to-all-start.3 = ((bf16[32,128,256]{2,1,0:T(8,128)(2,1)}), bf16[32,128,256]{2,1,0:T(8,128)(2,1)}, u32[]{:S(2)}, u32[]{:S(2)}) async-start(bf16[32,128,256]{2,1,0:T(8,128)(2,1)} %bitcast.36), calls=%async_computation.3 | async-start | bytes 4194304 | tf_op jit(solution)/shard_map/all_to_all | solution.py:300
  216.4 0.6 dynamic-slice_bitcast_fusion.7
  217.0 1.7 collective-permute-start.17
  218.7 2.7 collective-permute-start.18
  221.4 1.5 collective-permute-start.19
  222.9 0.5 collective-permute-done.17.refs_1_
  223.3 1.5 collective-permute-done.18.refs_2_
  224.8 3.8 %collective-permute-done.19.refs_3_ = bf16[64,256]{1,0:T(8,128)(2,1)S(1)} collective-permute-done((bf16[64,256]{1,0:T(8,128)(2,1)S(1)}, bf16[64,256]{1,0:T(8,128)(2,1)S(1)}, u32[]{:S(2)}, u32[]{:S(2)}) %collective-permute-start.19) | collective-permute-done | bytes 32800 | tf_op jit(solution)/shard_map/ppermute | solution.py:217
  228.7 0.6 copy-done.18
  229.3 1.5 shard_map.117
  230.8 34.4 %all-to-all-done.3 = bf16[32,128,256]{2,1,0:T(8,128)(2,1)} async-done(((bf16[32,128,256]{2,1,0:T(8,128)(2,1)}), bf16[32,128,256]{2,1,0:T(8,128)(2,1)}, u32[]{:S(2)}, u32[]{:S(2)}) %all-to-all-start.3) | async-done | bytes 2097184 | tf_op jit(solution)/shard_map/all_to_all | solution.py:300
  265.2 2.5 shard_map.118
  (40 shorter events, 0.1 us)
Async XLA Ops:
  3.1 60.5 %all-to-all-start = ((bf16[32,128,256]{2,1,0:T(8,128)(2,1)}), bf16[32,128,256]{2,1,0:T(8,128)(2,1)}, u32[]{:S(2)}, u32[]{:S(2)}) async-start(bf16[32,128,256]{2,1,0:T(8,128)(2,1)} %bitcast.35), calls=%async_computation | async-start | bytes 4194304 | tf_op jit(solution)/shard_map/all_to_all | solution.py:243
  16.1 6.0 %collective-permute-start = (bf16[64,256]{1,0:T(8,128)(2,1)}, bf16[64,256]{1,0:T(8,128)(2,1)S(1)}, u32[]{:S(2)}, u32[]{:S(2)}) collective-permute-start(bf16[64,256]{1,0:T(8,128)(2,1)} %get-tuple-element.30), channel_id=1, source_target_pairs={{0,16},{16,32},{32,48},{48,0},{1,17},{17,33},{33,49},{49,1},{2,18}... | collective-permute-start | bytes 98312 | tf_op jit(solution)/shard_map/ppermute | solution.py:217
  17.8 5.7 %collective-permute-start.1 = (bf16[64,256]{1,0:T(8,128)(2,1)}, bf16[64,256]{1,0:T(8,128)(2,1)S(1)}, u32[]{:S(2)}, u32[]{:S(2)}) collective-permute-start(bf16[64,256]{1,0:T(8,128)(2,1)} %get-tuple-element.31), channel_id=1, source_target_pairs={{0,32},{16,48},{32,0},{48,16},{1,33},{17,49},{33,1},{49,17},{2,34}... | collective-permute-start | bytes 98312 | tf_op jit(solution)/shard_map/ppermute | solution.py:217
  20.5 6.2 %collective-permute-start.2 = (bf16[64,256]{1,0:T(8,128)(2,1)}, bf16[64,256]{1,0:T(8,128)(2,1)S(1)}, u32[]{:S(2)}, u32[]{:S(2)}) collective-permute-start(bf16[64,256]{1,0:T(8,128)(2,1)} %get-tuple-element.32), channel_id=1, source_target_pairs={{0,48},{16,0},{32,16},{48,32},{1,49},{17,1},{33,17},{49,33},{2,50}... | collective-permute-start | bytes 98312 | tf_op jit(solution)/shard_map/ppermute | solution.py:217
  22.1 4.6 %copy-start.19 = (bf16[64,256]{1,0:T(8,128)(2,1)}, bf16[64,256]{1,0:T(8,128)(2,1)S(1)}, u32[]{:S(2)}) copy-start(bf16[64,256]{1,0:T(8,128)(2,1)S(1)} %collective-permute-done.refs_1_) | copy-start | bytes 98308
  23.5 3.2 %copy-start.20 = (bf16[64,256]{1,0:T(8,128)(2,1)}, bf16[64,256]{1,0:T(8,128)(2,1)S(1)}, u32[]{:S(2)}) copy-start(bf16[64,256]{1,0:T(8,128)(2,1)S(1)} %collective-permute-done.1.refs_2_) | copy-start | bytes 98308
  26.7 0.6 copy-start.21
  68.0 7.3 %copy-start.2 = (bf16[4,64,256]{2,1,0:T(8,128)(2,1)S(1)}, bf16[4,64,256]{2,1,0:T(8,128)(2,1)}, u32[]{:S(2)}) copy-start(bf16[4,64,256]{2,1,0:T(8,128)(2,1)} %shard_map.111.refs_0_) | copy-start | bytes 393220
  68.0 60.2 %all-to-all-start.1 = ((bf16[32,2,2,16,1024]{4,3,2,1,0:T(8,128)(2,1)}), bf16[32,2,2,16,1024]{4,3,2,1,0:T(8,128)(2,1)}, u32[]{:S(2)}, u32[]{:S(2)}) async-start(bf16[32,2,2,16,1024]{4,3,2,1,0:T(8,128)(2,1)} %bitcast.34), calls=%async_computation.1 | async-start | bytes 8388608 | tf_op jit(solution)/shard_map/all_to_all | solution.py:255
  75.3 10.2 %collective-permute-start.3 = (bf16[4,64,256]{2,1,0:T(8,128)(2,1)S(1)}, bf16[4,64,256]{2,1,0:T(8,128)(2,1)S(1)}, u32[]{:S(2)}, u32[]{:S(2)}) collective-permute-start(bf16[4,64,256]{2,1,0:T(8,128)(2,1)S(1)} %copy-done.2), channel_id=1, source_target_pairs={{0,64},{64,128},{128,192},{192,8},{8,72},{72,136},{136,200},{200,0... | collective-permute-start | bytes 393224 | tf_op jit(solution)/shard_map/ppermute | solution.py:222
  78.6 11.9 %collective-permute-start.4 = (bf16[4,64,256]{2,1,0:T(8,128)(2,1)S(1)}, bf16[4,64,256]{2,1,0:T(8,128)(2,1)S(1)}, u32[]{:S(2)}, u32[]{:S(2)}) collective-permute-start(bf16[4,64,256]{2,1,0:T(8,128)(2,1)S(1)} %copy-done.2), channel_id=1, source_target_pairs={{0,128},{64,192},{128,8},{192,72},{8,136},{72,200},{136,0},{200,64... | collective-permute-start | bytes 393224 | tf_op jit(solution)/shard_map/ppermute | solution.py:222
  78.7 18.4 %collective-permute-start.5 = (bf16[4,64,256]{2,1,0:T(8,128)(2,1)S(1)}, bf16[4,64,256]{2,1,0:T(8,128)(2,1)S(1)}, u32[]{:S(2)}, u32[]{:S(2)}) collective-permute-start(bf16[4,64,256]{2,1,0:T(8,128)(2,1)S(1)} %copy-done.2), channel_id=1, source_target_pairs={{0,192},{64,8},{128,72},{192,136},{8,200},{72,0},{136,64},{200,128... | collective-permute-start | bytes 393224 | tf_op jit(solution)/shard_map/ppermute | solution.py:222
  80.9 22.4 %collective-permute-start.6 = (bf16[4,64,256]{2,1,0:T(8,128)(2,1)S(1)}, bf16[4,64,256]{2,1,0:T(8,128)(2,1)S(1)}, u32[]{:S(2)}, u32[]{:S(2)}) collective-permute-start(bf16[4,64,256]{2,1,0:T(8,128)(2,1)S(1)} %copy-done.2), channel_id=1, source_target_pairs={{0,8},{64,72},{128,136},{192,200},{8,0},{72,64},{136,128},{200,192... | collective-permute-start | bytes 393224 | tf_op jit(solution)/shard_map/ppermute | solution.py:222
  85.1 18.2 %collective-permute-start.7 = (bf16[4,64,256]{2,1,0:T(8,128)(2,1)S(1)}, bf16[4,64,256]{2,1,0:T(8,128)(2,1)S(1)}, u32[]{:S(2)}, u32[]{:S(2)}) collective-permute-start(bf16[4,64,256]{2,1,0:T(8,128)(2,1)S(1)} %copy-done.2), channel_id=1, source_target_pairs={{0,72},{64,136},{128,200},{192,0},{8,64},{72,128},{136,192},{200,8... | collective-permute-start | bytes 393224 | tf_op jit(solution)/shard_map/ppermute | solution.py:222
  85.5 23.6 %copy-start.3 = (bf16[4,64,256]{2,1,0:T(8,128)(2,1)}, bf16[4,64,256]{2,1,0:T(8,128)(2,1)S(1)}, u32[]{:S(2)}) copy-start(bf16[4,64,256]{2,1,0:T(8,128)(2,1)S(1)} %collective-permute-done.3.refs_1_) | copy-start | bytes 393220
  85.5 22.4 %collective-permute-start.8 = (bf16[4,64,256]{2,1,0:T(8,128)(2,1)S(1)}, bf16[4,64,256]{2,1,0:T(8,128)(2,1)S(1)}, u32[]{:S(2)}, u32[]{:S(2)}) collective-permute-start(bf16[4,64,256]{2,1,0:T(8,128)(2,1)S(1)} %copy-done.2), channel_id=1, source_target_pairs={{0,136},{64,200},{128,0},{192,64},{8,128},{72,192},{136,8},{200,72... | collective-permute-start | bytes 393224 | tf_op jit(solution)/shard_map/ppermute | solution.py:222
  90.5 18.6 %copy-start.4 = (bf16[4,64,256]{2,1,0:T(8,128)(2,1)}, bf16[4,64,256]{2,1,0:T(8,128)(2,1)S(1)}, u32[]{:S(2)}) copy-start(bf16[4,64,256]{2,1,0:T(8,128)(2,1)S(1)} %collective-permute-done.4.refs_2_) | copy-start | bytes 393220
  90.5 17.4 %collective-permute-start.9 = (bf16[4,64,256]{2,1,0:T(8,128)(2,1)S(1)}, bf16[4,64,256]{2,1,0:T(8,128)(2,1)S(1)}, u32[]{:S(2)}, u32[]{:S(2)}) collective-permute-start(bf16[4,64,256]{2,1,0:T(8,128)(2,1)S(1)} %copy-done.2), channel_id=1, source_target_pairs={{0,200},{64,0},{128,64},{192,128},{8,192},{72,8},{136,72},{200,136... | collective-permute-start | bytes 393224 | tf_op jit(solution)/shard_map/ppermute | solution.py:222
  97.1 10.7 %copy-start.6 = (bf16[4,64,256]{2,1,0:T(8,128)(2,1)}, bf16[4,64,256]{2,1,0:T(8,128)(2,1)S(1)}, u32[]{:S(2)}) copy-start(bf16[4,64,256]{2,1,0:T(8,128)(2,1)S(1)} %collective-permute-done.5.refs_3_) | copy-start | bytes 393220
  103.3 4.6 %copy-start.8 = (bf16[4,64,256]{2,1,0:T(8,128)(2,1)}, bf16[4,64,256]{2,1,0:T(8,128)(2,1)S(1)}, u32[]{:S(2)}) copy-start(bf16[4,64,256]{2,1,0:T(8,128)(2,1)S(1)} %collective-permute-done.6.refs_4_) | copy-start | bytes 393220
  103.3 4.6 %copy-start.10 = (bf16[4,64,256]{2,1,0:T(8,128)(2,1)}, bf16[4,64,256]{2,1,0:T(8,128)(2,1)S(1)}, u32[]{:S(2)}) copy-start(bf16[4,64,256]{2,1,0:T(8,128)(2,1)S(1)} %collective-permute-done.7.refs_5_) | copy-start | bytes 393220
  107.8 0.6 copy-start.13
  108.5 0.6 copy-start.15
  137.2 10.0 %copy-start = (bf16[2,4,4,64,256]{4,3,2,1,0:T(8,128)(2,1)S(1)}, bf16[2,4,4,64,256]{4,3,2,1,0:T(8,128)(2,1)}, u32[]{:S(2)}) copy-start(bf16[2,4,4,64,256]{4,3,2,1,0:T(8,128)(2,1)} %get-tuple-element.38) | copy-start | bytes 3145732
  137.2 62.8 %all-to-all-start.2 = ((bf16[32,2,2,16,1024]{4,3,2,1,0:T(8,128)(2,1)}), bf16[32,2,2,16,1024]{4,3,2,1,0:T(8,128)(2,1)}, u32[]{:S(2)}, u32[]{:S(2)}) async-start(bf16[32,2,2,16,1024]{4,3,2,1,0:T(8,128)(2,1)} %get-tuple-element.37), calls=%async_computation.2 | async-start | bytes 8388608 | tf_op jit(solution)/shard_map/all_to_all | solution.py:265
  147.3 12.0 %collective-permute-start.10 = (bf16[4,64,256]{2,1,0:T(8,128)(2,1)S(1)}, bf16[4,64,256]{2,1,0:T(8,128)(2,1)S(1)}, u32[]{:S(2)}, u32[]{:S(2)}) collective-permute-start(bf16[4,64,256]{2,1,0:T(8,128)(2,1)S(1)} %get-tuple-element.58), channel_id=1, source_target_pairs={{0,8},{64,72},{128,136},{192,200},{8,0},{72,64},{136,128},{200,192... | collective-permute-start | bytes 393224 | tf_op jit(solution)/shard_map/ppermute | solution.py:222
  149.7 20.4 %collective-permute-start.11 = (bf16[4,64,256]{2,1,0:T(8,128)(2,1)S(1)}, bf16[4,64,256]{2,1,0:T(8,128)(2,1)S(1)}, u32[]{:S(2)}, u32[]{:S(2)}) collective-permute-start(bf16[4,64,256]{2,1,0:T(8,128)(2,1)S(1)} %get-tuple-element.57), channel_id=1, source_target_pairs={{0,192},{64,8},{128,72},{192,136},{8,200},{72,0},{136,64},{200,128... | collective-permute-start | bytes 393224 | tf_op jit(solution)/shard_map/ppermute | solution.py:222
  151.5 18.6 %collective-permute-start.12 = (bf16[4,64,256]{2,1,0:T(8,128)(2,1)S(1)}, bf16[4,64,256]{2,1,0:T(8,128)(2,1)S(1)}, u32[]{:S(2)}, u32[]{:S(2)}) collective-permute-start(bf16[4,64,256]{2,1,0:T(8,128)(2,1)S(1)} %get-tuple-element.56), channel_id=1, source_target_pairs={{0,72},{64,136},{128,200},{192,0},{8,64},{72,128},{136,192},{200,8... | collective-permute-start | bytes 393224 | tf_op jit(solution)/shard_map/ppermute | solution.py:222
  155.1 18.6 %collective-permute-start.13 = (bf16[4,64,256]{2,1,0:T(8,128)(2,1)S(1)}, bf16[4,64,256]{2,1,0:T(8,128)(2,1)S(1)}, u32[]{:S(2)}, u32[]{:S(2)}) collective-permute-start(bf16[4,64,256]{2,1,0:T(8,128)(2,1)S(1)} %get-tuple-element.55), channel_id=1, source_target_pairs={{0,128},{64,192},{128,8},{192,72},{8,136},{72,200},{136,0},{200,64... | collective-permute-start | bytes 393224 | tf_op jit(solution)/shard_map/ppermute | solution.py:222
  157.4 16.6 %collective-permute-start.14 = (bf16[4,64,256]{2,1,0:T(8,128)(2,1)S(1)}, bf16[4,64,256]{2,1,0:T(8,128)(2,1)S(1)}, u32[]{:S(2)}, u32[]{:S(2)}) collective-permute-start(bf16[4,64,256]{2,1,0:T(8,128)(2,1)S(1)} %get-tuple-element.54), channel_id=1, source_target_pairs={{0,136},{64,200},{128,0},{192,64},{8,128},{72,192},{136,8},{200,72... | collective-permute-start | bytes 393224 | tf_op jit(solution)/shard_map/ppermute | solution.py:222
  159.2 17.9 %copy-start.5 = (bf16[4,64,256]{2,1,0:T(8,128)(2,1)}, bf16[4,64,256]{2,1,0:T(8,128)(2,1)S(1)}, u32[]{:S(2)}) copy-start(bf16[4,64,256]{2,1,0:T(8,128)(2,1)S(1)} %collective-permute-done.10.refs_1_) | copy-start | bytes 393220
  159.2 17.2 %collective-permute-start.15 = (bf16[4,64,256]{2,1,0:T(8,128)(2,1)S(1)}, bf16[4,64,256]{2,1,0:T(8,128)(2,1)S(1)}, u32[]{:S(2)}, u32[]{:S(2)}) collective-permute-start(bf16[4,64,256]{2,1,0:T(8,128)(2,1)S(1)} %get-tuple-element.53), channel_id=1, source_target_pairs={{0,64},{64,128},{128,192},{192,8},{8,72},{72,136},{136,200},{200,0... | collective-permute-start | bytes 393224 | tf_op jit(solution)/shard_map/ppermute | solution.py:222
  170.2 7.0 %copy-start.7 = (bf16[4,64,256]{2,1,0:T(8,128)(2,1)}, bf16[4,64,256]{2,1,0:T(8,128)(2,1)S(1)}, u32[]{:S(2)}) copy-start(bf16[4,64,256]{2,1,0:T(8,128)(2,1)S(1)} %collective-permute-done.11.refs_2_) | copy-start | bytes 393220
  170.2 7.0 %collective-permute-start.16 = (bf16[4,64,256]{2,1,0:T(8,128)(2,1)S(1)}, bf16[4,64,256]{2,1,0:T(8,128)(2,1)}, u32[]{:S(2)}, u32[]{:S(2)}) collective-permute-start(bf16[4,64,256]{2,1,0:T(8,128)(2,1)S(1)} %get-tuple-element.52), channel_id=1, source_target_pairs={{0,200},{64,0},{128,64},{192,128},{8,192},{72,8},{136,72},{200,136... | collective-permute-start | bytes 393224 | tf_op jit(solution)/shard_map/ppermute | solution.py:222
  170.2 7.0 %copy-start.9 = (bf16[4,64,256]{2,1,0:T(8,128)(2,1)}, bf16[4,64,256]{2,1,0:T(8,128)(2,1)S(1)}, u32[]{:S(2)}) copy-start(bf16[4,64,256]{2,1,0:T(8,128)(2,1)S(1)} %collective-permute-done.12.refs_3_) | copy-start | bytes 393220
  173.7 2.8 %copy-start.11 = (bf16[4,64,256]{2,1,0:T(8,128)(2,1)}, bf16[4,64,256]{2,1,0:T(8,128)(2,1)S(1)}, u32[]{:S(2)}) copy-start(bf16[4,64,256]{2,1,0:T(8,128)(2,1)S(1)} %collective-permute-done.13.refs_4_) | copy-start | bytes 393220
  173.9 2.5 copy-start.12
  176.5 0.7 copy-start.14
  206.4 10.0 %copy-start.1 = (bf16[4,64,256]{2,1,0:T(8,128)(2,1)S(1)}, bf16[4,64,256]{2,1,0:T(8,128)(2,1)}, u32[]{:S(2)}) copy-start(bf16[4,64,256]{2,1,0:T(8,128)(2,1)} %shard_map.115) | copy-start | bytes 393220
  206.4 58.8 %all-to-all-start.3 = ((bf16[32,128,256]{2,1,0:T(8,128)(2,1)}), bf16[32,128,256]{2,1,0:T(8,128)(2,1)}, u32[]{:S(2)}, u32[]{:S(2)}) async-start(bf16[32,128,256]{2,1,0:T(8,128)(2,1)} %bitcast.36), calls=%async_computation.3 | async-start | bytes 4194304 | tf_op jit(solution)/shard_map/all_to_all | solution.py:300
  217.0 6.3 %collective-permute-start.17 = (bf16[64,256]{1,0:T(8,128)(2,1)S(1)}, bf16[64,256]{1,0:T(8,128)(2,1)S(1)}, u32[]{:S(2)}, u32[]{:S(2)}) collective-permute-start(bf16[64,256]{1,0:T(8,128)(2,1)S(1)} %get-tuple-element.61), channel_id=1, source_target_pairs={{0,16},{16,32},{32,48},{48,0},{1,17},{17,33},{33,49},{49,1},{2,18}... | collective-permute-start | bytes 98312 | tf_op jit(solution)/shard_map/ppermute | solution.py:217
  218.7 6.1 %collective-permute-start.18 = (bf16[64,256]{1,0:T(8,128)(2,1)S(1)}, bf16[64,256]{1,0:T(8,128)(2,1)S(1)}, u32[]{:S(2)}, u32[]{:S(2)}) collective-permute-start(bf16[64,256]{1,0:T(8,128)(2,1)S(1)} %get-tuple-element.60), channel_id=1, source_target_pairs={{0,32},{16,48},{32,0},{48,16},{1,33},{17,49},{33,1},{49,17},{2,34}... | collective-permute-start | bytes 98312 | tf_op jit(solution)/shard_map/ppermute | solution.py:217
  221.4 7.3 %collective-permute-start.19 = (bf16[64,256]{1,0:T(8,128)(2,1)S(1)}, bf16[64,256]{1,0:T(8,128)(2,1)S(1)}, u32[]{:S(2)}, u32[]{:S(2)}) collective-permute-start(bf16[64,256]{1,0:T(8,128)(2,1)S(1)} %get-tuple-element.59), channel_id=1, source_target_pairs={{0,48},{16,0},{32,16},{48,32},{1,49},{17,1},{33,17},{49,33},{2,50}... | collective-permute-start | bytes 98312 | tf_op jit(solution)/shard_map/ppermute | solution.py:217
  223.3 5.3 %copy-start.16 = (bf16[64,256]{1,0:T(8,128)(2,1)}, bf16[64,256]{1,0:T(8,128)(2,1)S(1)}, u32[]{:S(2)}) copy-start(bf16[64,256]{1,0:T(8,128)(2,1)S(1)} %collective-permute-done.17.refs_1_) | copy-start | bytes 98308
  224.8 3.8 %copy-start.17 = (bf16[64,256]{1,0:T(8,128)(2,1)}, bf16[64,256]{1,0:T(8,128)(2,1)S(1)}, u32[]{:S(2)}) copy-start(bf16[64,256]{1,0:T(8,128)(2,1)S(1)} %collective-permute-done.18.refs_2_) | copy-start | bytes 98308
  228.7 0.6 copy-start.18
